TPU v7x, 32 devices: a whole 2x2x4 slice. The times are simulated.
32 devices in a mesh: rep: 16 (over z, x, core), dom: 2 (over y).
Axes of the slice: x: 2, y: 2, z: 4, core: 2. Of those that a mesh axis runs over, the one named last changes fastest.
Arguments:
- particle_locations: float32 [16, 3, 2048], P('rep', None, 'dom'), may hold values from 0 to 1.5
- particle_speeds: float32 [16, 3, 2048], P('rep', None, 'dom'), may hold values from -6 to 6
- current_pushes: float32 [16, 3, 2048], P('rep', None, 'dom'), may hold values from -6 to 6
- particle_kinds: int32 [16, 2048], P('rep', 'dom'), may hold values from 0 to 15
- halo_particle_labels: int32 [16, 1536], P('rep', 'dom'), may hold values from 0 to 1023
- adjacent_block_labels: int32 [16, 16, 4], P('rep', 'dom'), may hold values from 0 to 13
- adjacent_place_totals: int32 [16, 16], P('rep', 'dom'), may hold values from 1 to 4, as said below
- kind_vectors: bfloat16 [16, 128], replicated, may hold values from -6 to 6
- kind_inertia: float32 [16], replicated, may hold values from 1 to 4
- stepwise_distance_coefficients: float32 [2, 8, 128], replicated, may hold values from -2 to 2
- signal_scaling_factors: float32 [2, 128], replicated, may hold values from 0.1 to 1.9
- feature_blend_coefficients: bfloat16 [2, 128, 128], replicated, may hold values from -0.5 to 0.5
- target_projection_array: bfloat16 [128, 128], replicated, may hold values from -0.5 to 0.5
- source_projection_array: bfloat16 [128, 128], replicated, may hold values from -0.5 to 0.5
- push_distance_taper: float32 [8], replicated, may hold values from -4 to 4
- thermal_levels: float32 [16], replicated, may hold values from 0.5 to 2
- granted_swaps: int32 [16], replicated, may hold values from 0 to 15, as said below
Outputs:
- positions_out: float32 [16, 3, 2048], P('rep', None, 'dom')
- velocities_out: float32 [16, 3, 2048], P('rep', None, 'dom')
- forces_out: float32 [16, 3, 2048], P('rep', None, 'dom')
Inputs may be any that keep to these rules, and one draw needn't show every extreme that they name: `halo_particle_labels`: each domain's block of 768 entries: the first 384 name its atoms imported by the next lower domain, the last 384 those imported by the next higher domain. `adjacent_block_labels`: numbers below 8 are the domain's own tiles; the rest are the imported atoms' tiles in extended order. `adjacent_place_totals`: in every replica some domain has all its tiles at 4 live slots. `granted_swaps`: each replica's partner is itself or a ladder neighbour, and the partner's partner is the replica. The pairs (0, 1), (7, 8) and (14, 15) are always accepted.
All inputs are finite; a program needn't handle non-finite values.
Results may differ from a plain program's by a relative error of at most 0.0067.
Values may be sent and summed in bfloat16 or wider, within the bound.
No kernel may reach another device: no remote copies, remote signals or barrier semaphores. Data moves between devices by JAX's collectives and lax.ppermute only.
A program may use at most 64 MiB of HBM per device.

v0:
```python
import math

import jax
import jax.numpy as jnp
from jax import lax
from jax.sharding import PartitionSpec as P

NB = 8
TILE = 128
NEI = 4


slab_width = 1.5
time_step = 0.5
basis_width = 0.3
norm_eps = 1e-06


def with_halo(cells, sides, width):
    for axis, dim in sides:
        count = lax.axis_size(axis)
        head = lax.slice_in_dim(cells, 0, width, axis=dim)
        tail = lax.slice_in_dim(cells, cells.shape[dim] - width, cells.shape[dim], axis=dim)
        cells = jnp.concatenate(
            [
                lax.ppermute(tail, axis, [(i, (i + 1) % count) for i in range(count)]),
                cells,
                lax.ppermute(head, axis, [((i + 1) % count, i) for i in range(count)]),
            ],
            axis=dim,
        )
    return cells


def from_behind(array, axis, by):
    count = lax.axis_size(axis)
    pairs = [(i, i + by) for i in range(count) if 0 <= i + by < count]
    return lax.ppermute(array, axis, pairs)


def slot_basis(near_pos, far_pos, live_flags):
    offsets = far_pos[:, :, None, :] - near_pos[:, None, :, None]
    distance = jnp.sqrt(jnp.sum(offsets * offsets, axis=0))
    centers = basis_width * jnp.arange(NB, dtype=jnp.float32)
    scaled = (distance[:, None, :, :] - centers[None, :, None, None]) / basis_width
    return (jnp.exp(-scaled * scaled) * live_flags[:, None, None, None]).astype(jnp.bfloat16)


def species_onehot(labels, width):
    return labels[:, None] == jnp.arange(width, dtype=jnp.int32)[None, :]


def embed_rows(labels, kind_vectors):
    onehot = species_onehot(labels, kind_vectors.shape[0]).astype(jnp.bfloat16)
    return jnp.dot(onehot, kind_vectors, preferred_element_type=jnp.float32).astype(jnp.bfloat16)


def inverse_mass(labels, kind_inertia):
    chosen_mass = jnp.where(
        species_onehot(labels, kind_inertia.shape[0]), kind_inertia[None, :], 0.0
    )
    return 1.0 / jnp.sum(chosen_mass, axis=1)


def tile_geometry(ext_pos, tile_lists, live_counts):
    tile_total = tile_lists.shape[0]
    near_all = jnp.transpose(
        ext_pos[:, : tile_total * TILE].reshape(3, tile_total, TILE), (1, 0, 2)
    )
    ext_tiled = ext_pos.reshape(3, -1, TILE)
    far_all = jnp.transpose(jnp.take(ext_tiled, tile_lists, axis=1), (1, 0, 2, 3))
    live_all = (jnp.arange(NEI, dtype=jnp.int32)[None, :] < live_counts[:, None]).astype(
        jnp.float32
    )
    return (near_all, far_all, live_all)


def tile_messages(geometry, ext_hidden, tile_lists, radial_row):
    near_all, far_all, live_all = geometry
    channels = ext_hidden.shape[1]
    feat_all = jnp.take(ext_hidden.reshape(-1, TILE, channels), tile_lists, axis=0)

    def one_tile(items):
        near_pos, far_pos, live_flags, far_feat = items
        basis_val = slot_basis(near_pos, far_pos, live_flags)
        summed = jnp.einsum(
            "kbij,kjc->bic", basis_val, far_feat, preferred_element_type=jnp.float32
        )
        return jnp.einsum("bic,bc->ic", summed, radial_row, precision=lax.Precision.HIGHEST)

    result = lax.map(one_tile, (near_all, far_all, live_all, feat_all))
    return result.reshape(-1, channels)


def refresh(hidden, messages, gain_row, mix_matrix):
    inverse = lax.rsqrt(jnp.mean(messages * messages, axis=-1, keepdims=True) + norm_eps)
    activation = jax.nn.silu(messages * inverse * gain_row).astype(jnp.bfloat16)
    return (
        hidden.astype(jnp.float32)
        + jnp.dot(activation, mix_matrix, preferred_element_type=jnp.float32)
    ).astype(jnp.bfloat16)


def tile_forces(geometry, query, ext_keys, tile_lists, push_distance_taper):
    near_all, far_all, live_all = geometry
    channels = query.shape[1]
    factor = 1.0 / math.sqrt(channels * NEI * TILE)
    asking_all = query.reshape(-1, TILE, channels)
    keys_all = jnp.take(ext_keys.reshape(-1, TILE, channels), tile_lists, axis=0)

    def one_tile(items):
        near_pos, far_pos, live_flags, asking, far_keys = items
        basis_val = slot_basis(near_pos, far_pos, live_flags)
        envelope = jnp.einsum(
            "kbij,b->kij",
            basis_val.astype(jnp.float32),
            push_distance_taper,
            precision=lax.Precision.HIGHEST,
        )
        scores = jnp.einsum("ic,kjc->kij", asking, far_keys, preferred_element_type=jnp.float32)
        pair_weight = scores * envelope * factor
        return (
            jnp.einsum("dkj,kij->di", far_pos, pair_weight, precision=lax.Precision.HIGHEST)
            - near_pos * jnp.sum(pair_weight, axis=(0, 2))[None, :]
        )

    result = lax.map(one_tile, (near_all, far_all, live_all, asking_all, keys_all))
    return jnp.transpose(result, (1, 0, 2)).reshape(3, -1)


def evaluate(
    displaced,
    labels,
    ghosts,
    tile_lists,
    live_counts,
    kind_vectors,
    stepwise_distance_coefficients,
    signal_scaling_factors,
    feature_blend_coefficients,
    target_projection_array,
    source_projection_array,
    push_distance_taper,
):
    ghost_count = ghosts.shape[0] // 2
    atom_count = displaced.shape[1]
    shift_vec = slab_width * (jnp.arange(3, dtype=jnp.int32) == 0).astype(jnp.float32)[:, None]
    packed_pos = jnp.take(displaced, ghosts, axis=1)
    bordered_pos = with_halo(packed_pos, (("dom", 1),), ghost_count)
    ext_pos = jnp.concatenate(
        [
            displaced,
            bordered_pos[:, :ghost_count] - shift_vec,
            bordered_pos[:, 3 * ghost_count :] + shift_vec,
        ],
        axis=1,
    )
    geometry = tile_geometry(ext_pos, tile_lists, live_counts)
    bordered_labels = with_halo(jnp.take(labels, ghosts), (("dom", 0),), ghost_count)
    ext_labels = jnp.concatenate(
        [labels, bordered_labels[:ghost_count], bordered_labels[3 * ghost_count :]]
    )
    ext_hidden = embed_rows(ext_labels, kind_vectors)
    hidden = ext_hidden[:atom_count]
    messages = tile_messages(geometry, ext_hidden, tile_lists, stepwise_distance_coefficients[0])
    hidden = refresh(hidden, messages, signal_scaling_factors[0], feature_blend_coefficients[0])
    bordered_middle = with_halo(jnp.take(hidden, ghosts, axis=0), (("dom", 0),), ghost_count)
    ext_hidden = jnp.concatenate(
        [hidden, bordered_middle[:ghost_count], bordered_middle[3 * ghost_count :]], axis=0
    )
    messages = tile_messages(geometry, ext_hidden, tile_lists, stepwise_distance_coefficients[1])
    hidden = refresh(hidden, messages, signal_scaling_factors[1], feature_blend_coefficients[1])
    query = jnp.dot(hidden, target_projection_array, preferred_element_type=jnp.float32).astype(
        jnp.bfloat16
    )
    bordered_final = with_halo(jnp.take(hidden, ghosts, axis=0), (("dom", 0),), ghost_count)
    final_ext = jnp.concatenate(
        [hidden, bordered_final[:ghost_count], bordered_final[3 * ghost_count :]], axis=0
    )
    ext_keys = jnp.dot(
        final_ext, source_projection_array, preferred_element_type=jnp.float32
    ).astype(jnp.bfloat16)
    return tile_forces(geometry, query, ext_keys, tile_lists, push_distance_taper)


def pick_partner(own_parts, low_parts, high_parts, swap_counterpart, thermal_copy_entry):
    return tuple(
        (
            jnp.where(
                swap_counterpart == thermal_copy_entry + 1,
                high_part,
                jnp.where(swap_counterpart == thermal_copy_entry - 1, low_part, own_part),
            )
            for own_part, low_part, high_part in zip(own_parts, low_parts, high_parts)
        )
    )


def local(
    particle_locations,
    particle_speeds,
    current_pushes,
    particle_kinds,
    halo_particle_labels,
    adjacent_block_labels,
    adjacent_place_totals,
    kind_vectors,
    kind_inertia,
    stepwise_distance_coefficients,
    signal_scaling_factors,
    feature_blend_coefficients,
    target_projection_array,
    source_projection_array,
    push_distance_taper,
    thermal_levels,
    granted_swaps,
):
    coords = particle_locations[0]
    speeds = particle_speeds[0]
    old_force = current_pushes[0]
    labels = particle_kinds[0]
    ghosts = halo_particle_labels[0]
    tile_lists = adjacent_block_labels[0]
    live_counts = adjacent_place_totals[0]
    thermal_copy_entry = lax.axis_index("rep")
    swap_counterpart = granted_swaps[thermal_copy_entry]
    thermal_quotient = jnp.sqrt(
        thermal_levels[thermal_copy_entry] / thermal_levels[swap_counterpart]
    )
    inv_mass = inverse_mass(labels, kind_inertia)
    displaced = (
        coords + time_step * speeds + 0.5 * time_step * time_step * old_force * inv_mass[None, :]
    )
    half_speed = speeds + 0.5 * time_step * old_force * inv_mass[None, :]
    updated_push = evaluate(
        displaced,
        labels,
        ghosts,
        tile_lists,
        live_counts,
        kind_vectors,
        stepwise_distance_coefficients,
        signal_scaling_factors,
        feature_blend_coefficients,
        target_projection_array,
        source_projection_array,
        push_distance_taper,
    )
    updated_velocity = half_speed + 0.5 * time_step * updated_push * inv_mass[None, :]
    lower_state = (
        from_behind(displaced.astype(jnp.bfloat16), "rep", 1).astype(displaced.dtype),
        from_behind(updated_velocity.astype(jnp.bfloat16), "rep", 1).astype(updated_velocity.dtype),
        from_behind(updated_push.astype(jnp.bfloat16), "rep", 1).astype(updated_push.dtype),
    )
    upper_state = (
        from_behind(displaced.astype(jnp.bfloat16), "rep", -1).astype(displaced.dtype),
        from_behind(updated_velocity.astype(jnp.bfloat16), "rep", -1).astype(
            updated_velocity.dtype
        ),
        from_behind(updated_push.astype(jnp.bfloat16), "rep", -1).astype(updated_push.dtype),
    )
    final_pos, selected_velocity, final_force = pick_partner(
        (displaced, updated_velocity, updated_push),
        lower_state,
        upper_state,
        swap_counterpart,
        thermal_copy_entry,
    )
    closing_velocity = selected_velocity * thermal_quotient
    return (final_pos[None], closing_velocity[None], final_force[None])


def solution(mesh):
    in_specs = (
        P("rep", None, "dom"),
        P("rep", None, "dom"),
        P("rep", None, "dom"),
        P("rep", "dom"),
        P("rep", "dom"),
        P("rep", "dom", None),
        P("rep", "dom"),
        P(),
        P(),
        P(),
        P(),
        P(),
        P(),
        P(),
        P(),
        P(),
        P(),
    )
    out_specs = (P("rep", None, "dom"), P("rep", None, "dom"), P("rep", None, "dom"))
    return jax.shard_map(local, mesh=mesh, in_specs=in_specs, out_specs=out_specs, check_vma=False)
```

profile of v0, /device:TPU:1, one launch (start us, length us, event | category | flops | bytes accessed | tf_op | source)
XLA Modules:
  0.0 137.8 jit_solution(1485806381351467666)
XLA Ops:
  0.7 0.8 select_reduce_fusion
  1.5 0.9 copy.142
  2.4 0.9 copy.143
  3.7 3.2 %gather_fusion.2 = s32[768]{0:T(1024)S(1)} fusion(s32[1024]{0:T(1024)S(1)} %bitcast.241, s32[1024]{0:T(1024)S(1)} %pad_clamp_fusion.3), kind=kCustom, calls=%fused_computation.7 | custom fusion | bytes 9216 | tf_op jit(solution)/shard_map/jit(_take)/gather | solution.py:159
  6.9 0.9 fusion.68
  7.9 1.6 %gather_fusion = f32[768,3]{1,0:T(8,128)S(1)} fusion(f32[3,1024]{0,1:T(8,128)S(1)} %get-tuple-element.315, s32[1024]{0:T(1024)S(1)} %pad_clamp_fusion.3), kind=kCustom, calls=%fused_computation.5 | custom fusion | bytes 21504 | tf_op jit(solution)/shard_map/jit(_take)/gather | solution.py:148
  9.7 2.1 %collective-permute-start.2 = (f32[3,384]{1,0:T(4,128)S(1)}, f32[3,384]{1,0:T(4,128)S(1)}, u32[]{:S(2)}, u32[]{:S(2)}) collective-permute-start(f32[3,384]{1,0:T(4,128)S(1)} %get-tuple-element.323), channel_id=1, source_target_pairs={{0,1},{1,0},{2,3},{3,2},{4,5},{5,4},{6,7},{7,6},{8,9},{9,8},{10,11... | collective-permute-start | bytes 13832 | tf_op jit(solution)/shard_map/ppermute | solution.py:26
  11.9 1.4 %collective-permute-start.4 = (s32[384]{0:T(512)S(1)}, s32[384]{0:T(512)S(1)}, u32[]{:S(2)}, u32[]{:S(2)}) collective-permute-start(s32[384]{0:T(512)S(1)} %get-tuple-element.331), channel_id=1, source_target_pairs={{0,1},{1,0},{2,3},{3,2},{4,5},{5,4},{6,7},{7,6},{8,9},{9,8},{10,11... | collective-permute-start | bytes 4616 | tf_op jit(solution)/shard_map/ppermute | solution.py:26
  14.7 1.3 collective-permute-done.5
  17.2 1.1 broadcast_select_fusion.1
  19.2 15.8 %while.30 = (s32[]{:T(128)}, f32[8,128,128]{2,1,0:T(8,128)S(1)}, f32[8,3,4,128]{3,2,1,0:T(4,128)S(1)}, f32[8,3,128]{2,1,0:T(4,128)S(1)}, f32[8,4]{1,0:T(8,128)S(...) while((s32[]{:T(128)}, f32[8,128,128]{2,1,0:T(8,128)S(1)}, ...), condition=%wide.region_3.5_spmd, body=%wide.region_1.0_spmd.sunk | while | flops 138133520 | bytes 1404117 | solution.py:91
  19.5 1.6 %fusion.102 = f32[128,128]{0,1:T(8,128)S(1)} fusion(f32[4]{0:T(128)S(1)} %fusion.101, f32[8]{0:T(128)S(1)} %iota_multiply_fusion.6, f32[4,128,128]{2,1,0:T(8,128)S(1)} %sqrt.32, f32[128,8]{0,1:T(8,128)S(1)} %bitcast.258, bf16[8,4,128,128]{3,2,1,0:T(8,128)(2,1)} %get-tuple-element.499, s32[]{:T(128)} %get-tuple-element.486), kind=kOutput, calls=%fused_computation.39.clone.1 | convolution fusion | flops 137609216 | bytes 463408 | tf_op jit(solution)/shard_map/while/body/eval_jaxpr/kbij,kjc->bic/dot_general | solution.py:86
  21.5 1.6 %fusion.102 = f32[128,128]{0,1:T(8,128)S(1)} fusion(f32[4]{0:T(128)S(1)} %fusion.101, f32[8]{0:T(128)S(1)} %iota_multiply_fusion.6, f32[4,128,128]{2,1,0:T(8,128)S(1)} %sqrt.32, f32[128,8]{0,1:T(8,128)S(1)} %bitcast.258, bf16[8,4,128,128]{3,2,1,0:T(8,128)(2,1)} %get-tuple-element.499, s32[]{:T(128)} %get-tuple-element.486), kind=kOutput, calls=%fused_computation.39.clone.1 | convolution fusion | flops 137609216 | bytes 463408 | tf_op jit(solution)/shard_map/while/body/eval_jaxpr/kbij,kjc->bic/dot_general | solution.py:86
  23.4 1.6 %fusion.102 = f32[128,128]{0,1:T(8,128)S(1)} fusion(f32[4]{0:T(128)S(1)} %fusion.101, f32[8]{0:T(128)S(1)} %iota_multiply_fusion.6, f32[4,128,128]{2,1,0:T(8,128)S(1)} %sqrt.32, f32[128,8]{0,1:T(8,128)S(1)} %bitcast.258, bf16[8,4,128,128]{3,2,1,0:T(8,128)(2,1)} %get-tuple-element.499, s32[]{:T(128)} %get-tuple-element.486), kind=kOutput, calls=%fused_computation.39.clone.1 | convolution fusion | flops 137609216 | bytes 463408 | tf_op jit(solution)/shard_map/while/body/eval_jaxpr/kbij,kjc->bic/dot_general | solution.py:86
  25.4 1.6 %fusion.102 = f32[128,128]{0,1:T(8,128)S(1)} fusion(f32[4]{0:T(128)S(1)} %fusion.101, f32[8]{0:T(128)S(1)} %iota_multiply_fusion.6, f32[4,128,128]{2,1,0:T(8,128)S(1)} %sqrt.32, f32[128,8]{0,1:T(8,128)S(1)} %bitcast.258, bf16[8,4,128,128]{3,2,1,0:T(8,128)(2,1)} %get-tuple-element.499, s32[]{:T(128)} %get-tuple-element.486), kind=kOutput, calls=%fused_computation.39.clone.1 | convolution fusion | flops 137609216 | bytes 463408 | tf_op jit(solution)/shard_map/while/body/eval_jaxpr/kbij,kjc->bic/dot_general | solution.py:86
  27.4 1.6 %fusion.102 = f32[128,128]{0,1:T(8,128)S(1)} fusion(f32[4]{0:T(128)S(1)} %fusion.101, f32[8]{0:T(128)S(1)} %iota_multiply_fusion.6, f32[4,128,128]{2,1,0:T(8,128)S(1)} %sqrt.32, f32[128,8]{0,1:T(8,128)S(1)} %bitcast.258, bf16[8,4,128,128]{3,2,1,0:T(8,128)(2,1)} %get-tuple-element.499, s32[]{:T(128)} %get-tuple-element.486), kind=kOutput, calls=%fused_computation.39.clone.1 | convolution fusion | flops 137609216 | bytes 463408 | tf_op jit(solution)/shard_map/while/body/eval_jaxpr/kbij,kjc->bic/dot_general | solution.py:86
  29.4 1.6 %fusion.102 = f32[128,128]{0,1:T(8,128)S(1)} fusion(f32[4]{0:T(128)S(1)} %fusion.101, f32[8]{0:T(128)S(1)} %iota_multiply_fusion.6, f32[4,128,128]{2,1,0:T(8,128)S(1)} %sqrt.32, f32[128,8]{0,1:T(8,128)S(1)} %bitcast.258, bf16[8,4,128,128]{3,2,1,0:T(8,128)(2,1)} %get-tuple-element.499, s32[]{:T(128)} %get-tuple-element.486), kind=kOutput, calls=%fused_computation.39.clone.1 | convolution fusion | flops 137609216 | bytes 463408 | tf_op jit(solution)/shard_map/while/body/eval_jaxpr/kbij,kjc->bic/dot_general | solution.py:86
  31.3 1.6 %fusion.102 = f32[128,128]{0,1:T(8,128)S(1)} fusion(f32[4]{0:T(128)S(1)} %fusion.101, f32[8]{0:T(128)S(1)} %iota_multiply_fusion.6, f32[4,128,128]{2,1,0:T(8,128)S(1)} %sqrt.32, f32[128,8]{0,1:T(8,128)S(1)} %bitcast.258, bf16[8,4,128,128]{3,2,1,0:T(8,128)(2,1)} %get-tuple-element.499, s32[]{:T(128)} %get-tuple-element.486), kind=kOutput, calls=%fused_computation.39.clone.1 | convolution fusion | flops 137609216 | bytes 463408 | tf_op jit(solution)/shard_map/while/body/eval_jaxpr/kbij,kjc->bic/dot_general | solution.py:86
  33.3 1.6 %fusion.102 = f32[128,128]{0,1:T(8,128)S(1)} fusion(f32[4]{0:T(128)S(1)} %fusion.101, f32[8]{0:T(128)S(1)} %iota_multiply_fusion.6, f32[4,128,128]{2,1,0:T(8,128)S(1)} %sqrt.32, f32[128,8]{0,1:T(8,128)S(1)} %bitcast.258, bf16[8,4,128,128]{3,2,1,0:T(8,128)(2,1)} %get-tuple-element.499, s32[]{:T(128)} %get-tuple-element.486), kind=kOutput, calls=%fused_computation.39.clone.1 | convolution fusion | flops 137609216 | bytes 463408 | tf_op jit(solution)/shard_map/while/body/eval_jaxpr/kbij,kjc->bic/dot_general | solution.py:86
  36.0 1.9 %gather_fusion.4 = bf16[768,128]{1,0:T(8,128)(2,1)S(1)} fusion(bf16[1024,128]{1,0:T(8,128)(2,1)S(1)} %fusion.45, s32[1024]{0:T(1024)S(1)} %pad_clamp_fusion), kind=kCustom, calls=%fused_computation.1.clone | custom fusion | bytes 396288 | tf_op jit(solution)/shard_map/jit(_take)/gather | solution.py:167
  38.3 1.3 collective-permute-start.7
  39.7 2.0 %collective-permute-done.6 = bf16[384,128]{1,0:T(8,128)(2,1)S(1)} collective-permute-done((bf16[384,128]{1,0:T(8,128)(2,1)S(1)}, bf16[384,128]{1,0:T(8,128)(2,1)S(1)}, u32[]{:S(2)}, u32[]{:S(2)}) %collective-permute-start.6) | collective-permute-done | bytes 98336 | tf_op jit(solution)/shard_map/ppermute | solution.py:26
  41.7 1.1 collective-permute-done.7
  43.5 1.1 broadcast_select_fusion
  44.7 15.8 %while.31 = (s32[]{:T(128)}, f32[8,128,128]{2,1,0:T(8,128)S(1)}, f32[8,3,4,128]{3,2,1,0:T(4,128)S(1)}, f32[8,3,128]{2,1,0:T(4,128)S(1)}, f32[8,4]{1,0:T(8,128)S(...) while((s32[]{:T(128)}, f32[8,128,128]{2,1,0:T(8,128)S(1)}, ...), condition=%wide.region_7.10_spmd, body=%wide.region_5.9_spmd.sunk | while | flops 138133520 | bytes 1404117 | solution.py:91
  45.0 1.6 %fusion.106 = f32[128,128]{0,1:T(8,128)S(1)} fusion(f32[4]{0:T(128)S(1)} %fusion.105, f32[8]{0:T(128)S(1)} %iota_multiply_fusion.7, f32[4,128,128]{2,1,0:T(8,128)S(1)} %sqrt.33, f32[128,8]{0,1:T(8,128)S(1)} %bitcast.257, bf16[8,4,128,128]{3,2,1,0:T(8,128)(2,1)} %get-tuple-element.523, s32[]{:T(128)} %get-tuple-element.510), kind=kOutput, calls=%fused_computation.60.clone.1 | convolution fusion | flops 137609216 | bytes 463408 | tf_op jit(solution)/shard_map/while/body/eval_jaxpr/kbij,kjc->bic/dot_general | solution.py:86
  46.9 1.6 %fusion.106 = f32[128,128]{0,1:T(8,128)S(1)} fusion(f32[4]{0:T(128)S(1)} %fusion.105, f32[8]{0:T(128)S(1)} %iota_multiply_fusion.7, f32[4,128,128]{2,1,0:T(8,128)S(1)} %sqrt.33, f32[128,8]{0,1:T(8,128)S(1)} %bitcast.257, bf16[8,4,128,128]{3,2,1,0:T(8,128)(2,1)} %get-tuple-element.523, s32[]{:T(128)} %get-tuple-element.510), kind=kOutput, calls=%fused_computation.60.clone.1 | convolution fusion | flops 137609216 | bytes 463408 | tf_op jit(solution)/shard_map/while/body/eval_jaxpr/kbij,kjc->bic/dot_general | solution.py:86
  48.9 1.6 %fusion.106 = f32[128,128]{0,1:T(8,128)S(1)} fusion(f32[4]{0:T(128)S(1)} %fusion.105, f32[8]{0:T(128)S(1)} %iota_multiply_fusion.7, f32[4,128,128]{2,1,0:T(8,128)S(1)} %sqrt.33, f32[128,8]{0,1:T(8,128)S(1)} %bitcast.257, bf16[8,4,128,128]{3,2,1,0:T(8,128)(2,1)} %get-tuple-element.523, s32[]{:T(128)} %get-tuple-element.510), kind=kOutput, calls=%fused_computation.60.clone.1 | convolution fusion | flops 137609216 | bytes 463408 | tf_op jit(solution)/shard_map/while/body/eval_jaxpr/kbij,kjc->bic/dot_general | solution.py:86
  50.9 1.6 %fusion.106 = f32[128,128]{0,1:T(8,128)S(1)} fusion(f32[4]{0:T(128)S(1)} %fusion.105, f32[8]{0:T(128)S(1)} %iota_multiply_fusion.7, f32[4,128,128]{2,1,0:T(8,128)S(1)} %sqrt.33, f32[128,8]{0,1:T(8,128)S(1)} %bitcast.257, bf16[8,4,128,128]{3,2,1,0:T(8,128)(2,1)} %get-tuple-element.523, s32[]{:T(128)} %get-tuple-element.510), kind=kOutput, calls=%fused_computation.60.clone.1 | convolution fusion | flops 137609216 | bytes 463408 | tf_op jit(solution)/shard_map/while/body/eval_jaxpr/kbij,kjc->bic/dot_general | solution.py:86
  52.9 1.6 %fusion.106 = f32[128,128]{0,1:T(8,128)S(1)} fusion(f32[4]{0:T(128)S(1)} %fusion.105, f32[8]{0:T(128)S(1)} %iota_multiply_fusion.7, f32[4,128,128]{2,1,0:T(8,128)S(1)} %sqrt.33, f32[128,8]{0,1:T(8,128)S(1)} %bitcast.257, bf16[8,4,128,128]{3,2,1,0:T(8,128)(2,1)} %get-tuple-element.523, s32[]{:T(128)} %get-tuple-element.510), kind=kOutput, calls=%fused_computation.60.clone.1 | convolution fusion | flops 137609216 | bytes 463408 | tf_op jit(solution)/shard_map/while/body/eval_jaxpr/kbij,kjc->bic/dot_general | solution.py:86
  54.8 1.6 %fusion.106 = f32[128,128]{0,1:T(8,128)S(1)} fusion(f32[4]{0:T(128)S(1)} %fusion.105, f32[8]{0:T(128)S(1)} %iota_multiply_fusion.7, f32[4,128,128]{2,1,0:T(8,128)S(1)} %sqrt.33, f32[128,8]{0,1:T(8,128)S(1)} %bitcast.257, bf16[8,4,128,128]{3,2,1,0:T(8,128)(2,1)} %get-tuple-element.523, s32[]{:T(128)} %get-tuple-element.510), kind=kOutput, calls=%fused_computation.60.clone.1 | convolution fusion | flops 137609216 | bytes 463408 | tf_op jit(solution)/shard_map/while/body/eval_jaxpr/kbij,kjc->bic/dot_general | solution.py:86
  56.8 1.6 %fusion.106 = f32[128,128]{0,1:T(8,128)S(1)} fusion(f32[4]{0:T(128)S(1)} %fusion.105, f32[8]{0:T(128)S(1)} %iota_multiply_fusion.7, f32[4,128,128]{2,1,0:T(8,128)S(1)} %sqrt.33, f32[128,8]{0,1:T(8,128)S(1)} %bitcast.257, bf16[8,4,128,128]{3,2,1,0:T(8,128)(2,1)} %get-tuple-element.523, s32[]{:T(128)} %get-tuple-element.510), kind=kOutput, calls=%fused_computation.60.clone.1 | convolution fusion | flops 137609216 | bytes 463408 | tf_op jit(solution)/shard_map/while/body/eval_jaxpr/kbij,kjc->bic/dot_general | solution.py:86
  58.8 1.6 %fusion.106 = f32[128,128]{0,1:T(8,128)S(1)} fusion(f32[4]{0:T(128)S(1)} %fusion.105, f32[8]{0:T(128)S(1)} %iota_multiply_fusion.7, f32[4,128,128]{2,1,0:T(8,128)S(1)} %sqrt.33, f32[128,8]{0,1:T(8,128)S(1)} %bitcast.257, bf16[8,4,128,128]{3,2,1,0:T(8,128)(2,1)} %get-tuple-element.523, s32[]{:T(128)} %get-tuple-element.510), kind=kOutput, calls=%fused_computation.60.clone.1 | convolution fusion | flops 137609216 | bytes 463408 | tf_op jit(solution)/shard_map/while/body/eval_jaxpr/kbij,kjc->bic/dot_general | solution.py:86
  61.5 1.9 %gather_fusion.6 = bf16[768,128]{1,0:T(8,128)(2,1)S(1)} fusion(bf16[1024,128]{1,0:T(8,128)(2,1)S(1)} %fusion.46, s32[1024]{0:T(1024)S(1)} %pad_clamp_fusion), kind=kCustom, calls=%fused_computation.4.clone | custom fusion | bytes 396288 | tf_op jit(solution)/shard_map/jit(_take)/gather | solution.py:176
  64.1 1.1 collective-permute-start.9
  65.4 1.8 %collective-permute-done.8 = bf16[384,128]{1,0:T(8,128)(2,1)S(1)} collective-permute-done((bf16[384,128]{1,0:T(8,128)(2,1)S(1)}, bf16[384,128]{1,0:T(8,128)(2,1)S(1)}, u32[]{:S(2)}, u32[]{:S(2)}) %collective-permute-start.8) | collective-permute-done | bytes 98336 | tf_op jit(solution)/shard_map/ppermute | solution.py:26
  67.2 1.1 collective-permute-done.9
  69.2 1.1 broadcast_select_fusion.2
  70.4 29.9 %while.32 = (s32[]{:T(128)}, f32[8,3,128]{2,1,0:T(4,128)S(1)}, f32[8,3,4,128]{3,1,2,0:T(4,128)S(1)}, bf16[8,4,128,128]{3,2,1,0:T(8,128)(2,1)}, bf16[8,128,128]{2...) while((s32[]{:T(128)}, f32[8,3,128]{2,1,0:T(4,128)S(1)}, ...), condition=%wide.region_12.15_spmd, body=%wide.region_9.14_spmd.sunk | while | flops 29295240 | bytes 4933369 | solution.py:127
  71.3 1.3 fusion.112
  72.7 1.2 fusion.113
  75.0 1.3 fusion.112
  76.4 1.2 fusion.113
  78.8 1.3 fusion.112
  80.2 1.2 fusion.113
  82.5 1.3 fusion.112
  83.9 1.2 fusion.113
  86.2 1.3 fusion.112
  87.7 1.2 fusion.113
  90.0 1.3 fusion.112
  91.4 1.1 fusion.113
  93.7 1.3 fusion.112
  95.1 1.1 fusion.113
  97.4 1.3 fusion.112
  98.9 1.2 fusion.113
  100.6 6.6 %collective-permute-start.12 = (bf16[3,1024]{0,1:T(8,128)(2,1)S(1)}, bf16[3,1024]{0,1:T(8,128)(2,1)S(1)}, u32[]{:S(2)}, u32[]{:S(2)}) collective-permute-start(bf16[3,1024]{0,1:T(8,128)(2,1)S(1)} %bitcast_convert_fusion), channel_id=1, source_target_pairs={{2,0},{4,2},{6,4},{8,6},{10,8},{12,10},{14,12},{16,14},{18,16},{20... | collective-permute-start | bytes 18440 | tf_op jit(solution)/shard_map/ppermute | solution.py:38
  107.1 3.0 %collective-permute-start.13 = (bf16[3,1024]{0,1:T(8,128)(2,1)S(1)}, bf16[3,1024]{0,1:T(8,128)(2,1)S(1)}, u32[]{:S(2)}, u32[]{:S(2)}) collective-permute-start(bf16[3,1024]{0,1:T(8,128)(2,1)S(1)} %bitcast_convert_fusion), channel_id=1, source_target_pairs={{0,2},{2,4},{4,6},{6,8},{8,10},{10,12},{12,14},{14,16},{16,18},{18... | collective-permute-start | bytes 18440 | tf_op jit(solution)/shard_map/ppermute | solution.py:38
  110.2 1.9 %collective-permute-start = (bf16[3,1024]{0,1:T(8,128)(2,1)S(1)}, bf16[3,1024]{0,1:T(8,128)(2,1)}, u32[]{:S(2)}, u32[]{:S(2)}) collective-permute-start(bf16[3,1024]{0,1:T(8,128)(2,1)S(1)} %copy-done.2), channel_id=1, source_target_pairs={{2,0},{4,2},{6,4},{8,6},{10,8},{12,10},{14,12},{16,14},{18,16},{20... | collective-permute-start | bytes 18440 | tf_op jit(solution)/shard_map/ppermute | solution.py:38
  112.1 3.6 %collective-permute-start.1 = (bf16[3,1024]{0,1:T(8,128)(2,1)S(1)}, bf16[3,1024]{0,1:T(8,128)(2,1)}, u32[]{:S(2)}, u32[]{:S(2)}) collective-permute-start(bf16[3,1024]{0,1:T(8,128)(2,1)S(1)} %copy-done.2), channel_id=1, source_target_pairs={{0,2},{2,4},{4,6},{6,8},{8,10},{10,12},{12,14},{14,16},{16,18},{18... | collective-permute-start | bytes 18440 | tf_op jit(solution)/shard_map/ppermute | solution.py:38
  123.0 2.0 %fusion.66 = (bf16[3,1024]{0,1:T(8,128)(2,1)}, f32[3,1024]{0,1:T(8,128)S(1)}, f32[3,1024]{0,1:T(8,128)S(1)}) fusion(f32[3,8,128]{0,2,1:T(8,128)S(1)} %copy.159, f32[1024]{0:T(1024)S(1)} %get-tuple-element.327, f32[1,3,1024]{1,2,0:T(8,128)S(1)} %copy.143, f32[1,3,1024]{1,2,0:T(8,128)S(1)} %copy.142, bf16[3,1024]{0,1:T(8,128)(2,1)} %copy-done.4, pred[]{:T(512)S(6)} %eq.52, ...), kind=kLoop, calls=%fused_computation.152 | loop fusion | flops 27648 | bytes 83970 | tf_op jit(solution)/shard_map/convert_element_type | solution.py:257
  125.0 1.9 %collective-permute-start.10 = (bf16[3,1024]{0,1:T(8,128)(2,1)}, bf16[3,1024]{0,1:T(8,128)(2,1)S(1)}, u32[]{:S(2)}, u32[]{:S(2)}) collective-permute-start(bf16[3,1024]{0,1:T(8,128)(2,1)} %get-tuple-element.310), channel_id=1, source_target_pairs={{2,0},{4,2},{6,4},{8,6},{10,8},{12,10},{14,12},{16,14},{18,16},{20... | collective-permute-start | bytes 18440 | tf_op jit(solution)/shard_map/ppermute | solution.py:38
  126.9 3.6 %collective-permute-start.11 = (bf16[3,1024]{0,1:T(8,128)(2,1)}, bf16[3,1024]{0,1:T(8,128)(2,1)S(1)}, u32[]{:S(2)}, u32[]{:S(2)}) collective-permute-start(bf16[3,1024]{0,1:T(8,128)(2,1)} %get-tuple-element.310), channel_id=1, source_target_pairs={{0,2},{2,4},{4,6},{6,8},{8,10},{10,12},{12,14},{14,16},{16,18},{18... | collective-permute-start | bytes 18440 | tf_op jit(solution)/shard_map/ppermute | solution.py:38
  130.6 1.1 select_bitcast_fusion
  133.3 3.7 %collective-permute-done.11 = bf16[3,1024]{0,1:T(8,128)(2,1)S(1)} collective-permute-done((bf16[3,1024]{0,1:T(8,128)(2,1)}, bf16[3,1024]{0,1:T(8,128)(2,1)S(1)}, u32[]{:S(2)}, u32[]{:S(2)}) %collective-permute-start.11) | collective-permute-done | bytes 6176 | tf_op jit(solution)/shard_map/ppermute | solution.py:38
  (311 shorter events, 28.2 us)
Async XLA Ops:
  0.6 67.6 %copy-start = (bf16[128,128]{1,0:T(8,128)(2,1)S(1)}, bf16[128,128]{1,0:T(8,128)(2,1)}, u32[]{:S(2)}) copy-start(bf16[128,128]{1,0:T(8,128)(2,1)} %param.40) | copy-start | bytes 98308
  0.6 3.0 %copy-start.1 = (s32[1,1024]{1,0:T(1,128)S(1)}, s32[1,1024]{1,0:T(1,128)}, u32[]{:S(2)}) copy-start(s32[1,1024]{1,0:T(1,128)} %param.30) | copy-start | bytes 12292
  0.7 2.7 %copy-start.8 = (f32[1,3,1024]{2,0,1:T(1,128)S(1)}, f32[1,3,1024]{2,0,1:T(1,128)}, u32[]{:S(2)}) copy-start(f32[1,3,1024]{2,0,1:T(1,128)} %param.27) | copy-start | bytes 36868
  0.7 2.9 %copy-start.13 = (s32[1,768]{1,0:T(1,128)S(1)}, s32[1,768]{1,0:T(1,128)}, u32[]{:S(2)}) copy-start(s32[1,768]{1,0:T(1,128)} %param.31) | copy-start | bytes 9220
  6.9 6.5 %copy-start.11 = (s32[1,8,4]{1,2,0:T(4,128)S(1)}, s32[1,8,4]{1,2,0:T(4,128)}, u32[]{:S(2)}) copy-start(s32[1,8,4]{1,2,0:T(4,128)} %param.32) | copy-start | bytes 388
  6.9 6.5 %copy-start.7 = (f32[1,3,1024]{2,0,1:T(1,128)S(1)}, f32[1,3,1024]{2,0,1:T(1,128)}, u32[]{:S(2)}) copy-start(f32[1,3,1024]{2,0,1:T(1,128)} %param.28) | copy-start | bytes 36868
  6.9 6.9 %copy-start.19 = (s32[1,8]{1,0:T(1,128)S(1)}, s32[1,8]{1,0:T(1,128)}, u32[]{:S(2)}) copy-start(s32[1,8]{1,0:T(1,128)} %param.33) | copy-start | bytes 100
  6.9 6.9 %copy-start.14 = (f32[2,8,128]{2,1,0:T(8,128)S(1)}, f32[2,8,128]{2,1,0:T(8,128)}, u32[]{:S(2)}) copy-start(f32[2,8,128]{2,1,0:T(8,128)} %param.36) | copy-start | bytes 24580
  6.9 6.9 %copy-start.18 = (f32[2,128]{1,0:T(2,128)S(1)}, f32[2,128]{1,0:T(2,128)}, u32[]{:S(2)}) copy-start(f32[2,128]{1,0:T(2,128)} %param.37) | copy-start | bytes 3076
  6.9 7.4 %copy-start.9 = (f32[1,3,1024]{2,0,1:T(1,128)S(1)}, f32[1,3,1024]{2,0,1:T(1,128)}, u32[]{:S(2)}) copy-start(f32[1,3,1024]{2,0,1:T(1,128)} %param.29) | copy-start | bytes 36868
  7.9 8.1 %copy-start.15 = (bf16[16,128]{1,0:T(8,128)(2,1)S(1)}, bf16[16,128]{1,0:T(8,128)(2,1)}, u32[]{:S(2)}) copy-start(bf16[16,128]{1,0:T(8,128)(2,1)} %param.34) | copy-start | bytes 12292
  9.7 8.7 %collective-permute-start.2 = (f32[3,384]{1,0:T(4,128)S(1)}, f32[3,384]{1,0:T(4,128)S(1)}, u32[]{:S(2)}, u32[]{:S(2)}) collective-permute-start(f32[3,384]{1,0:T(4,128)S(1)} %get-tuple-element.323), channel_id=1, source_target_pairs={{0,1},{1,0},{2,3},{3,2},{4,5},{5,4},{6,7},{7,6},{8,9},{9,8},{10,11... | collective-permute-start | bytes 13832 | tf_op jit(solution)/shard_map/ppermute | solution.py:26
  11.8 6.5 %collective-permute-start.3 = (f32[3,384]{1,0:T(4,128)S(1)}, f32[3,384]{1,0:T(4,128)S(1)}, u32[]{:S(2)}, u32[]{:S(2)}) collective-permute-start(f32[3,384]{1,0:T(4,128)S(1)} %get-tuple-element.324), channel_id=1, source_target_pairs={{1,0},{0,1},{3,2},{2,3},{5,4},{4,5},{7,6},{6,7},{9,8},{8,9},{11,10... | collective-permute-start | bytes 13832 | tf_op jit(solution)/shard_map/ppermute | solution.py:28
  11.9 2.8 %collective-permute-start.4 = (s32[384]{0:T(512)S(1)}, s32[384]{0:T(512)S(1)}, u32[]{:S(2)}, u32[]{:S(2)}) collective-permute-start(s32[384]{0:T(512)S(1)} %get-tuple-element.331), channel_id=1, source_target_pairs={{0,1},{1,0},{2,3},{3,2},{4,5},{5,4},{6,7},{7,6},{8,9},{9,8},{10,11... | collective-permute-start | bytes 4616 | tf_op jit(solution)/shard_map/ppermute | solution.py:26
  13.3 2.7 %collective-permute-start.5 = (s32[384]{0:T(512)S(1)}, s32[384]{0:T(512)S(1)}, u32[]{:S(2)}, u32[]{:S(2)}) collective-permute-start(s32[384]{0:T(512)S(1)} %get-tuple-element.332), channel_id=1, source_target_pairs={{1,0},{0,1},{3,2},{2,3},{5,4},{4,5},{7,6},{6,7},{9,8},{8,9},{11,10... | collective-permute-start | bytes 4616 | tf_op jit(solution)/shard_map/ppermute | solution.py:28
  19.2 16.0 %copy-start.17 = (f32[128]{0:T(128)S(1)}, f32[128]{0:T(128)}, u32[]{:S(2)}) copy-start(f32[128]{0:T(128)} %get-tuple-element.334) | copy-start | bytes 1540
  35.0 0.8 copy-start.5
  38.1 3.5 %collective-permute-start.6 = (bf16[384,128]{1,0:T(8,128)(2,1)S(1)}, bf16[384,128]{1,0:T(8,128)(2,1)S(1)}, u32[]{:S(2)}, u32[]{:S(2)}) collective-permute-start(bf16[384,128]{1,0:T(8,128)(2,1)S(1)} %get-tuple-element.321), channel_id=1, source_target_pairs={{0,1},{1,0},{2,3},{3,2},{4,5},{5,4},{6,7},{7,6},{8,9},{9,8},{10,11... | collective-permute-start | bytes 294920 | tf_op jit(solution)/shard_map/ppermute | solution.py:26
  38.3 4.4 %collective-permute-start.7 = (bf16[384,128]{1,0:T(8,128)(2,1)S(1)}, bf16[384,128]{1,0:T(8,128)(2,1)S(1)}, u32[]{:S(2)}, u32[]{:S(2)}) collective-permute-start(bf16[384,128]{1,0:T(8,128)(2,1)S(1)} %get-tuple-element.322), channel_id=1, source_target_pairs={{1,0},{0,1},{3,2},{2,3},{5,4},{4,5},{7,6},{6,7},{9,8},{8,9},{11,10... | collective-permute-start | bytes 294920 | tf_op jit(solution)/shard_map/ppermute | solution.py:28
  60.5 0.8 copy-start.6
  61.5 3.6 %copy-start.10 = (bf16[128,128]{1,0:T(8,128)(2,1)S(1)}, bf16[128,128]{1,0:T(8,128)(2,1)}, u32[]{:S(2)}) copy-start(bf16[128,128]{1,0:T(8,128)(2,1)} %param.39) | copy-start | bytes 98308
  63.6 3.5 %collective-permute-start.8 = (bf16[384,128]{1,0:T(8,128)(2,1)S(1)}, bf16[384,128]{1,0:T(8,128)(2,1)S(1)}, u32[]{:S(2)}, u32[]{:S(2)}) collective-permute-start(bf16[384,128]{1,0:T(8,128)(2,1)S(1)} %get-tuple-element.319), channel_id=1, source_target_pairs={{0,1},{1,0},{2,3},{3,2},{4,5},{5,4},{6,7},{7,6},{8,9},{9,8},{10,11... | collective-permute-start | bytes 294920 | tf_op jit(solution)/shard_map/ppermute | solution.py:26
  64.1 4.1 %collective-permute-start.9 = (bf16[384,128]{1,0:T(8,128)(2,1)S(1)}, bf16[384,128]{1,0:T(8,128)(2,1)S(1)}, u32[]{:S(2)}, u32[]{:S(2)}) collective-permute-start(bf16[384,128]{1,0:T(8,128)(2,1)S(1)} %get-tuple-element.320), channel_id=1, source_target_pairs={{1,0},{0,1},{3,2},{2,3},{5,4},{4,5},{7,6},{6,7},{9,8},{8,9},{11,10... | collective-permute-start | bytes 294920 | tf_op jit(solution)/shard_map/ppermute | solution.py:28
  69.2 1.2 copy-start.12
  100.3 9.9 %copy-start.2 = (bf16[3,1024]{0,1:T(8,128)(2,1)S(1)}, bf16[3,1024]{0,1:T(8,128)(2,1)}, u32[]{:S(2)}) copy-start(bf16[3,1024]{0,1:T(8,128)(2,1)} %get-tuple-element.314) | copy-start | bytes 18436
  100.3 15.5 %copy-start.20 = (s32[16]{0:T(128)S(1)}, s32[16]{0:T(128)}, u32[]{:S(2)}) copy-start(s32[16]{0:T(128)} %param.43) | copy-start | bytes 196
  100.3 19.3 %copy-start.16 = (f32[16]{0:T(128)S(1)}, f32[16]{0:T(128)}, u32[]{:S(2)}) copy-start(f32[16]{0:T(128)} %param.42) | copy-start | bytes 196
  100.6 21.0 %collective-permute-start.12 = (bf16[3,1024]{0,1:T(8,128)(2,1)S(1)}, bf16[3,1024]{0,1:T(8,128)(2,1)S(1)}, u32[]{:S(2)}, u32[]{:S(2)}) collective-permute-start(bf16[3,1024]{0,1:T(8,128)(2,1)S(1)} %bitcast_convert_fusion), channel_id=1, source_target_pairs={{2,0},{4,2},{6,4},{8,6},{10,8},{12,10},{14,12},{16,14},{18,16},{20... | collective-permute-start | bytes 18440 | tf_op jit(solution)/shard_map/ppermute | solution.py:38
  107.1 14.5 %collective-permute-start.13 = (bf16[3,1024]{0,1:T(8,128)(2,1)S(1)}, bf16[3,1024]{0,1:T(8,128)(2,1)S(1)}, u32[]{:S(2)}, u32[]{:S(2)}) collective-permute-start(bf16[3,1024]{0,1:T(8,128)(2,1)S(1)} %bitcast_convert_fusion), channel_id=1, source_target_pairs={{0,2},{2,4},{4,6},{6,8},{8,10},{10,12},{12,14},{14,16},{16,18},{18... | collective-permute-start | bytes 18440 | tf_op jit(solution)/shard_map/ppermute | solution.py:38
  110.2 20.4 %collective-permute-start = (bf16[3,1024]{0,1:T(8,128)(2,1)S(1)}, bf16[3,1024]{0,1:T(8,128)(2,1)}, u32[]{:S(2)}, u32[]{:S(2)}) collective-permute-start(bf16[3,1024]{0,1:T(8,128)(2,1)S(1)} %copy-done.2), channel_id=1, source_target_pairs={{2,0},{4,2},{6,4},{8,6},{10,8},{12,10},{14,12},{16,14},{18,16},{20... | collective-permute-start | bytes 18440 | tf_op jit(solution)/shard_map/ppermute | solution.py:38
  112.1 18.5 %collective-permute-start.1 = (bf16[3,1024]{0,1:T(8,128)(2,1)S(1)}, bf16[3,1024]{0,1:T(8,128)(2,1)}, u32[]{:S(2)}, u32[]{:S(2)}) collective-permute-start(bf16[3,1024]{0,1:T(8,128)(2,1)S(1)} %copy-done.2), channel_id=1, source_target_pairs={{0,2},{2,4},{4,6},{6,8},{8,10},{10,12},{12,14},{14,16},{16,18},{18... | collective-permute-start | bytes 18440 | tf_op jit(solution)/shard_map/ppermute | solution.py:38
  121.6 0.7 copy-start.3
  122.3 0.7 copy-start.4
  125.0 8.3 %collective-permute-start.10 = (bf16[3,1024]{0,1:T(8,128)(2,1)}, bf16[3,1024]{0,1:T(8,128)(2,1)S(1)}, u32[]{:S(2)}, u32[]{:S(2)}) collective-permute-start(bf16[3,1024]{0,1:T(8,128)(2,1)} %get-tuple-element.310), channel_id=1, source_target_pairs={{2,0},{4,2},{6,4},{8,6},{10,8},{12,10},{14,12},{16,14},{18,16},{20... | collective-permute-start | bytes 18440 | tf_op jit(solution)/shard_map/ppermute | solution.py:38
  126.9 10.0 %collective-permute-start.11 = (bf16[3,1024]{0,1:T(8,128)(2,1)}, bf16[3,1024]{0,1:T(8,128)(2,1)S(1)}, u32[]{:S(2)}, u32[]{:S(2)}) collective-permute-start(bf16[3,1024]{0,1:T(8,128)(2,1)} %get-tuple-element.310), channel_id=1, source_target_pairs={{0,2},{2,4},{4,6},{6,8},{8,10},{10,12},{12,14},{14,16},{16,18},{18... | collective-permute-start | bytes 18440 | tf_op jit(solution)/shard_map/ppermute | solution.py:38
where the time goes:
time: 139 us; the launch traced here: 138 us
  matrix products  48.9 us (35%)
  starting transfers between devices  27.5 us (20%)
  local copies, waits for them, and re-layouts  24.3 us (17%)
  other arithmetic  18.5 us (13%)
  waiting for transfers between devices  10.9 us (8%)
  between operations  5.95 us (4%)
  loops' own time  1.87 us (1%)
    dot_general x16, matrix products, one_tile(): jnp.einsum('kbij,kjc->bic', basis_val, far_feat, preferred_element_type=j...  26.3 us
    ppermute x6, starting transfers between devices, from_behind(): return lax.ppermute(array, axis, pairs)  20.7 us
    dot_general x8, matrix products, one_tile(): jnp.einsum('kbij,b->kij', basis_val.astype(jnp.float32), push_distance_ta...  10.2 us
    dot_general x8, matrix products, one_tile(): jnp.einsum('ic,kjc->kij', asking, far_keys, preferred_element_type=jnp.fl...  9.2 us
    unnamed x48, local copies, waits for them, and re-layouts  6.67 us
    convert_element_type x8, other arithmetic, slot_basis(): (jnp.exp(-scaled * scaled) * live_flags[:, None, None, None]).astype(jnp....  4.91 us
    ppermute x4, starting transfers between devices, with_halo(): lax.ppermute(tail, axis, [(i, (i + 1) % count) for i in range(count)])  4.18 us
    ppermute x4, waiting for transfers between devices, with_halo(): lax.ppermute(tail, axis, [(i, (i + 1) % count) for i in range(count)])  3.8 us
  transfers between devices with their start and end apart: 14, of which 6 were waited for; matrix products, arithmetic and copies ran while one was open for 7% of the time, Pallas kernels for 0%

commit v1 on v0

v1 whole, which is shorter than its diff:
```python
import functools
import math

import jax
import jax.numpy as jnp
from jax import lax
from jax.experimental import pallas as pl
from jax.experimental.pallas import tpu as pltpu
from jax.sharding import PartitionSpec as P

NB = 8
TILE = 128
NEI = 4

slab_width = 1.5
time_step = 0.5
basis_width = 0.3
norm_eps = 1e-06

f32 = jnp.float32
bf16 = jnp.bfloat16

LOG2E = math.log2(math.e)
SCALE = math.sqrt(LOG2E) / basis_width
LIFT = 24.0
FAR = LOG2E * 400.0


def distinct(offsets, count):
    return list(dict.fromkeys(o % count for o in offsets))


def domain_sets(count):
    layer1 = distinct([0, -1, 1], count)
    layer0 = distinct(layer1 + [o + s for o in layer1 for s in (-1, 1)], count)
    held = distinct(layer0 + [o + s for o in layer0 for s in (-1, 1)], count)
    return layer1, layer0, held


def dot(a, b):
    return jnp.dot(a, b, preferred_element_type=f32)


def pack_kernel(loc, speed, push, kinds, ghosts, lists, counts, inertia, out):
    labels = kinds[...]
    mass = jnp.zeros(labels.shape, f32)
    for s in range(inertia.shape[0]):
        mass = jnp.where(labels == s, inertia[s], mass)
    inv_mass = 1.0 / mass
    atoms, tiles = labels.shape[1], counts.shape[1]
    out[...] = jnp.zeros(out.shape, f32)
    for d in range(3):
        out[d : d + 1, 0:atoms] = (
            loc[d] + time_step * speed[d] + 0.5 * time_step * time_step * push[d] * inv_mass
        )
        out[3 + d : 4 + d, 0:atoms] = speed[d] + 0.5 * time_step * push[d] * inv_mass
    out[6:7, 0:atoms] = labels.astype(f32)
    out[7:8, 0 : ghosts.shape[1]] = ghosts[...].astype(f32)
    out[0:NEI, atoms : atoms + tiles] = lists[0].astype(f32)
    out[NEI : NEI + 1, atoms : atoms + tiles] = counts[...].astype(f32)


def weights_kernel(kind, coef, gain, mix, target, u_parts, kind_t, w_cols, gain_cols, mix_t, target_t):
    kinds_f = jnp.transpose(kind[...].astype(f32), (1, 0))
    kind_t[...] = kinds_f.astype(bf16)
    coef_t = [jnp.transpose(coef[layer], (1, 0)) for layer in range(2)]
    columns = []
    for b in range(NB):
        columns.append(kinds_f * (coef_t[0][:, b : b + 1] * math.exp(-b * b)))
        w_cols[b] = jnp.broadcast_to(coef_t[1][:, b : b + 1] * math.exp(-b * b), (TILE, TILE))
    u = jnp.concatenate(columns, axis=1)
    high = u.astype(bf16)
    u_parts[...] = jnp.concatenate([high, (u - high.astype(f32)).astype(bf16), high], axis=1)
    gain_t = jnp.transpose(gain[...], (1, 0))
    for layer in range(2):
        gain_cols[layer] = jnp.broadcast_to(gain_t[:, layer : layer + 1], (TILE, TILE))
        mix_t[layer] = jnp.transpose(mix[layer].astype(f32), (1, 0)).astype(bf16)
    target_t[...] = jnp.transpose(target[...].astype(f32), (1, 0)).astype(bf16)


def lanes_of(parts):
    return jnp.concatenate(parts, axis=1)


def refresh(hidden, messages, gain, mix_t):
    activations = []
    for block in messages:
        block = block * math.exp(-LIFT)
        inverse = lax.rsqrt(jnp.mean(block * block, axis=0, keepdims=True) + norm_eps)
        v = block * inverse * gain
        activations.append((v / (1.0 + jnp.exp(-v))).astype(bf16))
    mixed = dot(mix_t, lanes_of(activations))
    return [
        (block + mixed[:, t * TILE : (t + 1) * TILE]).astype(bf16)
        for t, block in enumerate(hidden)
    ]


def main_kernel(plan, *refs):
    count, atoms, ghost = plan
    layer1, layer0, held = domain_sets(count)
    tiles = atoms // TILE
    ghost_tiles = ghost // TILE
    ext_tiles = tiles + 2 * ghost_tiles
    n = len(held)
    me, swaps, levels, inertia, taper = refs[:5]
    data = dict(zip(held, refs[5 : 5 + n]))
    u_parts, kind_t, w_cols, gain_cols, mix_t, target_t, source = refs[5 + n : 12 + n]
    pos_out, vel_out, force_out = refs[12 + n : 15 + n]
    (
        basis,
        far_t,
        near_rhs,
        onehot,
        split_pos,
        diffs,
        species_sums,
        ghost_pick,
        hidden1,
        hidden2,
        ext_hidden,
        message_rows,
        turned,
        asked,
        pulls,
        ints,
        sm,
        sem,
    ) = refs[15 + n :]
    kept = basis.shape[0]

    for at, o in enumerate(layer0):
        ints[at] = data[o][:, atoms : atoms + TILE].astype(jnp.int32)
    copies = [
        pltpu.make_async_copy(ints.at[at], sm.at[at], sem.at[at]) for at in range(len(layer0))
    ]
    for c in copies:
        c.start()

    row_id = lax.broadcasted_iota(jnp.int32, (8, TILE), 0)
    species_id = lax.broadcasted_iota(jnp.int32, (16, TILE), 0).astype(f32)
    ones_block = jnp.where(row_id < 3, 1.0, 0.0)

    def picked(o, first):
        src = data[o]
        idx = src[7:8, first : first + TILE].astype(jnp.int32)
        idx = jnp.broadcast_to(idx, (8, TILE))
        lane = idx & (TILE - 1)
        block = idx // TILE
        got = jnp.zeros((8, TILE), f32)
        for c in range(tiles):
            here = jnp.take_along_axis(
                src[:, c * TILE : (c + 1) * TILE], lane, axis=1, mode="promise_in_bounds"
            )
            got = jnp.where(block == c, here, got)
        return got

    wide_row = lax.broadcasted_iota(jnp.int32, (24, 3 * TILE), 0)
    wide_block = lax.broadcasted_iota(jnp.int32, (24, 3 * TILE), 1) // TILE
    selector = jnp.where((wide_row & 7) == wide_block, 1.0, 0.0)

    for at, o in enumerate(layer0):
        lower, upper = (o - 1) % count, (o + 1) % count
        for e in range(ext_tiles):
            if e < tiles:
                block, shift = data[o][:, e * TILE : (e + 1) * TILE], 0.0
            elif e < tiles + ghost_tiles:
                block, shift = picked(lower, ghost + (e - tiles) * TILE), -slab_width
            else:
                block, shift = picked(upper, (e - tiles - ghost_tiles) * TILE), slab_width
            moved = jnp.where(row_id == 0, block + shift, block) * SCALE
            moved = jnp.where(row_id < 3, moved, jnp.where(row_id == 3, 1.0, 0.0))
            onehot[at, e] = jnp.where(species_id == block[6:7, :], 1.0, 0.0).astype(bf16)
            hi = moved.astype(bf16).astype(f32)
            mid = (moved - hi).astype(bf16).astype(f32)
            low = moved - hi - mid
            stack = jnp.concatenate([hi, mid, low, ones_block], axis=0)
            far_t[at, e] = jnp.transpose(stack, (1, 0)).astype(bf16)
            if o == 0:
                split_pos[e] = stack.astype(bf16)
            if e < tiles:
                less = lanes_of(
                    [
                        jnp.where(
                            row_id == 0,
                            -hi[d : d + 1],
                            jnp.where(
                                row_id == 1,
                                -mid[d : d + 1],
                                jnp.where(row_id == 2, -low[d : d + 1], 0.0),
                            ),
                        )
                        for d in range(3)
                    ]
                )
                near_rhs[at, e] = jnp.concatenate([selector, less], axis=0).astype(bf16)

    for c in copies:
        c.wait()

    def offsets(at, t):
        far = jnp.concatenate([far_t[at, sm[at, k, t]] for k in range(NEI)], axis=0)
        return dot(far, near_rhs[at, t])

    def species_step(at, t):
        lhs = lanes_of([onehot[at, sm[at, k, t]] for k in range(NEI)])
        sums = dot(lhs, basis[jnp.minimum(at, kept - 1), t])
        sums = jnp.concatenate([sums[:, b * TILE : (b + 1) * TILE] for b in range(NB)], axis=0)
        high = sums.astype(bf16)
        low = (sums - high.astype(f32)).astype(bf16)
        return jnp.concatenate([high, high, low], axis=0)

    steps = len(layer0) * tiles
    diffs[...] = offsets(0, 0)

    def basis_step(s, _):
        before = jnp.maximum(s - 1, 0)
        after = jnp.minimum(s + 1, steps - 1)
        at, t = s // tiles, s % tiles
        species_sums[before // tiles, before % tiles] = species_step(before // tiles, before % tiles)
        upcoming = offsets(after // tiles, after % tiles)
        place = jnp.minimum(at, kept - 1)
        for k in range(NEI):
            top = jnp.where(k < sm[at, NEI, t], f32(LIFT * LOG2E), f32(-1e30))
            rows = slice(k * TILE, (k + 1) * TILE)
            square = None
            for d in range(3):
                off = diffs[rows, d * TILE : (d + 1) * TILE]
                square = off * off if square is None else square + off * off
            square = jnp.minimum(jnp.maximum(square, 1e-30), FAR)
            length = square * lax.rsqrt(square)
            step = (4.0 * math.sqrt(LOG2E)) * length
            ratio = jnp.exp2((2.0 * math.sqrt(LOG2E)) * length)
            power = top - square
            for b in range(0, NB, 2):
                value = jnp.exp2(power)
                basis[place, t, rows, b * TILE : (b + 1) * TILE] = value.astype(bf16)
                basis[place, t, rows, (b + 1) * TILE : (b + 2) * TILE] = (value * ratio).astype(bf16)
                power = power + step
        diffs[...] = upcoming
        return 0

    lax.fori_loop(0, steps, basis_step, 0)
    species_sums[len(layer0) - 1, tiles - 1] = species_step(len(layer0) - 1, tiles - 1)

    for at, o in enumerate(layer0):
        chosen = data[o][7:8, 0 : 2 * ghost]

        def pick_step(c, _):
            first = pl.multiple_of(c * TILE, TILE)
            rows = lax.broadcasted_iota(jnp.int32, (TILE, 2 * ghost), 0) + first
            ghost_pick[at, pl.ds(first, TILE), :] = jnp.where(
                rows.astype(f32) == chosen, 1.0, 0.0
            ).astype(bf16)
            return 0

        lax.fori_loop(0, tiles, pick_step, 0)

    for at in range(len(layer0)):
        messages = dot(u_parts[...], lanes_of([species_sums[at, t] for t in range(tiles)]))
        hidden0 = dot(kind_t[...], lanes_of([onehot[at, t] for t in range(tiles)]))
        split = lambda x: [x[:, t * TILE : (t + 1) * TILE] for t in range(tiles)]
        for t, block in enumerate(
            refresh(split(hidden0), split(messages), gain_cols[0], mix_t[0])
        ):
            hidden1[at, t] = block

    def extend(source_hidden, sets, o):
        for t in range(tiles):
            ext_hidden[t] = source_hidden[sets.index(o), t]
        for side, other in ((0, (o - 1) % count), (1, (o + 1) % count)):
            at = sets.index(other)
            rows = lanes_of([source_hidden[at, t] for t in range(tiles)])
            first = ghost if side == 0 else 0
            got = dot(
                rows, ghost_pick[layer0.index(other), :, first : first + ghost]
            ).astype(bf16)
            for g in range(ghost_tiles):
                ext_hidden[tiles + side * ghost_tiles + g] = got[:, g * TILE : (g + 1) * TILE]

    for keep, o in enumerate(layer1):
        at = layer0.index(o)
        extend(hidden1, layer0, o)

        def second_step(t, _):
            lhs = lanes_of([ext_hidden[sm[at, k, t]] for k in range(NEI)])
            sums = dot(lhs, basis[keep, t])
            messages = jnp.zeros((TILE, TILE), f32)
            for b in range(NB):
                messages = messages + sums[:, b * TILE : (b + 1) * TILE] * w_cols[b]
            message_rows[t] = messages
            return 0

        lax.fori_loop(0, tiles, second_step, 0, unroll=2)
        for t, block in enumerate(
            refresh(
                [hidden1[at, t].astype(f32) for t in range(tiles)],
                [message_rows[t] for t in range(tiles)],
                gain_cols[1],
                mix_t[1],
            )
        ):
            hidden2[keep, t] = block

    extend(hidden2, layer1, 0)
    for e in range(ext_tiles):
        turned[e] = jnp.transpose(ext_hidden[e].astype(f32), (1, 0)).astype(bf16)
    query = dot(target_t[...], lanes_of([ext_hidden[t] for t in range(tiles)])).astype(bf16)
    wanted = dot(source[...], query).astype(bf16)
    for t in range(tiles):
        asked[t] = wanted[:, t * TILE : (t + 1) * TILE]

    factor = math.exp(-LIFT) / math.sqrt(TILE * NEI * TILE) / SCALE

    def force_step(t, _):
        lhs = jnp.concatenate([turned[sm[0, k, t]] for k in range(NEI)], axis=0)
        scores = dot(lhs, asked[t])
        envelope = jnp.zeros((NEI * TILE, TILE), f32)
        for b in range(NB):
            envelope = envelope + basis[0, t, :, b * TILE : (b + 1) * TILE].astype(f32) * (
                taper[b] * (math.exp(-b * b) * factor)
            )
        weight = (scores * envelope).astype(bf16)
        places = lanes_of([split_pos[sm[0, k, t]] for k in range(NEI)])
        got = dot(places, weight)
        pulls[t] = got[0:8] + got[8:16] + got[16:24]
        return 0

    lax.fori_loop(0, tiles, force_step, 0, unroll=2)

    p = swaps[me[0]]
    quotient = jnp.sqrt(jnp.full((1, TILE), levels[me[0]], f32) / jnp.full((1, TILE), levels[p], f32))
    own = data[0]
    labels = own[6:7, 0:atoms]
    mass = jnp.zeros(labels.shape, f32)
    for s in range(inertia.shape[0]):
        mass = jnp.where(labels == s, inertia[s], mass)
    inv_mass = 1.0 / mass
    for t in range(tiles):
        lanes = slice(t * TILE, (t + 1) * TILE)
        got = pulls[t]
        force = got - own[:, lanes] * SCALE * got[3:4]
        velocity = own[3:6, lanes] + 0.5 * time_step * force[0:3] * inv_mass[:, lanes]
        velocity = velocity * quotient
        for d in range(3):
            pos_out[d, :, lanes] = own[d : d + 1, lanes]
            force_out[d, :, lanes] = force[d : d + 1]
            vel_out[d, :, lanes] = velocity[d : d + 1]


def local(
    count,
    replicas,
    particle_locations,
    particle_speeds,
    current_pushes,
    particle_kinds,
    halo_particle_labels,
    adjacent_block_labels,
    adjacent_place_totals,
    kind_vectors,
    kind_inertia,
    stepwise_distance_coefficients,
    signal_scaling_factors,
    feature_blend_coefficients,
    target_projection_array,
    source_projection_array,
    push_distance_taper,
    thermal_levels,
    granted_swaps,
):
    atoms = particle_locations.shape[2]
    ghost = halo_particle_labels.shape[1] // 2
    channels = kind_vectors.shape[1]
    tiles = atoms // TILE
    ext_tiles = tiles + 2 * (ghost // TILE)
    layer1, layer0, held = domain_sets(count)
    vmem = pl.BlockSpec(memory_space=pltpu.VMEM)
    smem = pl.BlockSpec(memory_space=pltpu.SMEM)
    shape = jax.ShapeDtypeStruct

    packed = pl.pallas_call(
        pack_kernel,
        out_shape=shape((8, atoms + TILE), f32),
        in_specs=[vmem] * 7 + [smem],
        out_specs=vmem,
    )(
        jnp.transpose(particle_locations, (1, 0, 2)),
        jnp.transpose(particle_speeds, (1, 0, 2)),
        jnp.transpose(current_pushes, (1, 0, 2)),
        particle_kinds,
        halo_particle_labels,
        jnp.transpose(adjacent_block_labels, (0, 2, 1)),
        adjacent_place_totals,
        kind_inertia,
    )

    me = lax.axis_index("rep")
    partner = granted_swaps[me]
    even = [(i, i ^ 1) for i in range(replicas)]
    odd = [(i, ((i + 1) ^ 1) - 1) for i in range(1, replicas - 1)]
    odd_all = [(a * count + d, b * count + d) for a, b in odd for d in range(count)] + [
        (r * count + d, r * count + (d + 1) % count) for r in (0, replicas - 1) for d in range(count)
    ]
    from_even = lax.ppermute(packed, "rep", even)
    from_odd = lax.ppermute(packed, ("rep", "dom"), odd_all)
    low = jnp.minimum(me, partner)
    chosen = jnp.where(partner == me, packed, jnp.where(low % 2 == 0, from_even, from_odd))
    data = [
        chosen
        if o == 0
        else lax.ppermute(chosen, "dom", [((d + o) % count, d) for d in range(count)])
        for o in held
    ]

    weights = pl.pallas_call(
        weights_kernel,
        out_shape=[
            shape((channels, 3 * NB * kind_vectors.shape[0]), bf16),
            shape((channels, kind_vectors.shape[0]), bf16),
            shape((NB, channels, TILE), f32),
            shape((2, channels, TILE), f32),
            shape((2, channels, channels), bf16),
            shape((channels, channels), bf16),
        ],
        in_specs=[vmem] * 5,
        out_specs=[vmem] * 6,
        cost_estimate=pl.CostEstimate(flops=10**6, bytes_accessed=10**6, transcendentals=0),
    )(
        kind_vectors,
        stepwise_distance_coefficients,
        signal_scaling_factors,
        feature_blend_coefficients,
        target_projection_array,
    )

    outs = pl.pallas_call(
        functools.partial(main_kernel, (count, atoms, ghost)),
        out_shape=[shape((3, 1, atoms), f32)] * 3,
        in_specs=[smem] * 5 + [vmem] * (len(held) + 7),
        out_specs=[vmem] * 3,
        scratch_shapes=[
            pltpu.VMEM((len(layer1) + (len(layer0) > len(layer1)), tiles, NEI * TILE, NB * TILE), bf16),
            pltpu.VMEM((len(layer0), ext_tiles, TILE, 32), bf16),
            pltpu.VMEM((len(layer0), tiles, 32, 3 * TILE), bf16),
            pltpu.VMEM((len(layer0), ext_tiles, 16, TILE), bf16),
            pltpu.VMEM((ext_tiles, 32, TILE), bf16),
            pltpu.VMEM((NEI * TILE, 3 * TILE), f32),
            pltpu.VMEM((len(layer0), tiles, 3 * NB * 16, TILE), bf16),
            pltpu.VMEM((len(layer0), atoms, 2 * ghost), bf16),
            pltpu.VMEM((len(layer0), tiles, TILE, TILE), bf16),
            pltpu.VMEM((len(layer1), tiles, TILE, TILE), bf16),
            pltpu.VMEM((ext_tiles, TILE, TILE), bf16),
            pltpu.VMEM((tiles, TILE, TILE), f32),
            pltpu.VMEM((ext_tiles, TILE, TILE), bf16),
            pltpu.VMEM((tiles, TILE, TILE), bf16),
            pltpu.VMEM((tiles, 8, TILE), f32),
            pltpu.VMEM((len(layer0), 8, TILE), jnp.int32),
            pltpu.SMEM((len(layer0), 8, TILE), jnp.int32),
            pltpu.SemaphoreType.DMA((len(layer0),)),
        ],
        compiler_params=pltpu.CompilerParams(vmem_limit_bytes=58 * 2**20),
    )(
        me.reshape(1),
        granted_swaps,
        thermal_levels,
        kind_inertia,
        push_distance_taper,
        *data,
        *weights,
        source_projection_array,
    )
    return tuple(jnp.transpose(x, (1, 0, 2)) for x in outs)


def solution(mesh):
    in_specs = (
        P("rep", None, "dom"),
        P("rep", None, "dom"),
        P("rep", None, "dom"),
        P("rep", "dom"),
        P("rep", "dom"),
        P("rep", "dom", None),
        P("rep", "dom"),
    ) + (P(),) * 10
    out_specs = (P("rep", None, "dom"), P("rep", None, "dom"), P("rep", None, "dom"))
    step = functools.partial(local, mesh.shape["dom"], mesh.shape["rep"])
    return jax.shard_map(step, mesh=mesh, in_specs=in_specs, out_specs=out_specs, check_vma=False)
```

time: 139 us -> 34.7 us (0.25)
  the two profiles are of different devices: /device:TPU:1 before, /device:TPU:0 now
where the time goes in v1:
time: 34.7 us; the launch traced here: 34.4 us
  Pallas kernels  25.9 us (75%)
  starting transfers between devices  5.07 us (15%)
  between operations  1.99 us (6%)
  local copies, waits for them, and re-layouts  1.19 us (3%)
    pallas_call x1, Pallas kernels, local(): pl.pallas_call(functools.partial(main_kernel, (count, atoms, ghost)), out...  22 us
    ppermute x1, starting transfers between devices, local(): from_odd = lax.ppermute(packed, ('rep', 'dom'), odd_all)  2.97 us
    pallas_call x1, Pallas kernels, local(): pl.pallas_call(weights_kernel, out_shape=[shape((channels, 3 * NB * kind_...  2.46 us
    ppermute x1, starting transfers between devices, local(): lax.ppermute(chosen, 'dom', [((d + o) % count, d) for d in range(count)])  2.02 us
    pallas_call x1, Pallas kernels, local(): pl.pallas_call(pack_kernel, out_shape=shape((8, atoms + TILE), f32), in_s...  1.43 us
  transfers between devices with their start and end apart: 3, of which 1 were waited for; matrix products, arithmetic and copies ran while one was open for 2% of the time, Pallas kernels for 7%

profile of v1, /device:TPU:0, one launch (start us, length us, event | category | flops | bytes accessed | tf_op | source)
XLA Modules:
  0.0 34.4 jit_solution(17032470964590296455)
XLA Ops:
  0.6 0.0 copy-start.3
  0.6 1.4 %shard_map.184 = f32[8,1152]{1,0:T(8,128)} custom-call(f32[3,1,1024]{2,1,0:T(1,128)} %bitcast.9, f32[3,1,1024]{2,1,0:T(1,128)} %bitcast.10, f32[3,1,1024]{2,1,0:T(1,128)} %bitcast.11, s32[1,1024]{1,0:T(1,128)} %kinds.1, s32[1,768]{1,0:T(1,128)} %ghosts.1, s32[1,4,8]{2,1,0:T(4,128)} %bitcast.12, s32[1,8]{1,0:T(1,128)} %counts.1, f32[16]{0:T(128)} %refs_3_.1), custom_call_target="tpu_custom_call" | custom-call | tf_op jit(solution)/shard_map/pallas_call | solution.py:382
  2.1 0.0 copy-start.1
  2.1 3.0 %collective-permute-start.1 = (f32[8,1152]{1,0:T(8,128)}, f32[8,1152]{1,0:T(8,128)S(1)}, u32[]{:S(2)}, u32[]{:S(2)}) collective-permute-start(f32[8,1152]{1,0:T(8,128)} %shard_map.184), channel_id=1, source_target_pairs={{2,4},{3,5},{4,2},{5,3},{6,8},{7,9},{8,6},{9,7},{10,12},{11,13},{1... | collective-permute-start | bytes 110600 | tf_op jit(solution)/shard_map/ppermute | solution.py:406
  5.0 0.1 collective-permute-start
  5.1 0.0 copy-done.3
  5.1 0.6 %dynamic_slice.3 = s32[1]{0:T(128)} dynamic-slice(s32[16]{0:T(128)S(1)} %copy-done.3, s32[]{:T(128)S(6)} %select_n.24), dynamic_slice_sizes={1} | dynamic-slice | bytes 12 | tf_op jit(solution)/shard_map/dynamic_slice | solution.py:399
  7.0 0.2 collective-permute-done.1
  7.3 0.0 collective-permute-done
  7.3 0.0 copy-done.1
  7.3 0.0 copy-start
  7.3 2.0 %collective-permute-start.2 = (f32[8,1152]{1,0:T(8,128)S(1)}, f32[8,1152]{1,0:T(8,128)S(1)}, u32[]{:S(2)}, u32[]{:S(2)}) collective-permute-start(f32[8,1152]{1,0:T(8,128)S(1)} %select_select_fusion.refs_5_), channel_id=1, source_target_pairs={{1,0},{0,1},{3,2},{2,3},{5,4},{4,5},{7,6},{6,7},{9,8},{8,9},{11,10... | collective-permute-start | bytes 110600 | tf_op jit(solution)/shard_map/ppermute | solution.py:412
  9.3 2.5 %shard_map.185 = (bf16[128,384]{1,0:T(8,128)(2,1)}, bf16[128,16]{1,0:T(8,128)(2,1)}, f32[8,128,128]{2,1,0:T(8,128)}, f32[2,128,128]{2,1,0:T(8,128)}, bf16[2,128,...) custom-call(bf16[16,128]{1,0:T(8,128)(2,1)} %kind.1, f32[2,8,128]{2,1,0:T(8,128)} %coef.1, f32[2,128]{1,0:T(2,128)} %gain.1, ...), custom_call_target="tpu_custom_call" | custom-call | flops 1000000 | bytes 1000000 | tf_op jit(solution)/shard_map/pallas_call | solution.py:416
  11.8 0.0 copy-done
  11.8 0.0 collective-permute-done.2.refs_6_
  11.8 0.0 copy-start.2
  11.8 0.6 %copy-done.2 = f32[8,1152]{1,0:T(8,128)} copy-done((f32[8,1152]{1,0:T(8,128)}, f32[8,1152]{1,0:T(8,128)S(1)}, u32[]{:S(2)}) %copy-start.2) | copy-done | bytes 36888
  12.4 22.0 %shard_map.186 = (f32[3,1,1024]{2,1,0:T(1,128)}, f32[3,1,1024]{2,1,0:T(1,128)}, f32[3,1,1024]{2,1,0:T(1,128)}) custom-call(s32[1]{0:T(128)} %bitcast.refs_0_, s32[16]{0:T(128)} %refs_1_.1, f32[16]{0:T(128)} %refs_2_.1, f32[16]{0:T(128)} %refs_3_.1, f32[8]{0:T(128)} %refs_4_.1, f32[8,1152]{1,0:T(8,128)} %copy-done, f32[8,1152]{1,0:T(8,128)} %copy-done.2, ...), custom_call_target="tpu_custom_call" | custom-call | tf_op jit(solution)/shard_map/pallas_call | solution.py:437
  (1 shorter events, 0.0 us)
Async XLA Ops:
  0.6 4.5 %copy-start.3 = (s32[16]{0:T(128)S(1)}, s32[16]{0:T(128)}, u32[]{:S(2)}) copy-start(s32[16]{0:T(128)} %refs_1_.1) | copy-start | bytes 196
  2.1 5.2 %copy-start.1 = (f32[8,1152]{1,0:T(8,128)S(1)}, f32[8,1152]{1,0:T(8,128)}, u32[]{:S(2)}) copy-start(f32[8,1152]{1,0:T(8,128)} %shard_map.184) | copy-start | bytes 110596
  2.1 5.2 %collective-permute-start.1 = (f32[8,1152]{1,0:T(8,128)}, f32[8,1152]{1,0:T(8,128)S(1)}, u32[]{:S(2)}, u32[]{:S(2)}) collective-permute-start(f32[8,1152]{1,0:T(8,128)} %shard_map.184), channel_id=1, source_target_pairs={{2,4},{3,5},{4,2},{5,3},{6,8},{7,9},{8,6},{9,7},{10,12},{11,13},{1... | collective-permute-start | bytes 110600 | tf_op jit(solution)/shard_map/ppermute | solution.py:406
  5.0 2.2 %collective-permute-start = (f32[8,1152]{1,0:T(8,128)}, f32[8,1152]{1,0:T(8,128)S(1)}, u32[]{:S(2)}, u32[]{:S(2)}) collective-permute-start(f32[8,1152]{1,0:T(8,128)} %shard_map.184), channel_id=1, source_target_pairs={{0,2},{2,0},{4,6},{6,4},{8,10},{10,8},{12,14},{14,12},{16,18},{18,... | collective-permute-start | bytes 110600 | tf_op jit(solution)/shard_map/ppermute | solution.py:405
  7.3 4.5 %copy-start = (f32[8,1152]{1,0:T(8,128)}, f32[8,1152]{1,0:T(8,128)S(1)}, u32[]{:S(2)}) copy-start(f32[8,1152]{1,0:T(8,128)S(1)} %select_select_fusion.refs_5_) | copy-start | bytes 110596
  7.3 4.5 %collective-permute-start.2 = (f32[8,1152]{1,0:T(8,128)S(1)}, f32[8,1152]{1,0:T(8,128)S(1)}, u32[]{:S(2)}, u32[]{:S(2)}) collective-permute-start(f32[8,1152]{1,0:T(8,128)S(1)} %select_select_fusion.refs_5_), channel_id=1, source_target_pairs={{1,0},{0,1},{3,2},{2,3},{5,4},{4,5},{7,6},{6,7},{9,8},{8,9},{11,10... | collective-permute-start | bytes 110600 | tf_op jit(solution)/shard_map/ppermute | solution.py:412
  11.8 0.6 %copy-start.2 = (f32[8,1152]{1,0:T(8,128)}, f32[8,1152]{1,0:T(8,128)S(1)}, u32[]{:S(2)}) copy-start(f32[8,1152]{1,0:T(8,128)S(1)} %collective-permute-done.2.refs_6_) | copy-start | bytes 110596

commit v2 on v1

v2 whole, which is shorter than its diff:
```python
import functools
import math

import jax
import jax.numpy as jnp
from jax import lax
from jax.experimental import pallas as pl
from jax.experimental.pallas import tpu as pltpu
from jax.sharding import PartitionSpec as P

NB = 8
TILE = 128
NEI = 4

slab_width = 1.5
time_step = 0.5
basis_width = 0.3
norm_eps = 1e-06

f32 = jnp.float32
bf16 = jnp.bfloat16

LOG2E = math.log2(math.e)
SCALE = math.sqrt(LOG2E) / basis_width
TOP = 34.0
UNLIFT = 2.0**-TOP
STEEP = 4.0 * LOG2E
FAR = (40.0 * LOG2E) ** 2
BODY = 4


def distinct(offsets, count):
    return list(dict.fromkeys(o % count for o in offsets))


def domain_sets(count):
    layer1 = distinct([0, -1, 1], count)
    layer0 = distinct(layer1 + [o + s for o in layer1 for s in (-1, 1)], count)
    held = distinct(layer0 + [o + s for o in layer0 for s in (-1, 1)], count)
    return layer1, layer0, held


def dot(a, b):
    return jnp.dot(a, b, preferred_element_type=f32)


def pack_kernel(loc, speed, push, kinds, ghosts, lists, counts, inertia, out):
    labels = kinds[...]
    mass = jnp.zeros(labels.shape, f32)
    for s in range(inertia.shape[0]):
        mass = jnp.where(labels == s, inertia[s], mass)
    inv_mass = 1.0 / mass
    atoms, tiles = labels.shape[1], counts.shape[1]
    out[...] = jnp.zeros(out.shape, f32)
    for d in range(3):
        out[d : d + 1, 0:atoms] = (
            loc[d] + time_step * speed[d] + 0.5 * time_step * time_step * push[d] * inv_mass
        )
        out[3 + d : 4 + d, 0:atoms] = speed[d] + 0.5 * time_step * push[d] * inv_mass
    out[6:7, 0:atoms] = labels.astype(f32)
    out[7:8, 0 : ghosts.shape[1]] = ghosts[...].astype(f32)
    out[0:NEI, atoms : atoms + tiles] = lists[0].astype(f32)
    out[NEI : NEI + 1, atoms : atoms + tiles] = counts[...].astype(f32)


def weights_kernel(kind, coef, gain, mix, target, source, wide, columns):
    species = kind.shape[0]
    kinds_f = jnp.transpose(kind[...].astype(f32), (1, 0))
    coef_t = [jnp.transpose(coef[layer], (1, 0)) for layer in range(2)]
    u = []
    for b in range(NB):
        u.append(kinds_f * (coef_t[0][:, b : b + 1] * math.exp(-b * b)))
        columns[b] = jnp.broadcast_to(coef_t[1][:, b : b + 1] * math.exp(-b * b), columns.shape[1:])
    u = jnp.concatenate(u, axis=1)
    high = u.astype(bf16)
    wide[:, 0:TILE] = high
    wide[:, TILE : 2 * TILE] = (u - high.astype(f32)).astype(bf16)
    wide[:, 2 * TILE : 3 * TILE] = high
    gain_t = jnp.transpose(gain[...], (1, 0))
    for layer in range(2):
        columns[NB + layer] = jnp.broadcast_to(gain_t[:, layer : layer + 1], columns.shape[1:])
        wide[:, (3 + 2 * layer) * TILE : (4 + 2 * layer) * TILE] = jnp.transpose(
            mix[layer].astype(f32), (1, 0)
        ).astype(bf16)
    wide[:, 4 * TILE : 5 * TILE] = jnp.concatenate(
        [kinds_f, jnp.zeros((kinds_f.shape[0], TILE - species), f32)], axis=1
    ).astype(bf16)
    both = lax.dot_general(
        source[...], target[...], (((1,), (1,)), ((), ())), preferred_element_type=f32
    )
    high = both.astype(bf16)
    wide[:, 6 * TILE : 7 * TILE] = high
    wide[:, 7 * TILE : 8 * TILE] = (both - high.astype(f32)).astype(bf16)


def lanes_of(parts):
    return jnp.concatenate(parts, axis=1)


def activate(messages, gain):
    messages = messages * UNLIFT
    inverse = lax.rsqrt(jnp.mean(messages * messages, axis=0, keepdims=True) + norm_eps)
    v = messages * inverse * gain
    return (v / (1.0 + jnp.exp(-v))).astype(bf16)


def main_kernel(plan, *refs):
    count, atoms, ghost = plan
    layer1, layer0, held = domain_sets(count)
    tiles = atoms // TILE
    ghost_tiles = ghost // TILE
    ext_tiles = tiles + 2 * ghost_tiles
    n = len(held)
    swaps, levels, taper, inertia = refs[:4]
    refs = refs[4:]
    outside = refs[: n + 2]
    pos_out, vel_out, force_out = refs[n + 2 : n + 5]
    held_data, wide, columns = refs[n + 5 : n + 8]
    arrivals = refs[n + 8]
    data = {o: held_data.at[at] for at, o in enumerate(held)}
    inward = [
        pltpu.make_async_copy(src, dst, arrivals.at[at])
        for at, (src, dst) in enumerate(
            zip(outside, [held_data.at[at] for at in range(n)] + [wide, columns])
        )
    ]
    for c in inward:
        c.start()
    for c in inward[:n]:
        c.wait()
    (
        far_t,
        near_rhs,
        onehot,
        split_pos,
        species_sums,
        ghost_pick,
        hidden1,
        hidden2,
        ext_hidden,
        message_rows,
        envelopes,
        turned,
        asked,
        pulls,
        ints,
        sm,
        sem,
    ) = refs[n + 9 : -2 * BODY]
    basis, squares = refs[-2 * BODY : -BODY], refs[-BODY:]
    u_parts = wide.at[:, 0 : 3 * TILE]
    mix_kind = wide.at[:, 3 * TILE : 4 * TILE + 16]
    mix_second = wide.at[:, 5 * TILE : 6 * TILE]
    both_parts = wide.at[:, 6 * TILE : 8 * TILE]
    kept = basis[0].shape[0]

    for at, o in enumerate(layer0):
        ints[at] = data[o][:, atoms : atoms + TILE].astype(jnp.int32)
    copies = [
        pltpu.make_async_copy(ints.at[at], sm.at[at], sem.at[at]) for at in range(len(layer0))
    ]
    for c in copies:
        c.start()

    row_id = lax.broadcasted_iota(jnp.int32, (8, TILE), 0)
    species_id = lax.broadcasted_iota(jnp.int32, (16, TILE), 0).astype(f32)
    def picked(o, first):
        src = data[o]
        idx = src[7:8, first : first + TILE].astype(jnp.int32)
        idx = jnp.broadcast_to(idx, (8, TILE))
        lane = idx & (TILE - 1)
        block = idx // TILE
        got = jnp.zeros((8, TILE), f32)
        for c in range(tiles):
            here = jnp.take_along_axis(
                src[:, c * TILE : (c + 1) * TILE], lane, axis=1, mode="promise_in_bounds"
            )
            got = jnp.where(block == c, here, got)
        return got

    def thirds(x):
        hi = x.astype(bf16).astype(f32)
        mid = (x - hi).astype(bf16).astype(f32)
        return hi, mid, x - hi - mid

    def rows_of(*rows):
        block = jnp.zeros((8, TILE), f32)
        for r, row in enumerate(rows):
            block = jnp.where(row_id == r, row, block)
        return block

    nowhere = rows_of(1e30, 0.0, 0.0, 1.0, 1.0, 1.0, 1.0)
    blank = jnp.zeros((8, TILE), f32)
    for at in range(len(layer0)):
        far_t[at, ext_tiles] = jnp.transpose(
            jnp.concatenate([blank] * 6 + [nowhere, rows_of(1e30)], axis=0), (1, 0)
        ).astype(bf16)

    for at, o in enumerate(layer0):
        lower, upper = (o - 1) % count, (o + 1) % count
        for e in range(ext_tiles):
            if e < tiles:
                block, shift = data[o][:, e * TILE : (e + 1) * TILE], 0.0
            elif e < tiles + ghost_tiles:
                block, shift = picked(lower, ghost + (e - tiles) * TILE), -slab_width
            else:
                block, shift = picked(upper, (e - tiles - ghost_tiles) * TILE), slab_width
            moved = jnp.where(row_id == 0, block + shift, block) - 0.5 * slab_width
            moved = jnp.where(row_id < 3, moved * SCALE, 0.0)
            onehot[at, e] = jnp.where(species_id == block[6:7, :], 1.0, 0.0).astype(bf16)
            hi, mid, low = thirds(moved)
            size = jnp.sum(moved * moved, axis=0, keepdims=True)
            sizes, steep_sizes = thirds(size), thirds(size * STEEP)
            far_t[at, e] = jnp.transpose(
                jnp.concatenate(
                    [hi, hi, hi, mid, mid, low]
                    + [rows_of(*sizes, 1.0, 1.0, 1.0, 1.0), rows_of(*steep_sizes)],
                    axis=0,
                ),
                (1, 0),
            ).astype(bf16)
            if o == 0:
                split_pos[e] = jnp.concatenate([hi, mid, low, rows_of(1.0)], axis=0).astype(bf16)
            if e < tiles:
                first, second, third = thirds(moved * -2.0)
                power = [-first, -second, -third, -first, -second, -first]
                power += [rows_of(-1.0, -1.0, -1.0, *[-x for x in sizes], TOP), blank]
                first, second, third = thirds(moved * (-2.0 * STEEP))
                steep = [first, second, third, first, second, first]
                steep += [rows_of(0.0, 0.0, 0.0, *steep_sizes), rows_of(1.0, 1.0, 1.0)]
                near_rhs[at, e] = lanes_of(
                    [jnp.concatenate(power, axis=0), jnp.concatenate(steep, axis=0)]
                ).astype(bf16)

    for c in copies:
        c.wait()

    def offsets(at, t):
        far = [
            far_t[at, jnp.where(k < sm[at, NEI, t], sm[at, k, t], ext_tiles)] for k in range(NEI)
        ]
        return dot(jnp.concatenate(far, axis=0), near_rhs[at, t])

    bodies = tiles // BODY
    steps = len(layer0) * bodies

    def basis_step(at, body, u, own):
        t = BODY * body + u
        place = jnp.minimum(at, kept - 1)
        sums = [None] * (NB // 2)
        for half in range(NEI // 2):
            rows = slice(2 * half * TILE, 2 * (half + 1) * TILE)
            lhs = lanes_of([onehot[at, sm[at, 2 * half + k, t]] for k in range(2)])
            power = squares[u][rows, 0:TILE]
            square = jnp.minimum(jnp.maximum(squares[u][rows, TILE : 2 * TILE], 1e-30), FAR)
            slope = square * lax.rsqrt(square)
            ratio = jnp.exp2(slope)
            step = slope + slope
            envelope = None
            for p in range(NB // 2):
                even = jnp.exp2(power)
                odd = even * ratio
                pair = lanes_of([even.astype(bf16), odd.astype(bf16)])
                basis[u][place, body, rows, 2 * p * TILE : 2 * (p + 1) * TILE] = pair
                part = dot(lhs, pair)
                sums[p] = part if half == 0 else sums[p] + part
                if own:
                    part = even * envelope_factor(2 * p) + odd * envelope_factor(2 * p + 1)
                    envelope = part if p == 0 else envelope + part
                if p < NB // 2 - 1:
                    power = power + step
            if own:
                envelopes[t, rows] = envelope
        sums = [x[:, k * TILE : (k + 1) * TILE] for x in sums for k in range(2)]
        sums = jnp.concatenate(sums, axis=0)
        high = sums.astype(bf16)
        low = (sums - high.astype(f32)).astype(bf16)
        species_sums[at, t] = jnp.concatenate([high, high, low], axis=0)

    def envelope_factor(b):
        return taper[b] * (math.exp(-b * b) * UNLIFT / (math.sqrt(TILE * NEI * TILE) * SCALE))

    def first_layer(at):
        messages = dot(u_parts[...], lanes_of([species_sums[at, t] for t in range(tiles)]))
        activations = [
            activate(messages[:, t * TILE : (t + 1) * TILE], columns[NB]) for t in range(tiles)
        ]
        kinds = lanes_of([onehot[at, t] for t in range(tiles)])
        hidden = dot(mix_kind[...], jnp.concatenate([lanes_of(activations), kinds], axis=0))
        for t in range(tiles):
            hidden1[at, t] = hidden[:, t * TILE : (t + 1) * TILE].astype(bf16)

    squares[0][...] = offsets(0, 0)

    def body_step(own, m, _):
        at, body = m // bodies, m % bodies
        after = jnp.minimum(m + 1, steps - 1)
        for u in range(BODY):
            if u == BODY - 1:
                upcoming = offsets(after // bodies, BODY * (after % bodies))
            else:
                upcoming = offsets(at, BODY * body + u + 1)
            basis_step(at, body, u, own)
            squares[(u + 1) % BODY][...] = upcoming
        return 0

    for c in inward[n:]:
        c.wait()
    lax.fori_loop(0, bodies, functools.partial(body_step, True), 0)
    lax.fori_loop(bodies, steps, functools.partial(body_step, False), 0)

    for at, o in enumerate(layer0):
        chosen = data[o][7:8, 0 : 2 * ghost]

        def pick_step(c, _):
            first = pl.multiple_of(c * TILE, TILE)
            rows = lax.broadcasted_iota(jnp.int32, (TILE, 2 * ghost), 0) + first
            ghost_pick[at, pl.ds(first, TILE), :] = jnp.where(
                rows.astype(f32) == chosen, 1.0, 0.0
            ).astype(bf16)
            return 0

        lax.fori_loop(0, tiles, pick_step, 0)

    for at in range(len(layer0)):
        first_layer(at)

    def extend(target, source_hidden, sets, o):
        for side, other in ((0, (o - 1) % count), (1, (o + 1) % count)):
            at = sets.index(other)
            rows = lanes_of([source_hidden[at, t] for t in range(tiles)])
            first = ghost if side == 0 else 0
            got = dot(
                rows, ghost_pick[layer0.index(other), :, first : first + ghost]
            ).astype(bf16)
            for g in range(ghost_tiles):
                target[tiles + side * ghost_tiles + g] = got[:, g * TILE : (g + 1) * TILE]

    def second_step(keep, t):
        at = layer0.index(layer1[keep])
        lhs = lanes_of([ext_hidden[keep, sm[at, k, t]] for k in range(NEI)])
        sums = dot(lhs, basis[t % BODY][keep, t // BODY])
        messages = None
        for b in range(NB):
            part = sums[:, b * TILE : (b + 1) * TILE] * columns[b]
            messages = part if messages is None else messages + part
        message_rows[keep, t] = messages

    def finish_second(keep, activations):
        at = layer0.index(layer1[keep])
        added = dot(mix_second[...], lanes_of(activations))
        for t in range(tiles):
            block = hidden1[at, t].astype(f32) + added[:, t * TILE : (t + 1) * TILE]
            hidden2[keep, t] = block.astype(bf16)

    def turn(block):
        return jnp.transpose(block.astype(f32), (1, 0)).astype(bf16)

    def import_final():
        extend(last, hidden2, layer1, 0)
        for e in range(tiles, ext_tiles):
            turned[e] = turn(last[e])

    last = ext_hidden.at[len(layer1)]
    order = list(range(1, len(layer1))) + [0]
    for keep in order:
        o = layer1[keep]
        for t in range(tiles):
            ext_hidden[keep, t] = hidden1[layer0.index(o), t]
        extend(ext_hidden.at[keep], hidden1, layer0, o)
    pending = []
    for keep in order:
        activations = []
        for t in range(tiles):
            second_step(keep, t)
            if t:
                activations.append(activate(message_rows[keep, t - 1], columns[NB + 1]))
            if pending and t % 2:
                pending.pop(0)()
        activations.append(activate(message_rows[keep, tiles - 1], columns[NB + 1]))
        for job in pending:
            job()
        pending = [functools.partial(finish_second, keep, activations)]
        if keep and keep == order[-2]:
            pending.append(import_final)
    for job in pending:
        job()
    if len(order) == 1:
        import_final()
    own_hidden = [hidden2[0, t] for t in range(tiles)]
    for t in range(tiles):
        turned[t] = turn(own_hidden[t])
    own_hidden = lanes_of(own_hidden)
    wanted = dot(both_parts[...], jnp.concatenate([own_hidden, own_hidden], axis=0)).astype(bf16)
    for t in range(tiles):
        asked[t] = wanted[:, t * TILE : (t + 1) * TILE]

    for t in range(tiles):
        lhs = jnp.concatenate([turned[sm[0, k, t]] for k in range(NEI)], axis=0)
        weight = (dot(lhs, asked[t]) * envelopes[t]).astype(bf16)
        places = lanes_of([split_pos[sm[0, k, t]] for k in range(NEI)])
        got = dot(places, weight)
        pulls[t] = jnp.concatenate([got[0:8] + got[8:16] + got[16:24], got[24:32]], axis=0)

    me = lax.axis_index("rep")
    quotient = jnp.sqrt(
        jnp.full((1, TILE), levels[me], f32) / jnp.full((1, TILE), levels[swaps[me]], f32)
    )
    own = data[0]
    labels = own[6:7, 0:atoms]
    mass = jnp.zeros(labels.shape, f32)
    for s in range(inertia.shape[0]):
        mass = jnp.where(labels == s, inertia[s], mass)
    inv_mass = 1.0 / mass
    for t in range(tiles):
        lanes = slice(t * TILE, (t + 1) * TILE)
        got = pulls[t]
        force = got[0:8] - (own[:, lanes] - 0.5 * slab_width) * SCALE * got[8:9]
        velocity = own[3:6, lanes] + 0.5 * time_step * force[0:3] * inv_mass[:, lanes]
        velocity = velocity * quotient
        for d in range(3):
            pos_out[d, :, lanes] = own[d : d + 1, lanes]
            force_out[d, :, lanes] = force[d : d + 1]
            vel_out[d, :, lanes] = velocity[d : d + 1]


def local(
    count,
    replicas,
    particle_locations,
    particle_speeds,
    current_pushes,
    particle_kinds,
    halo_particle_labels,
    adjacent_block_labels,
    adjacent_place_totals,
    kind_vectors,
    kind_inertia,
    stepwise_distance_coefficients,
    signal_scaling_factors,
    feature_blend_coefficients,
    target_projection_array,
    source_projection_array,
    push_distance_taper,
    thermal_levels,
    granted_swaps,
):
    atoms = particle_locations.shape[2]
    ghost = halo_particle_labels.shape[1] // 2
    channels = kind_vectors.shape[1]
    tiles = atoms // TILE
    ext_tiles = tiles + 2 * (ghost // TILE)
    layer1, layer0, held = domain_sets(count)
    vmem = pl.BlockSpec(memory_space=pltpu.VMEM)
    smem = pl.BlockSpec(memory_space=pltpu.SMEM)
    shape = jax.ShapeDtypeStruct

    packed = pl.pallas_call(
        pack_kernel,
        out_shape=shape((8, atoms + TILE), f32),
        in_specs=[vmem] * 7 + [smem],
        out_specs=vmem,
    )(
        jnp.transpose(particle_locations, (1, 0, 2)),
        jnp.transpose(particle_speeds, (1, 0, 2)),
        jnp.transpose(current_pushes, (1, 0, 2)),
        particle_kinds,
        halo_particle_labels,
        jnp.transpose(adjacent_block_labels, (0, 2, 1)),
        adjacent_place_totals,
        kind_inertia,
    )

    even = [(i, i ^ 1) for i in range(replicas)]
    odd = [(i, ((i + 1) ^ 1) - 1) for i in range(1, replicas - 1)]
    odd_all = [(a * count + d, b * count + d) for a, b in odd for d in range(count)] + [
        (r * count + d, r * count + (d + 1) % count) for r in (0, replicas - 1) for d in range(count)
    ]
    from_even = lax.ppermute(packed, "rep", even)
    from_odd = lax.ppermute(packed, ("rep", "dom"), odd_all)
    me = lax.axis_index("rep")
    partner = granted_swaps[me]
    low = jnp.minimum(me, partner)
    chosen = jnp.where(partner == me, packed, jnp.where(low % 2 == 0, from_even, from_odd))
    data = [
        chosen
        if o == 0
        else lax.ppermute(chosen, "dom", [((d + o) % count, d) for d in range(count)])
        for o in held
    ]

    weights = pl.pallas_call(
        weights_kernel,
        out_shape=[shape((channels, 8 * TILE), bf16), shape((NB + 2, channels, TILE), f32)],
        in_specs=[vmem] * 6,
        out_specs=[vmem] * 2,
        cost_estimate=pl.CostEstimate(flops=10**6, bytes_accessed=10**6, transcendentals=0),
    )(
        kind_vectors,
        stepwise_distance_coefficients,
        signal_scaling_factors,
        feature_blend_coefficients,
        target_projection_array,
        source_projection_array,
    )

    n0, n1 = len(layer0), len(layer1)
    kept = (n1 + (n0 > n1), tiles // BODY, NEI * TILE, NB * TILE)
    buffers = [
        ((n0, ext_tiles + 1, TILE, 64), bf16),
        ((n0, tiles, 64, 2 * TILE), bf16),
        ((n0, ext_tiles, 16, TILE), bf16),
        ((ext_tiles, 32, TILE), bf16),
        ((n0, tiles, 3 * NB * 16, TILE), bf16),
        ((n0, atoms, 2 * ghost), bf16),
        ((n0, tiles, TILE, TILE), bf16),
        ((n1, tiles, TILE, TILE), bf16),
        ((n1 + 1, ext_tiles, TILE, TILE), bf16),
        ((n1, tiles, TILE, TILE), f32),
        ((tiles, NEI * TILE, TILE), f32),
        ((ext_tiles, TILE, TILE), bf16),
        ((tiles, TILE, TILE), bf16),
        ((tiles, 16, TILE), f32),
        ((n0, 8, TILE), jnp.int32),
    ]
    scratch = [
        pltpu.VMEM((len(held), 8, atoms + TILE), f32),
        pltpu.VMEM((channels, 8 * TILE), bf16),
        pltpu.VMEM((NB + 2, channels, TILE), f32),
        pltpu.SemaphoreType.DMA((len(held) + 2,)),
    ]
    scratch += [pltpu.VMEM(*buffer) for buffer in buffers] + [
        pltpu.SMEM((n0, 8, TILE), jnp.int32),
        pltpu.SemaphoreType.DMA((n0,)),
    ]
    scratch += [pltpu.VMEM(kept, bf16)] * BODY
    scratch += [pltpu.VMEM((NEI * TILE, 2 * TILE), f32)] * BODY

    outs = pl.pallas_call(
        functools.partial(main_kernel, (count, atoms, ghost)),
        out_shape=[shape((3, 1, atoms), f32)] * 3,
        in_specs=[smem] * 4 + [pl.BlockSpec(memory_space=pl.ANY)] * (len(held) + 2),
        out_specs=[vmem] * 3,
        scratch_shapes=scratch,
        compiler_params=pltpu.CompilerParams(vmem_limit_bytes=58 * 2**20),
    )(
        granted_swaps,
        thermal_levels,
        push_distance_taper,
        kind_inertia,
        *data,
        *weights,
    )
    return tuple(jnp.transpose(x, (1, 0, 2)) for x in outs)


def solution(mesh):
    in_specs = (
        P("rep", None, "dom"),
        P("rep", None, "dom"),
        P("rep", None, "dom"),
        P("rep", "dom"),
        P("rep", "dom"),
        P("rep", "dom", None),
        P("rep", "dom"),
    ) + (P(),) * 10
    out_specs = (P("rep", None, "dom"), P("rep", None, "dom"), P("rep", None, "dom"))
    step = functools.partial(local, mesh.shape["dom"], mesh.shape["rep"])
    return jax.shard_map(step, mesh=mesh, in_specs=in_specs, out_specs=out_specs, check_vma=False)
```

time: 34.7 us -> 29.6 us (0.85)
  Pallas kernels: 25.9 us -> 20.8 us
    pallas_call x1, Pallas kernels: 22 us -> 16.9 us  [local(): pl.pallas_call(functools.partial(main_kernel, (count, atoms, ghost)), out...]
  transfers between devices with their start and end apart: 3 -> 3, of which waited for: 1 -> 1; matrix products, arithmetic and copies ran while one was open for 2% -> 2% of each run, Pallas kernels for 7% -> 9%
where the time goes in v2:
time: 29.6 us; the launch traced here: 29.3 us
  Pallas kernels  20.8 us (70%)
  starting transfers between devices  5.07 us (17%)
  between operations  1.99 us (7%)
  local copies, waits for them, and re-layouts  1.2 us (4%)
    pallas_call x1, Pallas kernels, local(): pl.pallas_call(functools.partial(main_kernel, (count, atoms, ghost)), out...  16.9 us
    ppermute x1, starting transfers between devices, local(): from_odd = lax.ppermute(packed, ('rep', 'dom'), odd_all)  2.97 us
    pallas_call x1, Pallas kernels, local(): pl.pallas_call(weights_kernel, out_shape=[shape((channels, 8 * TILE), bf1...  2.5 us
    ppermute x1, starting transfers between devices, local(): lax.ppermute(chosen, 'dom', [((d + o) % count, d) for d in range(count)])  2.02 us
    pallas_call x1, Pallas kernels, local(): pl.pallas_call(pack_kernel, out_shape=shape((8, atoms + TILE), f32), in_s...  1.43 us
    unnamed x8, local copies, waits for them, and re-layouts  0.61 us
  transfers between devices with their start and end apart: 3, of which 1 were waited for; matrix products, arithmetic and copies ran while one was open for 2% of the time, Pallas kernels for 9%

profile of v2, /device:TPU:0, one launch (start us, length us, event | category | flops | bytes accessed | tf_op | source)
XLA Modules:
  0.0 29.3 jit_solution(869475926003368889)
XLA Ops:
  0.6 0.0 copy-start.3
  0.6 1.4 %shard_map.184 = f32[8,1152]{1,0:T(8,128)} custom-call(f32[3,1,1024]{2,1,0:T(1,128)} %bitcast.8, f32[3,1,1024]{2,1,0:T(1,128)} %bitcast.9, f32[3,1,1024]{2,1,0:T(1,128)} %bitcast.10, s32[1,1024]{1,0:T(1,128)} %kinds.1, s32[1,768]{1,0:T(1,128)} %ghosts.1, s32[1,4,8]{2,1,0:T(4,128)} %bitcast.11, s32[1,8]{1,0:T(1,128)} %counts.1, f32[16]{0:T(128)} %refs_3_.1), custom_call_target="tpu_custom_call" | custom-call | tf_op jit(solution)/shard_map/pallas_call | solution.py:458
  2.1 0.0 copy-start.1
  2.1 3.0 %collective-permute-start.1 = (f32[8,1152]{1,0:T(8,128)}, f32[8,1152]{1,0:T(8,128)S(1)}, u32[]{:S(2)}, u32[]{:S(2)}) collective-permute-start(f32[8,1152]{1,0:T(8,128)} %shard_map.184), channel_id=1, source_target_pairs={{2,4},{3,5},{4,2},{5,3},{6,8},{7,9},{8,6},{9,7},{10,12},{11,13},{1... | collective-permute-start | bytes 110600 | tf_op jit(solution)/shard_map/ppermute | solution.py:480
  5.0 0.1 collective-permute-start
  5.1 0.0 copy-done.3
  5.1 0.6 %dynamic_slice.3 = s32[1]{0:T(128)} dynamic-slice(s32[16]{0:T(128)S(1)} %copy-done.3, s32[]{:T(128)S(6)} %select_n.24), dynamic_slice_sizes={1} | dynamic-slice | bytes 12 | tf_op jit(solution)/shard_map/dynamic_slice | solution.py:482
  7.0 0.2 collective-permute-done.1
  7.3 0.0 collective-permute-done
  7.3 0.0 copy-done.1
  7.3 0.0 copy-start
  7.3 2.0 %collective-permute-start.2 = (f32[8,1152]{1,0:T(8,128)S(1)}, f32[8,1152]{1,0:T(8,128)S(1)}, u32[]{:S(2)}, u32[]{:S(2)}) collective-permute-start(f32[8,1152]{1,0:T(8,128)S(1)} %select_select_fusion.refs_4_), channel_id=1, source_target_pairs={{1,0},{0,1},{3,2},{2,3},{5,4},{4,5},{7,6},{6,7},{9,8},{8,9},{11,10... | collective-permute-start | bytes 110600 | tf_op jit(solution)/shard_map/ppermute | solution.py:488
  9.3 2.5 %shard_map.185 = (bf16[128,1024]{1,0:T(8,128)(2,1)}, f32[10,128,128]{2,1,0:T(8,128)}) custom-call(bf16[16,128]{1,0:T(8,128)(2,1)} %kind.1, f32[2,8,128]{2,1,0:T(8,128)} %coef.1, f32[2,128]{1,0:T(2,128)} %gain.1, bf16[2,128,128]{2,1,0:T(8,128)(2,1)} %mix.1, bf16[128,128]{1,0:T(8,128)(2,1)} %target.1, bf16[128,128]{1,0:T(8,128)(2,1)} %source.1), custom_call_target="tpu_custom_call" | custom-call | flops 1000000 | bytes 1000000 | tf_op jit(solution)/shard_map/pallas_call | solution.py:492
  11.8 0.0 copy-done
  11.8 0.0 collective-permute-done.2.refs_5_
  11.8 0.0 copy-start.2
  11.8 0.6 %copy-done.2 = f32[8,1152]{1,0:T(8,128)} copy-done((f32[8,1152]{1,0:T(8,128)}, f32[8,1152]{1,0:T(8,128)S(1)}, u32[]{:S(2)}) %copy-start.2) | copy-done | bytes 36888
  12.4 16.9 %shard_map.186 = (f32[3,1,1024]{2,1,0:T(1,128)}, f32[3,1,1024]{2,1,0:T(1,128)}, f32[3,1,1024]{2,1,0:T(1,128)}) custom-call(s32[16]{0:T(128)} %refs_0_.1, f32[16]{0:T(128)} %refs_1_.1, f32[8]{0:T(128)} %refs_2_.1, f32[16]{0:T(128)} %refs_3_.1, f32[8,1152]{1,0:T(8,128)} %copy-done, f32[8,1152]{1,0:T(8,128)} %copy-done.2, ...), custom_call_target="tpu_custom_call" | custom-call | tf_op jit(solution)/shard_map/pallas_call | solution.py:539
  (1 shorter events, 0.0 us)
Async XLA Ops:
  0.6 4.5 %copy-start.3 = (s32[16]{0:T(128)S(1)}, s32[16]{0:T(128)}, u32[]{:S(2)}) copy-start(s32[16]{0:T(128)} %refs_0_.1) | copy-start | bytes 196
  2.1 5.2 %copy-start.1 = (f32[8,1152]{1,0:T(8,128)S(1)}, f32[8,1152]{1,0:T(8,128)}, u32[]{:S(2)}) copy-start(f32[8,1152]{1,0:T(8,128)} %shard_map.184) | copy-start | bytes 110596
  2.1 5.2 %collective-permute-start.1 = (f32[8,1152]{1,0:T(8,128)}, f32[8,1152]{1,0:T(8,128)S(1)}, u32[]{:S(2)}, u32[]{:S(2)}) collective-permute-start(f32[8,1152]{1,0:T(8,128)} %shard_map.184), channel_id=1, source_target_pairs={{2,4},{3,5},{4,2},{5,3},{6,8},{7,9},{8,6},{9,7},{10,12},{11,13},{1... | collective-permute-start | bytes 110600 | tf_op jit(solution)/shard_map/ppermute | solution.py:480
  5.0 2.2 %collective-permute-start = (f32[8,1152]{1,0:T(8,128)}, f32[8,1152]{1,0:T(8,128)S(1)}, u32[]{:S(2)}, u32[]{:S(2)}) collective-permute-start(f32[8,1152]{1,0:T(8,128)} %shard_map.184), channel_id=1, source_target_pairs={{0,2},{2,0},{4,6},{6,4},{8,10},{10,8},{12,14},{14,12},{16,18},{18,... | collective-permute-start | bytes 110600 | tf_op jit(solution)/shard_map/ppermute | solution.py:479
  7.3 4.5 %copy-start = (f32[8,1152]{1,0:T(8,128)}, f32[8,1152]{1,0:T(8,128)S(1)}, u32[]{:S(2)}) copy-start(f32[8,1152]{1,0:T(8,128)S(1)} %select_select_fusion.refs_4_) | copy-start | bytes 110596
  7.3 4.5 %collective-permute-start.2 = (f32[8,1152]{1,0:T(8,128)S(1)}, f32[8,1152]{1,0:T(8,128)S(1)}, u32[]{:S(2)}, u32[]{:S(2)}) collective-permute-start(f32[8,1152]{1,0:T(8,128)S(1)} %select_select_fusion.refs_4_), channel_id=1, source_target_pairs={{1,0},{0,1},{3,2},{2,3},{5,4},{4,5},{7,6},{6,7},{9,8},{8,9},{11,10... | collective-permute-start | bytes 110600 | tf_op jit(solution)/shard_map/ppermute | solution.py:488
  11.8 0.6 %copy-start.2 = (f32[8,1152]{1,0:T(8,128)}, f32[8,1152]{1,0:T(8,128)S(1)}, u32[]{:S(2)}) copy-start(f32[8,1152]{1,0:T(8,128)S(1)} %collective-permute-done.2.refs_5_) | copy-start | bytes 110596

commit v3 on v2

--- a/solution.py
+++ b/solution.py
@@ -63,7 +63,22 @@
     out[NEI : NEI + 1, atoms : atoms + tiles] = counts[...].astype(f32)
 
 
-def weights_kernel(kind, coef, gain, mix, target, source, wide, columns):
+def weights_kernel(
+    kind, coef, gain, mix, target, source, swaps, levels, taper, inertia, wide, columns, small
+):
+    me = lax.axis_index("rep")
+    lane = lax.broadcasted_iota(jnp.int32, (1, TILE), 1)
+    factors, masses = jnp.zeros((1, TILE), f32), jnp.zeros((1, TILE), f32)
+    for b in range(NB):
+        scale = math.exp(-b * b) * UNLIFT / (math.sqrt(TILE * NEI * TILE) * SCALE)
+        factors = jnp.where(lane == b, taper[b] * scale, factors)
+    for s in range(inertia.shape[0]):
+        masses = jnp.where(lane == s, inertia[s], masses)
+    quotient = jnp.full((1, TILE), levels[me], f32) / jnp.full((1, TILE), levels[swaps[me]], f32)
+    small[0:1] = factors
+    small[1:2] = masses
+    small[2:3] = jnp.sqrt(quotient)
+    small[3:8] = jnp.zeros((5, TILE), f32)
     species = kind.shape[0]
     kinds_f = jnp.transpose(kind[...].astype(f32), (1, 0))
     coef_t = [jnp.transpose(coef[layer], (1, 0)) for layer in range(2)]
@@ -105,23 +120,21 @@
 
 
 def main_kernel(plan, *refs):
-    count, atoms, ghost = plan
+    count, atoms, ghost, species = plan
     layer1, layer0, held = domain_sets(count)
     tiles = atoms // TILE
     ghost_tiles = ghost // TILE
     ext_tiles = tiles + 2 * ghost_tiles
     n = len(held)
-    swaps, levels, taper, inertia = refs[:4]
-    refs = refs[4:]
-    outside = refs[: n + 2]
-    pos_out, vel_out, force_out = refs[n + 2 : n + 5]
-    held_data, wide, columns = refs[n + 5 : n + 8]
-    arrivals = refs[n + 8]
+    outside = refs[: n + 3]
+    outputs = refs[n + 3 : n + 6]
+    held_data, wide, columns, small = refs[n + 6 : n + 10]
+    pos_out, vel_out, force_out, arrivals, departures = refs[n + 10 : n + 15]
     data = {o: held_data.at[at] for at, o in enumerate(held)}
     inward = [
         pltpu.make_async_copy(src, dst, arrivals.at[at])
         for at, (src, dst) in enumerate(
-            zip(outside, [held_data.at[at] for at in range(n)] + [wide, columns])
+            zip(outside, [held_data.at[at] for at in range(n)] + [wide, columns, small])
         )
     ]
     for c in inward:
@@ -146,7 +159,7 @@
         ints,
         sm,
         sem,
-    ) = refs[n + 9 : -2 * BODY]
+    ) = refs[n + 15 : -2 * BODY]
     basis, squares = refs[-2 * BODY : -BODY], refs[-BODY:]
     u_parts = wide.at[:, 0 : 3 * TILE]
     mix_kind = wide.at[:, 3 * TILE : 4 * TILE + 16]
@@ -161,6 +174,14 @@
     ]
     for c in copies:
         c.start()
+
+    outward = [
+        pltpu.make_async_copy(src, dst, departures.at[at])
+        for at, (src, dst) in enumerate(zip((pos_out, vel_out, force_out), outputs))
+    ]
+    for d in range(3):
+        pos_out[d] = data[0][d : d + 1, 0:atoms]
+    outward[0].start()
 
     row_id = lax.broadcasted_iota(jnp.int32, (8, TILE), 0)
     species_id = lax.broadcasted_iota(jnp.int32, (16, TILE), 0).astype(f32)
@@ -265,7 +286,7 @@
                 part = dot(lhs, pair)
                 sums[p] = part if half == 0 else sums[p] + part
                 if own:
-                    part = even * envelope_factor(2 * p) + odd * envelope_factor(2 * p + 1)
+                    part = even * small[0, 2 * p] + odd * small[0, 2 * p + 1]
                     envelope = part if p == 0 else envelope + part
                 if p < NB // 2 - 1:
                     power = power + step
@@ -276,9 +297,6 @@
         high = sums.astype(bf16)
         low = (sums - high.astype(f32)).astype(bf16)
         species_sums[at, t] = jnp.concatenate([high, high, low], axis=0)
-
-    def envelope_factor(b):
-        return taper[b] * (math.exp(-b * b) * UNLIFT / (math.sqrt(TILE * NEI * TILE) * SCALE))
 
     def first_layer(at):
         messages = dot(u_parts[...], lanes_of([species_sums[at, t] for t in range(tiles)]))
@@ -392,36 +410,53 @@
         turned[t] = turn(own_hidden[t])
     own_hidden = lanes_of(own_hidden)
     wanted = dot(both_parts[...], jnp.concatenate([own_hidden, own_hidden], axis=0)).astype(bf16)
-    for t in range(tiles):
-        asked[t] = wanted[:, t * TILE : (t + 1) * TILE]
-
-    for t in range(tiles):
-        lhs = jnp.concatenate([turned[sm[0, k, t]] for k in range(NEI)], axis=0)
-        weight = (dot(lhs, asked[t]) * envelopes[t]).astype(bf16)
-        places = lanes_of([split_pos[sm[0, k, t]] for k in range(NEI)])
-        got = dot(places, weight)
-        pulls[t] = jnp.concatenate([got[0:8] + got[8:16] + got[16:24], got[24:32]], axis=0)
-
-    me = lax.axis_index("rep")
-    quotient = jnp.sqrt(
-        jnp.full((1, TILE), levels[me], f32) / jnp.full((1, TILE), levels[swaps[me]], f32)
-    )
+    empty = jnp.zeros((TILE, TILE), bf16)
+    duos = range(tiles // 2)
+    for q in duos:
+        first, second = (wanted[:, t * TILE : (t + 1) * TILE] for t in (2 * q, 2 * q + 1))
+        asked[q] = jnp.concatenate([lanes_of([first, empty]), lanes_of([empty, second])], axis=0)
+
+    def weigh(q):
+        lhs = [lanes_of([turned[sm[0, k, t]] for t in (2 * q, 2 * q + 1)]) for k in range(NEI)]
+        scores = dot(jnp.concatenate(lhs, axis=0), asked[q])
+        return (scores * lanes_of([envelopes[t] for t in (2 * q, 2 * q + 1)])).astype(bf16)
+
+    def pull(q, weight):
+        places = [
+            lanes_of([split_pos[sm[0, k, t]] for k in range(NEI)]) for t in (2 * q, 2 * q + 1)
+        ]
+        got = dot(jnp.concatenate(places, axis=0), weight)
+        for side in range(2):
+            part = got[32 * side : 32 * (side + 1), side * TILE : (side + 1) * TILE]
+            pulls[2 * q + side] = jnp.concatenate(
+                [part[0:8] + part[8:16] + part[16:24], part[24:32]], axis=0
+            )
+
+    weights = {0: weigh(0)}
+    for q in duos:
+        if q + 1 in duos:
+            weights[q + 1] = weigh(q + 1)
+        pull(q, weights.pop(q))
+
     own = data[0]
     labels = own[6:7, 0:atoms]
     mass = jnp.zeros(labels.shape, f32)
-    for s in range(inertia.shape[0]):
-        mass = jnp.where(labels == s, inertia[s], mass)
+    for s in range(species):
+        mass = jnp.where(labels == s, small[1, s], mass)
     inv_mass = 1.0 / mass
     for t in range(tiles):
         lanes = slice(t * TILE, (t + 1) * TILE)
         got = pulls[t]
         force = got[0:8] - (own[:, lanes] - 0.5 * slab_width) * SCALE * got[8:9]
         velocity = own[3:6, lanes] + 0.5 * time_step * force[0:3] * inv_mass[:, lanes]
-        velocity = velocity * quotient
+        velocity = velocity * small[2, 0]
         for d in range(3):
-            pos_out[d, :, lanes] = own[d : d + 1, lanes]
             force_out[d, :, lanes] = force[d : d + 1]
             vel_out[d, :, lanes] = velocity[d : d + 1]
+    for c in outward[1:]:
+        c.start()
+    for c in outward:
+        c.wait()
 
 
 def local(
@@ -491,9 +526,14 @@
 
     weights = pl.pallas_call(
         weights_kernel,
-        out_shape=[shape((channels, 8 * TILE), bf16), shape((NB + 2, channels, TILE), f32)],
-        in_specs=[vmem] * 6,
-        out_specs=[vmem] * 2,
+        out_shape=[
+            shape((channels, 8 * TILE), bf16),
+            shape((NB + 2, channels, TILE), f32),
+            shape((8, TILE), f32),
+        ],
+        in_specs=[vmem] * 6 + [smem] * 4,
+        out_specs=[vmem] * 3,
+        compiler_params=pltpu.CompilerParams(vmem_limit_bytes=8 * 2**20),
         cost_estimate=pl.CostEstimate(flops=10**6, bytes_accessed=10**6, transcendentals=0),
     )(
         kind_vectors,
@@ -502,6 +542,10 @@
         feature_blend_coefficients,
         target_projection_array,
         source_projection_array,
+        granted_swaps,
+        thermal_levels,
+        push_distance_taper,
+        kind_inertia,
     )
 
     n0, n1 = len(layer0), len(layer1)
@@ -519,35 +563,38 @@
         ((n1, tiles, TILE, TILE), f32),
         ((tiles, NEI * TILE, TILE), f32),
         ((ext_tiles, TILE, TILE), bf16),
-        ((tiles, TILE, TILE), bf16),
+        ((tiles // 2, 2 * TILE, 2 * TILE), bf16),
         ((tiles, 16, TILE), f32),
         ((n0, 8, TILE), jnp.int32),
     ]
-    scratch = [
-        pltpu.VMEM((len(held), 8, atoms + TILE), f32),
-        pltpu.VMEM((channels, 8 * TILE), bf16),
-        pltpu.VMEM((NB + 2, channels, TILE), f32),
-        pltpu.SemaphoreType.DMA((len(held) + 2,)),
-    ]
+    inner = [
+        ((len(held), 8, atoms + TILE), f32),
+        ((channels, 8 * TILE), bf16),
+        ((NB + 2, channels, TILE), f32),
+    ]
+    outgoing = [((3, 1, atoms), f32)] * 3
+    outer = [(kept, bf16)] * BODY + [((NEI * TILE, 2 * TILE), f32)] * BODY
+    scratch = [pltpu.VMEM(*buffer) for buffer in inner] + [pltpu.SMEM((8, TILE), f32)]
+    scratch += [pltpu.VMEM(*buffer) for buffer in outgoing]
+    scratch += [pltpu.SemaphoreType.DMA((len(held) + 3,)), pltpu.SemaphoreType.DMA((3,))]
     scratch += [pltpu.VMEM(*buffer) for buffer in buffers] + [
         pltpu.SMEM((n0, 8, TILE), jnp.int32),
         pltpu.SemaphoreType.DMA((n0,)),
     ]
-    scratch += [pltpu.VMEM(kept, bf16)] * BODY
-    scratch += [pltpu.VMEM((NEI * TILE, 2 * TILE), f32)] * BODY
+    scratch += [pltpu.VMEM(*buffer) for buffer in outer]
+    limit = 6 * 2**20 + sum(
+        math.prod(dims[:-1]) * max(dims[-1], TILE) * jnp.dtype(kind).itemsize
+        for dims, kind in inner + outgoing + buffers + outer
+    )
 
     outs = pl.pallas_call(
-        functools.partial(main_kernel, (count, atoms, ghost)),
+        functools.partial(main_kernel, (count, atoms, ghost, kind_vectors.shape[0])),
         out_shape=[shape((3, 1, atoms), f32)] * 3,
-        in_specs=[smem] * 4 + [pl.BlockSpec(memory_space=pl.ANY)] * (len(held) + 2),
-        out_specs=[vmem] * 3,
+        in_specs=[pl.BlockSpec(memory_space=pl.ANY)] * (len(held) + 3),
+        out_specs=[pl.BlockSpec(memory_space=pl.ANY)] * 3,
         scratch_shapes=scratch,
-        compiler_params=pltpu.CompilerParams(vmem_limit_bytes=58 * 2**20),
+        compiler_params=pltpu.CompilerParams(vmem_limit_bytes=limit),
     )(
-        granted_swaps,
-        thermal_levels,
-        push_distance_taper,
-        kind_inertia,
         *data,
         *weights,
     )

time: 29.6 us -> 26.9 us (0.909)
  Pallas kernels: 20.8 us -> 17.6 us
  waiting for transfers between devices: 0.23 us -> 1.06 us
  starting transfers between devices: 5.07 us -> 4.64 us
    pallas_call x1, Pallas kernels: 16.9 us -> 14.8 us  [local(): pl.pallas_call(functools.partial(main_kernel, (count, atoms, ghost, kind_...]
    pallas_call x1, Pallas kernels: 2.5 us -> 1.32 us  [local(): pl.pallas_call(weights_kernel, out_shape=[shape((channels, 8 * TILE), bf1...]
    ppermute x1, waiting for transfers between devices: 0.01 us -> 1.06 us  [local(): lax.ppermute(chosen, 'dom', [((d + o) % count, d) for d in range(count)])]
    ppermute x1, starting transfers between devices: 2.02 us -> 1.58 us  [local(): lax.ppermute(chosen, 'dom', [((d + o) % count, d) for d in range(count)])]
    unnamed x8 -> x20, local copies, waits for them, and re-layouts: 0.61 us -> 0.71 us
  transfers between devices with their start and end apart: 3 -> 3, of which waited for: 1 -> 1; matrix products, arithmetic and copies ran while one was open for 2% -> 2% of each run, Pallas kernels for 9% -> 5%
where the time goes in v3:
time: 26.9 us; the launch traced here: 26.7 us
  Pallas kernels  17.6 us (65%)
  starting transfers between devices  4.64 us (17%)
  between operations  2.09 us (8%)
  local copies, waits for them, and re-layouts  1.29 us (5%)
  waiting for transfers between devices  1.06 us (4%)
    pallas_call x1, Pallas kernels, local(): pl.pallas_call(functools.partial(main_kernel, (count, atoms, ghost, kind_...  14.8 us
    ppermute x1, starting transfers between devices, local(): from_odd = lax.ppermute(packed, ('rep', 'dom'), odd_all)  2.97 us
    ppermute x1, starting transfers between devices, local(): lax.ppermute(chosen, 'dom', [((d + o) % count, d) for d in range(count)])  1.58 us
    pallas_call x1, Pallas kernels, local(): pl.pallas_call(pack_kernel, out_shape=shape((8, atoms + TILE), f32), in_s...  1.44 us
    pallas_call x1, Pallas kernels, local(): pl.pallas_call(weights_kernel, out_shape=[shape((channels, 8 * TILE), bf1...  1.32 us
    ppermute x1, waiting for transfers between devices, local(): lax.ppermute(chosen, 'dom', [((d + o) % count, d) for d in range(count)])  1.06 us
    unnamed x20, local copies, waits for them, and re-layouts  0.71 us
    dynamic_slice x1, local copies, waits for them, and re-layouts, local(): partner = granted_swaps[me]  0.58 us
  transfers between devices with their start and end apart: 3, of which 1 were waited for; matrix products, arithmetic and copies ran while one was open for 2% of the time, Pallas kernels for 5%

profile of v3, /device:TPU:0, one launch (start us, length us, event | category | flops | bytes accessed | tf_op | source)
XLA Modules:
  0.0 26.7 jit_solution(5346761797825697236)
XLA Ops:
  0.6 1.4 %shard_map.184 = f32[8,1152]{1,0:T(8,128)} custom-call(f32[3,1,1024]{2,1,0:T(1,128)} %bitcast.8, f32[3,1,1024]{2,1,0:T(1,128)} %bitcast.9, f32[3,1,1024]{2,1,0:T(1,128)} %bitcast.10, s32[1,1024]{1,0:T(1,128)} %kinds.1, s32[1,768]{1,0:T(1,128)} %ghosts.1, s32[1,4,8]{2,1,0:T(4,128)} %bitcast.11, s32[1,8]{1,0:T(1,128)} %counts.1, f32[16]{0:T(128)} %inertia.3), custom_call_target="tpu_custom_call" | custom-call | tf_op jit(solution)/shard_map/pallas_call | solution.py:493
  2.1 3.0 %collective-permute-start.1 = (f32[8,1152]{1,0:T(8,128)}, f32[8,1152]{1,0:T(8,128)S(1)}, u32[]{:S(2)}, u32[]{:S(2)}) collective-permute-start(f32[8,1152]{1,0:T(8,128)} %shard_map.184), channel_id=1, source_target_pairs={{2,4},{3,5},{4,2},{5,3},{6,8},{7,9},{8,6},{9,7},{10,12},{11,13},{1... | collective-permute-start | bytes 110600 | tf_op jit(solution)/shard_map/ppermute | solution.py:515
  5.0 0.1 collective-permute-start
  5.1 0.0 copy-start.7
  5.1 0.7 %copy-done.7 = s32[16]{0:T(128)S(1)} copy-done((s32[16]{0:T(128)S(1)}, s32[16]{0:T(128)}, u32[]{:S(2)}) %copy-start.7) | copy-done | bytes 88
  5.8 0.6 %dynamic_slice.3 = s32[1]{0:T(128)} dynamic-slice(s32[16]{0:T(128)S(1)} %copy-done.7, s32[]{:T(128)S(6)} %select_n.24), dynamic_slice_sizes={1} | dynamic-slice | bytes 12 | tf_op jit(solution)/shard_map/dynamic_slice | solution.py:517
  7.7 0.0 copy-start
  7.7 0.0 copy-start.1
  7.7 0.0 copy-start.2
  7.7 0.0 copy-start.3
  7.7 0.0 copy-start.4
  7.7 0.0 copy-start.5
  7.8 0.0 copy-start.6
  7.8 0.0 copy-start.8
  7.8 0.0 copy-start.9
  7.8 0.0 collective-permute-done.1
  7.8 0.0 collective-permute-done
  7.8 1.6 %collective-permute-start.2 = (f32[8,1152]{1,0:T(8,128)S(1)}, f32[8,1152]{1,0:T(8,128)S(1)}, u32[]{:S(2)}, u32[]{:S(2)}) collective-permute-start(f32[8,1152]{1,0:T(8,128)S(1)} %select_select_fusion.refs_0_), channel_id=1, source_target_pairs={{1,0},{0,1},{3,2},{2,3},{5,4},{4,5},{7,6},{6,7},{9,8},{8,9},{11,10... | collective-permute-start | bytes 110600 | tf_op jit(solution)/shard_map/ppermute | solution.py:523
  9.4 0.0 copy-done
  9.4 0.0 copy-done.1
  9.4 0.0 copy-done.2
  9.4 0.0 copy-done.3
  9.4 0.0 copy-done.4
  9.4 0.0 copy-done.5
  9.5 0.0 copy-done.6
  9.5 0.0 copy-done.8
  9.5 0.0 copy-done.9
  9.5 1.3 %shard_map.185 = (bf16[128,1024]{1,0:T(8,128)(2,1)S(1)}, f32[10,128,128]{2,1,0:T(8,128)S(1)}, f32[8,128]{1,0:T(8,128)S(1)}) custom-call(bf16[16,128]{1,0:T(8,128)(2,1)S(1)} %copy-done.4, f32[2,8,128]{2,1,0:T(8,128)S(1)} %copy-done.3, f32[2,128]{1,0:T(2,128)S(1)} %copy-done.6, bf16[2,128,128]{2,1,0:T(8,128)(2,1)S(1)} %copy-done, ...), custom_call_target="tpu_custom_call" | custom-call | flops 1000000 | bytes 1000000 | tf_op jit(solution)/shard_map/pallas_call | solution.py:527
  10.8 1.1 %collective-permute-done.2.refs_1_ = f32[8,1152]{1,0:T(8,128)S(1)} collective-permute-done((f32[8,1152]{1,0:T(8,128)S(1)}, f32[8,1152]{1,0:T(8,128)S(1)}, u32[]{:S(2)}, u32[]{:S(2)}) %collective-permute-start.2) | collective-permute-done | bytes 36896 | tf_op jit(solution)/shard_map/ppermute | solution.py:523
  11.9 14.8 %shard_map.186 = (f32[3,1,1024]{2,1,0:T(1,128)}, f32[3,1,1024]{2,1,0:T(1,128)}, f32[3,1,1024]{2,1,0:T(1,128)}) custom-call(f32[8,1152]{1,0:T(8,128)S(1)} %select_select_fusion.refs_0_, f32[8,1152]{1,0:T(8,128)S(1)} %collective-permute-done.2.refs_1_, bf16[128,1024]{1,0:T(8,128)(2,1)S(1)} %get-tuple-element.9.refs_2_, ...), custom_call_target="tpu_custom_call" | custom-call | tf_op jit(solution)/shard_map/pallas_call | solution.py:590
  (1 shorter events, 0.0 us)
Async XLA Ops:
  2.1 5.7 %collective-permute-start.1 = (f32[8,1152]{1,0:T(8,128)}, f32[8,1152]{1,0:T(8,128)S(1)}, u32[]{:S(2)}, u32[]{:S(2)}) collective-permute-start(f32[8,1152]{1,0:T(8,128)} %shard_map.184), channel_id=1, source_target_pairs={{2,4},{3,5},{4,2},{5,3},{6,8},{7,9},{8,6},{9,7},{10,12},{11,13},{1... | collective-permute-start | bytes 110600 | tf_op jit(solution)/shard_map/ppermute | solution.py:515
  5.0 2.8 %collective-permute-start = (f32[8,1152]{1,0:T(8,128)}, f32[8,1152]{1,0:T(8,128)S(1)}, u32[]{:S(2)}, u32[]{:S(2)}) collective-permute-start(f32[8,1152]{1,0:T(8,128)} %shard_map.184), channel_id=1, source_target_pairs={{0,2},{2,0},{4,6},{6,4},{8,10},{10,8},{12,14},{14,12},{16,18},{18,... | collective-permute-start | bytes 110600 | tf_op jit(solution)/shard_map/ppermute | solution.py:514
  5.1 0.7 %copy-start.7 = (s32[16]{0:T(128)S(1)}, s32[16]{0:T(128)}, u32[]{:S(2)}) copy-start(s32[16]{0:T(128)} %swaps.1) | copy-start | bytes 196
  7.7 1.7 %copy-start = (bf16[2,128,128]{2,1,0:T(8,128)(2,1)S(1)}, bf16[2,128,128]{2,1,0:T(8,128)(2,1)}, u32[]{:S(2)}) copy-start(bf16[2,128,128]{2,1,0:T(8,128)(2,1)} %mix.1) | copy-start | bytes 196612
  7.7 1.7 %copy-start.1 = (bf16[128,128]{1,0:T(8,128)(2,1)S(1)}, bf16[128,128]{1,0:T(8,128)(2,1)}, u32[]{:S(2)}) copy-start(bf16[128,128]{1,0:T(8,128)(2,1)} %target.1) | copy-start | bytes 98308
  7.7 1.7 %copy-start.2 = (bf16[128,128]{1,0:T(8,128)(2,1)S(1)}, bf16[128,128]{1,0:T(8,128)(2,1)}, u32[]{:S(2)}) copy-start(bf16[128,128]{1,0:T(8,128)(2,1)} %source.1) | copy-start | bytes 98308
  7.7 1.7 %copy-start.3 = (f32[2,8,128]{2,1,0:T(8,128)S(1)}, f32[2,8,128]{2,1,0:T(8,128)}, u32[]{:S(2)}) copy-start(f32[2,8,128]{2,1,0:T(8,128)} %coef.1) | copy-start | bytes 24580
  7.7 1.7 %copy-start.4 = (bf16[16,128]{1,0:T(8,128)(2,1)S(1)}, bf16[16,128]{1,0:T(8,128)(2,1)}, u32[]{:S(2)}) copy-start(bf16[16,128]{1,0:T(8,128)(2,1)} %kind.1) | copy-start | bytes 12292
  7.7 1.7 %copy-start.5 = (f32[16]{0:T(128)S(1)}, f32[16]{0:T(128)}, u32[]{:S(2)}) copy-start(f32[16]{0:T(128)} %inertia.3) | copy-start | bytes 196
  7.8 1.7 %copy-start.6 = (f32[2,128]{1,0:T(2,128)S(1)}, f32[2,128]{1,0:T(2,128)}, u32[]{:S(2)}) copy-start(f32[2,128]{1,0:T(2,128)} %gain.1) | copy-start | bytes 3076
  7.8 1.7 %copy-start.8 = (f32[16]{0:T(128)S(1)}, f32[16]{0:T(128)}, u32[]{:S(2)}) copy-start(f32[16]{0:T(128)} %levels.1) | copy-start | bytes 196
  7.8 1.7 %copy-start.9 = (f32[8]{0:T(128)S(1)}, f32[8]{0:T(128)}, u32[]{:S(2)}) copy-start(f32[8]{0:T(128)} %taper.1) | copy-start | bytes 100
  7.8 4.0 %collective-permute-start.2 = (f32[8,1152]{1,0:T(8,128)S(1)}, f32[8,1152]{1,0:T(8,128)S(1)}, u32[]{:S(2)}, u32[]{:S(2)}) collective-permute-start(f32[8,1152]{1,0:T(8,128)S(1)} %select_select_fusion.refs_0_), channel_id=1, source_target_pairs={{1,0},{0,1},{3,2},{2,3},{5,4},{4,5},{7,6},{6,7},{9,8},{8,9},{11,10... | collective-permute-start | bytes 110600 | tf_op jit(solution)/shard_map/ppermute | solution.py:523

commit v4 on v3

--- a/solution.py
+++ b/solution.py
@@ -26,7 +26,6 @@
 UNLIFT = 2.0**-TOP
 STEEP = 4.0 * LOG2E
 FAR = (40.0 * LOG2E) ** 2
-BODY = 4
 
 
 def distinct(offsets, count):
@@ -159,13 +158,13 @@
         ints,
         sm,
         sem,
-    ) = refs[n + 15 : -2 * BODY]
-    basis, squares = refs[-2 * BODY : -BODY], refs[-BODY:]
+    ) = refs[n + 15 : -3]
+    basis, squares = refs[-3], refs[-2:]
     u_parts = wide.at[:, 0 : 3 * TILE]
     mix_kind = wide.at[:, 3 * TILE : 4 * TILE + 16]
     mix_second = wide.at[:, 5 * TILE : 6 * TILE]
     both_parts = wide.at[:, 6 * TILE : 8 * TILE]
-    kept = basis[0].shape[0]
+    kept = basis.shape[0]
 
     for at, o in enumerate(layer0):
         ints[at] = data[o][:, atoms : atoms + TILE].astype(jnp.int32)
@@ -262,18 +261,15 @@
         ]
         return dot(jnp.concatenate(far, axis=0), near_rhs[at, t])
 
-    bodies = tiles // BODY
-    steps = len(layer0) * bodies
-
-    def basis_step(at, body, u, own):
-        t = BODY * body + u
-        place = jnp.minimum(at, kept - 1)
+    def basis_step(at, t, values):
+        own = at == 0
+        place = min(at, kept - 1)
         sums = [None] * (NB // 2)
         for half in range(NEI // 2):
             rows = slice(2 * half * TILE, 2 * (half + 1) * TILE)
             lhs = lanes_of([onehot[at, sm[at, 2 * half + k, t]] for k in range(2)])
-            power = squares[u][rows, 0:TILE]
-            square = jnp.minimum(jnp.maximum(squares[u][rows, TILE : 2 * TILE], 1e-30), FAR)
+            power = values[rows, 0:TILE]
+            square = jnp.minimum(jnp.maximum(values[rows, TILE : 2 * TILE], 1e-30), FAR)
             slope = square * lax.rsqrt(square)
             ratio = jnp.exp2(slope)
             step = slope + slope
@@ -282,7 +278,7 @@
                 even = jnp.exp2(power)
                 odd = even * ratio
                 pair = lanes_of([even.astype(bf16), odd.astype(bf16)])
-                basis[u][place, body, rows, 2 * p * TILE : 2 * (p + 1) * TILE] = pair
+                basis[place, t, rows, 2 * p * TILE : 2 * (p + 1) * TILE] = pair
                 part = dot(lhs, pair)
                 sums[p] = part if half == 0 else sums[p] + part
                 if own:
@@ -306,42 +302,17 @@
         kinds = lanes_of([onehot[at, t] for t in range(tiles)])
         hidden = dot(mix_kind[...], jnp.concatenate([lanes_of(activations), kinds], axis=0))
         for t in range(tiles):
-            hidden1[at, t] = hidden[:, t * TILE : (t + 1) * TILE].astype(bf16)
-
-    squares[0][...] = offsets(0, 0)
-
-    def body_step(own, m, _):
-        at, body = m // bodies, m % bodies
-        after = jnp.minimum(m + 1, steps - 1)
-        for u in range(BODY):
-            if u == BODY - 1:
-                upcoming = offsets(after // bodies, BODY * (after % bodies))
-            else:
-                upcoming = offsets(at, BODY * body + u + 1)
-            basis_step(at, body, u, own)
-            squares[(u + 1) % BODY][...] = upcoming
-        return 0
-
-    for c in inward[n:]:
-        c.wait()
-    lax.fori_loop(0, bodies, functools.partial(body_step, True), 0)
-    lax.fori_loop(bodies, steps, functools.partial(body_step, False), 0)
-
-    for at, o in enumerate(layer0):
-        chosen = data[o][7:8, 0 : 2 * ghost]
-
-        def pick_step(c, _):
-            first = pl.multiple_of(c * TILE, TILE)
-            rows = lax.broadcasted_iota(jnp.int32, (TILE, 2 * ghost), 0) + first
-            ghost_pick[at, pl.ds(first, TILE), :] = jnp.where(
-                rows.astype(f32) == chosen, 1.0, 0.0
-            ).astype(bf16)
-            return 0
-
-        lax.fori_loop(0, tiles, pick_step, 0)
-
-    for at in range(len(layer0)):
-        first_layer(at)
+            block = hidden[:, t * TILE : (t + 1) * TILE].astype(bf16)
+            hidden1[at, t] = block
+            if at < len(layer1):
+                ext_hidden[at, t] = block
+
+    def pick_step(at, c):
+        chosen = data[layer0[at]][7:8, 0 : 2 * ghost]
+        rows = lax.broadcasted_iota(jnp.int32, (TILE, 2 * ghost), 0) + c * TILE
+        ghost_pick[at, c * TILE : (c + 1) * TILE, :] = jnp.where(
+            rows.astype(f32) == chosen, 1.0, 0.0
+        ).astype(bf16)
 
     def extend(target, source_hidden, sets, o):
         for side, other in ((0, (o - 1) % count), (1, (o + 1) % count)):
@@ -357,7 +328,7 @@
     def second_step(keep, t):
         at = layer0.index(layer1[keep])
         lhs = lanes_of([ext_hidden[keep, sm[at, k, t]] for k in range(NEI)])
-        sums = dot(lhs, basis[t % BODY][keep, t // BODY])
+        sums = dot(lhs, basis[keep, t])
         messages = None
         for b in range(NB):
             part = sums[:, b * TILE : (b + 1) * TILE] * columns[b]
@@ -381,12 +352,47 @@
 
     last = ext_hidden.at[len(layer1)]
     order = list(range(1, len(layer1))) + [0]
-    for keep in order:
-        o = layer1[keep]
-        for t in range(tiles):
-            ext_hidden[keep, t] = hidden1[layer0.index(o), t]
-        extend(ext_hidden.at[keep], hidden1, layer0, o)
-    pending = []
+    jobs = [
+        functools.partial(pick_step, at, c) for at in range(len(layer0)) for c in range(tiles)
+    ]
+    imports = {
+        keep: functools.partial(extend, ext_hidden.at[keep], hidden1, layer0, o)
+        for keep, o in enumerate(layer1)
+    }
+    import_of = dict(imports)
+    ready = set()
+
+    def close_first(at):
+        first_layer(at)
+        ready.add(layer0[at])
+        for keep, o in enumerate(layer1):
+            if keep in imports and {(o - 1) % count, (o + 1) % count} <= ready:
+                jobs.append(imports.pop(keep))
+
+    for c in inward[n:]:
+        c.wait()
+    sequence = [(at, t) for at in range(len(layer0)) for t in range(tiles)]
+    squares[0][...] = offsets(0, 0)
+    for i, (at, t) in enumerate(sequence):
+        if i + 1 < len(sequence):
+            upcoming = offsets(*sequence[i + 1])
+        basis_step(at, t, squares[i % 2])
+        if i + 1 < len(sequence):
+            squares[(i + 1) % 2][...] = upcoming
+        if at:
+            for _ in range(min(len(jobs), 4)):
+                jobs.pop(0)()
+        if t == tiles - 1 and at < len(layer0) - 1:
+            jobs.insert(0, functools.partial(close_first, at))
+    for job in jobs:
+        job()
+    jobs = []
+    close_first(len(layer0) - 1)
+    if import_of[order[0]] in jobs:
+        jobs.remove(import_of[order[0]])
+        import_of[order[0]]()
+    pending = list(jobs)
+
     for keep in order:
         activations = []
         for t in range(tiles):
@@ -549,7 +555,7 @@
     )
 
     n0, n1 = len(layer0), len(layer1)
-    kept = (n1 + (n0 > n1), tiles // BODY, NEI * TILE, NB * TILE)
+    kept = (n1 + (n0 > n1), tiles, NEI * TILE, NB * TILE)
     buffers = [
         ((n0, ext_tiles + 1, TILE, 64), bf16),
         ((n0, tiles, 64, 2 * TILE), bf16),
@@ -573,7 +579,7 @@
         ((NB + 2, channels, TILE), f32),
     ]
     outgoing = [((3, 1, atoms), f32)] * 3
-    outer = [(kept, bf16)] * BODY + [((NEI * TILE, 2 * TILE), f32)] * BODY
+    outer = [(kept, bf16)] + [((NEI * TILE, 2 * TILE), f32)] * 2
     scratch = [pltpu.VMEM(*buffer) for buffer in inner] + [pltpu.SMEM((8, TILE), f32)]
     scratch += [pltpu.VMEM(*buffer) for buffer in outgoing]
     scratch += [pltpu.SemaphoreType.DMA((len(held) + 3,)), pltpu.SemaphoreType.DMA((3,))]
@@ -582,7 +588,7 @@
         pltpu.SemaphoreType.DMA((n0,)),
     ]
     scratch += [pltpu.VMEM(*buffer) for buffer in outer]
-    limit = 6 * 2**20 + sum(
+    limit = 9 * 2**20 + sum(
         math.prod(dims[:-1]) * max(dims[-1], TILE) * jnp.dtype(kind).itemsize
         for dims, kind in inner + outgoing + buffers + outer
     )

time: 26.9 us -> 25.3 us (0.941)
  Pallas kernels: 17.6 us -> 16 us
    pallas_call x1, Pallas kernels: 14.8 us -> 13.3 us  [local(): pl.pallas_call(functools.partial(main_kernel, (count, atoms, ghost, kind_...]
where the time goes in v4:
time: 25.3 us; the launch traced here: 25.1 us
  Pallas kernels  16 us (63%)
  starting transfers between devices  4.64 us (18%)
  between operations  2.09 us (8%)
  local copies, waits for them, and re-layouts  1.29 us (5%)
  waiting for transfers between devices  1.06 us (4%)
    pallas_call x1, Pallas kernels, local(): pl.pallas_call(functools.partial(main_kernel, (count, atoms, ghost, kind_...  13.3 us
    ppermute x1, starting transfers between devices, local(): from_odd = lax.ppermute(packed, ('rep', 'dom'), odd_all)  2.97 us
    ppermute x1, starting transfers between devices, local(): lax.ppermute(chosen, 'dom', [((d + o) % count, d) for d in range(count)])  1.58 us
    pallas_call x1, Pallas kernels, local(): pl.pallas_call(pack_kernel, out_shape=shape((8, atoms + TILE), f32), in_s...  1.44 us
    pallas_call x1, Pallas kernels, local(): pl.pallas_call(weights_kernel, out_shape=[shape((channels, 8 * TILE), bf1...  1.32 us
    ppermute x1, waiting for transfers between devices, local(): lax.ppermute(chosen, 'dom', [((d + o) % count, d) for d in range(count)])  1.06 us
    unnamed x20, local copies, waits for them, and re-layouts  0.71 us
    dynamic_slice x1, local copies, waits for them, and re-layouts, local(): partner = granted_swaps[me]  0.58 us
  transfers between devices with their start and end apart: 3, of which 1 were waited for; matrix products, arithmetic and copies ran while one was open for 2% of the time, Pallas kernels for 5%

profile of v4, /device:TPU:0, one launch (start us, length us, event | category | flops | bytes accessed | tf_op | source)
XLA Modules:
  0.0 25.1 jit_solution(14021585676207192251)
XLA Ops:
  0.6 1.4 %shard_map.184 = f32[8,1152]{1,0:T(8,128)} custom-call(f32[3,1,1024]{2,1,0:T(1,128)} %bitcast.8, f32[3,1,1024]{2,1,0:T(1,128)} %bitcast.9, f32[3,1,1024]{2,1,0:T(1,128)} %bitcast.10, s32[1,1024]{1,0:T(1,128)} %kinds.1, s32[1,768]{1,0:T(1,128)} %ghosts.1, s32[1,4,8]{2,1,0:T(4,128)} %bitcast.11, s32[1,8]{1,0:T(1,128)} %counts.1, f32[16]{0:T(128)} %inertia.3), custom_call_target="tpu_custom_call" | custom-call | tf_op jit(solution)/shard_map/pallas_call | solution.py:499
  2.1 3.0 %collective-permute-start.1 = (f32[8,1152]{1,0:T(8,128)}, f32[8,1152]{1,0:T(8,128)S(1)}, u32[]{:S(2)}, u32[]{:S(2)}) collective-permute-start(f32[8,1152]{1,0:T(8,128)} %shard_map.184), channel_id=1, source_target_pairs={{2,4},{3,5},{4,2},{5,3},{6,8},{7,9},{8,6},{9,7},{10,12},{11,13},{1... | collective-permute-start | bytes 110600 | tf_op jit(solution)/shard_map/ppermute | solution.py:521
  5.0 0.1 collective-permute-start
  5.1 0.0 copy-start.7
  5.1 0.7 %copy-done.7 = s32[16]{0:T(128)S(1)} copy-done((s32[16]{0:T(128)S(1)}, s32[16]{0:T(128)}, u32[]{:S(2)}) %copy-start.7) | copy-done | bytes 88
  5.8 0.6 %dynamic_slice.3 = s32[1]{0:T(128)} dynamic-slice(s32[16]{0:T(128)S(1)} %copy-done.7, s32[]{:T(128)S(6)} %select_n.24), dynamic_slice_sizes={1} | dynamic-slice | bytes 12 | tf_op jit(solution)/shard_map/dynamic_slice | solution.py:523
  7.7 0.0 copy-start
  7.7 0.0 copy-start.1
  7.7 0.0 copy-start.2
  7.7 0.0 copy-start.3
  7.7 0.0 copy-start.4
  7.7 0.0 copy-start.5
  7.8 0.0 copy-start.6
  7.8 0.0 copy-start.8
  7.8 0.0 copy-start.9
  7.8 0.0 collective-permute-done.1
  7.8 0.0 collective-permute-done
  7.8 1.6 %collective-permute-start.2 = (f32[8,1152]{1,0:T(8,128)S(1)}, f32[8,1152]{1,0:T(8,128)S(1)}, u32[]{:S(2)}, u32[]{:S(2)}) collective-permute-start(f32[8,1152]{1,0:T(8,128)S(1)} %select_select_fusion.refs_0_), channel_id=1, source_target_pairs={{1,0},{0,1},{3,2},{2,3},{5,4},{4,5},{7,6},{6,7},{9,8},{8,9},{11,10... | collective-permute-start | bytes 110600 | tf_op jit(solution)/shard_map/ppermute | solution.py:529
  9.4 0.0 copy-done
  9.4 0.0 copy-done.1
  9.4 0.0 copy-done.2
  9.4 0.0 copy-done.3
  9.4 0.0 copy-done.4
  9.4 0.0 copy-done.5
  9.5 0.0 copy-done.6
  9.5 0.0 copy-done.8
  9.5 0.0 copy-done.9
  9.5 1.3 %shard_map.185 = (bf16[128,1024]{1,0:T(8,128)(2,1)S(1)}, f32[10,128,128]{2,1,0:T(8,128)S(1)}, f32[8,128]{1,0:T(8,128)S(1)}) custom-call(bf16[16,128]{1,0:T(8,128)(2,1)S(1)} %copy-done.4, f32[2,8,128]{2,1,0:T(8,128)S(1)} %copy-done.3, f32[2,128]{1,0:T(2,128)S(1)} %copy-done.6, bf16[2,128,128]{2,1,0:T(8,128)(2,1)S(1)} %copy-done, ...), custom_call_target="tpu_custom_call" | custom-call | flops 1000000 | bytes 1000000 | tf_op jit(solution)/shard_map/pallas_call | solution.py:533
  10.8 1.1 %collective-permute-done.2.refs_1_ = f32[8,1152]{1,0:T(8,128)S(1)} collective-permute-done((f32[8,1152]{1,0:T(8,128)S(1)}, f32[8,1152]{1,0:T(8,128)S(1)}, u32[]{:S(2)}, u32[]{:S(2)}) %collective-permute-start.2) | collective-permute-done | bytes 36896 | tf_op jit(solution)/shard_map/ppermute | solution.py:529
  11.9 13.3 %shard_map.186 = (f32[3,1,1024]{2,1,0:T(1,128)}, f32[3,1,1024]{2,1,0:T(1,128)}, f32[3,1,1024]{2,1,0:T(1,128)}) custom-call(f32[8,1152]{1,0:T(8,128)S(1)} %select_select_fusion.refs_0_, f32[8,1152]{1,0:T(8,128)S(1)} %collective-permute-done.2.refs_1_, bf16[128,1024]{1,0:T(8,128)(2,1)S(1)} %get-tuple-element.9.refs_2_, ...), custom_call_target="tpu_custom_call" | custom-call | tf_op jit(solution)/shard_map/pallas_call | solution.py:596
  (1 shorter events, 0.0 us)
Async XLA Ops:
  2.1 5.7 %collective-permute-start.1 = (f32[8,1152]{1,0:T(8,128)}, f32[8,1152]{1,0:T(8,128)S(1)}, u32[]{:S(2)}, u32[]{:S(2)}) collective-permute-start(f32[8,1152]{1,0:T(8,128)} %shard_map.184), channel_id=1, source_target_pairs={{2,4},{3,5},{4,2},{5,3},{6,8},{7,9},{8,6},{9,7},{10,12},{11,13},{1... | collective-permute-start | bytes 110600 | tf_op jit(solution)/shard_map/ppermute | solution.py:521
  5.0 2.8 %collective-permute-start = (f32[8,1152]{1,0:T(8,128)}, f32[8,1152]{1,0:T(8,128)S(1)}, u32[]{:S(2)}, u32[]{:S(2)}) collective-permute-start(f32[8,1152]{1,0:T(8,128)} %shard_map.184), channel_id=1, source_target_pairs={{0,2},{2,0},{4,6},{6,4},{8,10},{10,8},{12,14},{14,12},{16,18},{18,... | collective-permute-start | bytes 110600 | tf_op jit(solution)/shard_map/ppermute | solution.py:520
  5.1 0.7 %copy-start.7 = (s32[16]{0:T(128)S(1)}, s32[16]{0:T(128)}, u32[]{:S(2)}) copy-start(s32[16]{0:T(128)} %swaps.1) | copy-start | bytes 196
  7.7 1.7 %copy-start = (bf16[2,128,128]{2,1,0:T(8,128)(2,1)S(1)}, bf16[2,128,128]{2,1,0:T(8,128)(2,1)}, u32[]{:S(2)}) copy-start(bf16[2,128,128]{2,1,0:T(8,128)(2,1)} %mix.1) | copy-start | bytes 196612
  7.7 1.7 %copy-start.1 = (bf16[128,128]{1,0:T(8,128)(2,1)S(1)}, bf16[128,128]{1,0:T(8,128)(2,1)}, u32[]{:S(2)}) copy-start(bf16[128,128]{1,0:T(8,128)(2,1)} %target.1) | copy-start | bytes 98308
  7.7 1.7 %copy-start.2 = (bf16[128,128]{1,0:T(8,128)(2,1)S(1)}, bf16[128,128]{1,0:T(8,128)(2,1)}, u32[]{:S(2)}) copy-start(bf16[128,128]{1,0:T(8,128)(2,1)} %source.1) | copy-start | bytes 98308
  7.7 1.7 %copy-start.3 = (f32[2,8,128]{2,1,0:T(8,128)S(1)}, f32[2,8,128]{2,1,0:T(8,128)}, u32[]{:S(2)}) copy-start(f32[2,8,128]{2,1,0:T(8,128)} %coef.1) | copy-start | bytes 24580
  7.7 1.7 %copy-start.4 = (bf16[16,128]{1,0:T(8,128)(2,1)S(1)}, bf16[16,128]{1,0:T(8,128)(2,1)}, u32[]{:S(2)}) copy-start(bf16[16,128]{1,0:T(8,128)(2,1)} %kind.1) | copy-start | bytes 12292
  7.7 1.7 %copy-start.5 = (f32[16]{0:T(128)S(1)}, f32[16]{0:T(128)}, u32[]{:S(2)}) copy-start(f32[16]{0:T(128)} %inertia.3) | copy-start | bytes 196
  7.8 1.7 %copy-start.6 = (f32[2,128]{1,0:T(2,128)S(1)}, f32[2,128]{1,0:T(2,128)}, u32[]{:S(2)}) copy-start(f32[2,128]{1,0:T(2,128)} %gain.1) | copy-start | bytes 3076
  7.8 1.7 %copy-start.8 = (f32[16]{0:T(128)S(1)}, f32[16]{0:T(128)}, u32[]{:S(2)}) copy-start(f32[16]{0:T(128)} %levels.1) | copy-start | bytes 196
  7.8 1.7 %copy-start.9 = (f32[8]{0:T(128)S(1)}, f32[8]{0:T(128)}, u32[]{:S(2)}) copy-start(f32[8]{0:T(128)} %taper.1) | copy-start | bytes 100
  7.8 4.0 %collective-permute-start.2 = (f32[8,1152]{1,0:T(8,128)S(1)}, f32[8,1152]{1,0:T(8,128)S(1)}, u32[]{:S(2)}, u32[]{:S(2)}) collective-permute-start(f32[8,1152]{1,0:T(8,128)S(1)} %select_select_fusion.refs_0_), channel_id=1, source_target_pairs={{1,0},{0,1},{3,2},{2,3},{5,4},{4,5},{7,6},{6,7},{9,8},{8,9},{11,10... | collective-permute-start | bytes 110600 | tf_op jit(solution)/shard_map/ppermute | solution.py:529

commit v5 on v4

--- a/solution.py
+++ b/solution.py
@@ -43,7 +43,24 @@
     return jnp.dot(a, b, preferred_element_type=f32)
 
 
-def pack_kernel(loc, speed, push, kinds, ghosts, lists, counts, inertia, out):
+def pack_kernel(
+    loc, speed, push, kinds, ghosts, lists, counts, inertia, swaps, levels, taper, out, small
+):
+    me = lax.axis_index("rep")
+    lane = lax.broadcasted_iota(jnp.int32, (1, TILE), 1)
+    factors, masses = jnp.zeros((1, TILE), f32), jnp.zeros((1, TILE), f32)
+    for b in range(NB):
+        scale = math.exp(-b * b) * UNLIFT / (math.sqrt(TILE * NEI * TILE) * SCALE)
+        factors = jnp.where(lane == b, taper[b] * scale, factors)
+    for s in range(inertia.shape[0]):
+        masses = jnp.where(lane == s, inertia[s], masses)
+    quotient = jnp.full((1, TILE), levels[me], f32) / jnp.full((1, TILE), levels[swaps[me]], f32)
+    small[0:1] = factors
+    small[1:2] = masses
+    small[2:3] = jnp.sqrt(quotient)
+    partner = swaps[me]
+    rung = jnp.where(partner == me, 0, 1 + (jnp.minimum(me, partner) & 1))
+    small[3:8] = jnp.full((5, TILE), rung, jnp.int32).astype(f32)
     labels = kinds[...]
     mass = jnp.zeros(labels.shape, f32)
     for s in range(inertia.shape[0]):
@@ -63,21 +80,8 @@
 
 
 def weights_kernel(
-    kind, coef, gain, mix, target, source, swaps, levels, taper, inertia, wide, columns, small
+    kind, coef, gain, mix, projections, wide, columns
 ):
-    me = lax.axis_index("rep")
-    lane = lax.broadcasted_iota(jnp.int32, (1, TILE), 1)
-    factors, masses = jnp.zeros((1, TILE), f32), jnp.zeros((1, TILE), f32)
-    for b in range(NB):
-        scale = math.exp(-b * b) * UNLIFT / (math.sqrt(TILE * NEI * TILE) * SCALE)
-        factors = jnp.where(lane == b, taper[b] * scale, factors)
-    for s in range(inertia.shape[0]):
-        masses = jnp.where(lane == s, inertia[s], masses)
-    quotient = jnp.full((1, TILE), levels[me], f32) / jnp.full((1, TILE), levels[swaps[me]], f32)
-    small[0:1] = factors
-    small[1:2] = masses
-    small[2:3] = jnp.sqrt(quotient)
-    small[3:8] = jnp.zeros((5, TILE), f32)
     species = kind.shape[0]
     kinds_f = jnp.transpose(kind[...].astype(f32), (1, 0))
     coef_t = [jnp.transpose(coef[layer], (1, 0)) for layer in range(2)]
@@ -99,9 +103,7 @@
     wide[:, 4 * TILE : 5 * TILE] = jnp.concatenate(
         [kinds_f, jnp.zeros((kinds_f.shape[0], TILE - species), f32)], axis=1
     ).astype(bf16)
-    both = lax.dot_general(
-        source[...], target[...], (((1,), (1,)), ((), ())), preferred_element_type=f32
-    )
+    both = projections[...]
     high = both.astype(bf16)
     wide[:, 6 * TILE : 7 * TILE] = high
     wide[:, 7 * TILE : 8 * TILE] = (both - high.astype(f32)).astype(bf16)
@@ -125,21 +127,33 @@
     ghost_tiles = ghost // TILE
     ext_tiles = tiles + 2 * ghost_tiles
     n = len(held)
-    outside = refs[: n + 3]
-    outputs = refs[n + 3 : n + 6]
-    held_data, wide, columns, small = refs[n + 6 : n + 10]
-    pos_out, vel_out, force_out, arrivals, departures = refs[n + 10 : n + 15]
+    offers = refs[: 3 * n]
+    tables = refs[3 * n : 3 * n + 3]
+    refs = refs[3 * n + 3 :]
+    outputs = refs[:3]
+    offered, held_data, rung, wide, columns, small = refs[3:9]
+    pos_out, vel_out, force_out, arrivals, departures = refs[9:14]
     data = {o: held_data.at[at] for at, o in enumerate(held)}
     inward = [
         pltpu.make_async_copy(src, dst, arrivals.at[at])
         for at, (src, dst) in enumerate(
-            zip(outside, [held_data.at[at] for at in range(n)] + [wide, columns, small])
+            zip(
+                (*offers, tables[2], *tables),
+                [offered.at[at] for at in range(3 * n)] + [rung, wide, columns, small],
+            )
         )
     ]
     for c in inward:
         c.start()
-    for c in inward[:n]:
+    for c in inward[: 3 * n + 1]:
         c.wait()
+    place = rung[3:4]
+    for at in range(n):
+        for first in range(0, atoms + TILE, TILE):
+            lanes = slice(first, first + TILE)
+            here, even, odd = (offered[3 * at + k, :, lanes] for k in range(3))
+            held_data[at, :, lanes] = jnp.where(place == 0.0, here, jnp.where(place == 1.0, even, odd))
+
     (
         far_t,
         near_rhs,
@@ -158,7 +172,7 @@
         ints,
         sm,
         sem,
-    ) = refs[n + 15 : -3]
+    ) = refs[14:-3]
     basis, squares = refs[-3], refs[-2:]
     u_parts = wide.at[:, 0 : 3 * TILE]
     mix_kind = wide.at[:, 3 * TILE : 4 * TILE + 16]
@@ -369,7 +383,7 @@
             if keep in imports and {(o - 1) % count, (o + 1) % count} <= ready:
                 jobs.append(imports.pop(keep))
 
-    for c in inward[n:]:
+    for c in inward[3 * n + 1 :]:
         c.wait()
     sequence = [(at, t) for at in range(len(layer0)) for t in range(tiles)]
     squares[0][...] = offsets(0, 0)
@@ -496,11 +510,11 @@
     smem = pl.BlockSpec(memory_space=pltpu.SMEM)
     shape = jax.ShapeDtypeStruct
 
-    packed = pl.pallas_call(
+    packed, small = pl.pallas_call(
         pack_kernel,
-        out_shape=shape((8, atoms + TILE), f32),
-        in_specs=[vmem] * 7 + [smem],
-        out_specs=vmem,
+        out_shape=[shape((8, atoms + TILE), f32), shape((8, TILE), f32)],
+        in_specs=[vmem] * 7 + [smem] * 4,
+        out_specs=[vmem] * 2,
     )(
         jnp.transpose(particle_locations, (1, 0, 2)),
         jnp.transpose(particle_speeds, (1, 0, 2)),
@@ -510,35 +524,35 @@
         jnp.transpose(adjacent_block_labels, (0, 2, 1)),
         adjacent_place_totals,
         kind_inertia,
+        granted_swaps,
+        thermal_levels,
+        push_distance_taper,
     )
 
     even = [(i, i ^ 1) for i in range(replicas)]
     odd = [(i, ((i + 1) ^ 1) - 1) for i in range(1, replicas - 1)]
-    odd_all = [(a * count + d, b * count + d) for a, b in odd for d in range(count)] + [
+    rim = [
         (r * count + d, r * count + (d + 1) % count) for r in (0, replicas - 1) for d in range(count)
     ]
-    from_even = lax.ppermute(packed, "rep", even)
-    from_odd = lax.ppermute(packed, ("rep", "dom"), odd_all)
-    me = lax.axis_index("rep")
-    partner = granted_swaps[me]
-    low = jnp.minimum(me, partner)
-    chosen = jnp.where(partner == me, packed, jnp.where(low % 2 == 0, from_even, from_odd))
-    data = [
-        chosen
-        if o == 0
-        else lax.ppermute(chosen, "dom", [((d + o) % count, d) for d in range(count)])
-        for o in held
-    ]
-
+    offers = []
+    for o in held:
+        beside = [((d + o) % count, d) for d in range(count)]
+        here = packed if o == 0 else lax.ppermute(packed, "dom", beside)
+        across = [(a * count + c, b * count + d) for a, b in odd for c, d in beside]
+        offers += [
+            here,
+            lax.ppermute(here, "rep", even),
+            lax.ppermute(packed, ("rep", "dom"), across + rim),
+        ]
+    projections = dot(source_projection_array, target_projection_array.T)
     weights = pl.pallas_call(
         weights_kernel,
         out_shape=[
             shape((channels, 8 * TILE), bf16),
             shape((NB + 2, channels, TILE), f32),
-            shape((8, TILE), f32),
         ],
-        in_specs=[vmem] * 6 + [smem] * 4,
-        out_specs=[vmem] * 3,
+        in_specs=[vmem] * 5,
+        out_specs=[vmem] * 2,
         compiler_params=pltpu.CompilerParams(vmem_limit_bytes=8 * 2**20),
         cost_estimate=pl.CostEstimate(flops=10**6, bytes_accessed=10**6, transcendentals=0),
     )(
@@ -546,12 +560,7 @@
         stepwise_distance_coefficients,
         signal_scaling_factors,
         feature_blend_coefficients,
-        target_projection_array,
-        source_projection_array,
-        granted_swaps,
-        thermal_levels,
-        push_distance_taper,
-        kind_inertia,
+        projections,
     )
 
     n0, n1 = len(layer0), len(layer1)
@@ -574,7 +583,9 @@
         ((n0, 8, TILE), jnp.int32),
     ]
     inner = [
+        ((3 * len(held), 8, atoms + TILE), f32),
         ((len(held), 8, atoms + TILE), f32),
+        ((8, TILE), f32),
         ((channels, 8 * TILE), bf16),
         ((NB + 2, channels, TILE), f32),
     ]
@@ -582,7 +593,7 @@
     outer = [(kept, bf16)] + [((NEI * TILE, 2 * TILE), f32)] * 2
     scratch = [pltpu.VMEM(*buffer) for buffer in inner] + [pltpu.SMEM((8, TILE), f32)]
     scratch += [pltpu.VMEM(*buffer) for buffer in outgoing]
-    scratch += [pltpu.SemaphoreType.DMA((len(held) + 3,)), pltpu.SemaphoreType.DMA((3,))]
+    scratch += [pltpu.SemaphoreType.DMA((3 * len(held) + 4,)), pltpu.SemaphoreType.DMA((3,))]
     scratch += [pltpu.VMEM(*buffer) for buffer in buffers] + [
         pltpu.SMEM((n0, 8, TILE), jnp.int32),
         pltpu.SemaphoreType.DMA((n0,)),
@@ -596,13 +607,14 @@
     outs = pl.pallas_call(
         functools.partial(main_kernel, (count, atoms, ghost, kind_vectors.shape[0])),
         out_shape=[shape((3, 1, atoms), f32)] * 3,
-        in_specs=[pl.BlockSpec(memory_space=pl.ANY)] * (len(held) + 3),
+        in_specs=[pl.BlockSpec(memory_space=pl.ANY)] * (3 * len(held) + 3),
         out_specs=[pl.BlockSpec(memory_space=pl.ANY)] * 3,
         scratch_shapes=scratch,
         compiler_params=pltpu.CompilerParams(vmem_limit_bytes=limit),
     )(
-        *data,
+        *offers,
         *weights,
+        small,
     )
     return tuple(jnp.transpose(x, (1, 0, 2)) for x in outs)
 

time: 25.3 us -> 24 us (0.949)
  between operations: 2.09 us -> 0.73 us
  local copies, waits for them, and re-layouts: 1.29 us -> 0.06 us
  starting transfers between devices: 4.64 us -> 5.45 us
  waiting for transfers between devices: 1.06 us -> 1.59 us
    ppermute x3 -> x5, starting transfers between devices: 4.64 us -> 5.45 us  [the longest x1 3.03 us: local(): here = packed if o == 0 else lax.ppermute(packed, 'dom', beside)]
    unnamed x20 -> x16, local copies, waits for them, and re-layouts: 0.71 us -> 0.06 us
    dynamic_slice x1 -> x0, local copies, waits for them, and re-layouts: 0.58 us -> none  [local(): partner = granted_swaps[me]]
    pallas_call x1, Pallas kernels: 1.32 us -> 0.75 us  [local(): pl.pallas_call(weights_kernel, out_shape=[shape((channels, 8 * TILE), bf1...]
    ppermute x3 -> x5, waiting for transfers between devices: 1.06 us -> 1.59 us  [the longest x2 1.46 us: local(): lax.ppermute(packed, ('rep', 'dom'), across + rim)]
    pallas_call x1, Pallas kernels: 13.3 us -> 13.6 us  [local(): pl.pallas_call(functools.partial(main_kernel, (count, atoms, ghost, kind_...]
  transfers between devices with their start and end apart: 3 -> 5, of which waited for: 1 -> 3; matrix products, arithmetic and copies ran while one was open for 2% -> 1% of each run, Pallas kernels for 5% -> 3%
where the time goes in v5:
time: 24 us; the launch traced here: 23.7 us
  Pallas kernels  15.8 us (66%)
  starting transfers between devices  5.45 us (23%)
  waiting for transfers between devices  1.59 us (7%)
  between operations  0.73 us (3%)
    pallas_call x1, Pallas kernels, local(): pl.pallas_call(functools.partial(main_kernel, (count, atoms, ghost, kind_...  13.6 us
    ppermute x1, starting transfers between devices, local(): here = packed if o == 0 else lax.ppermute(packed, 'dom', beside)  3.03 us
    ppermute x2, starting transfers between devices, local(): lax.ppermute(packed, ('rep', 'dom'), across + rim)  2.03 us
    pallas_call x1, Pallas kernels, local(): pl.pallas_call(pack_kernel, out_shape=[shape((8, atoms + TILE), f32), sha...  1.47 us
    ppermute x2, waiting for transfers between devices, local(): lax.ppermute(packed, ('rep', 'dom'), across + rim)  1.46 us
    pallas_call x1, Pallas kernels, local(): pl.pallas_call(weights_kernel, out_shape=[shape((channels, 8 * TILE), bf1...  0.75 us
  transfers between devices with their start and end apart: 5, of which 3 were waited for; matrix products, arithmetic and copies ran while one was open for 1% of the time, Pallas kernels for 3%

profile of v5, /device:TPU:0, one launch (start us, length us, event | category | flops | bytes accessed | tf_op | source)
XLA Modules:
  0.0 23.7 jit_solution(4785050062243829074)
XLA Ops:
  0.6 0.0 copy-start
  0.7 0.0 copy-start.7
  0.7 1.5 %shard_map.184 = (f32[8,1152]{1,0:T(8,128)}, f32[8,128]{1,0:T(8,128)}) custom-call(f32[3,1,1024]{2,1,0:T(1,128)} %bitcast.9, f32[3,1,1024]{2,1,0:T(1,128)} %bitcast.10, f32[3,1,1024]{2,1,0:T(1,128)} %bitcast.11, s32[1,1024]{1,0:T(1,128)} %kinds.1, s32[1,768]{1,0:T(1,128)} %ghosts.1, s32[1,4,8]{2,1,0:T(4,128)} %bitcast.12, s32[1,8]{1,0:T(1,128)} %counts.1, ...), custom_call_target="tpu_custom_call" | custom-call | tf_op jit(solution)/shard_map/pallas_call | solution.py:513
  2.1 0.0 copy-start.1
  2.1 0.0 copy-start.3
  2.1 0.0 copy-start.5
  2.2 0.0 copy-start.6
  2.2 3.0 %collective-permute-start.2 = (f32[8,1152]{1,0:T(8,128)}, f32[8,1152]{1,0:T(8,128)S(1)}, u32[]{:S(2)}, u32[]{:S(2)}) collective-permute-start(f32[8,1152]{1,0:T(8,128)} %get-tuple-element.10.refs_0_), channel_id=1, source_target_pairs={{1,0},{0,1},{3,2},{2,3},{5,4},{4,5},{7,6},{6,7},{9,8},{8,9},{11,10... | collective-permute-start | bytes 110600 | tf_op jit(solution)/shard_map/ppermute | solution.py:540
  5.2 0.1 collective-permute-start.4
  5.3 1.9 %collective-permute-start.1 = (f32[8,1152]{1,0:T(8,128)}, f32[8,1152]{1,0:T(8,128)S(1)}, u32[]{:S(2)}, u32[]{:S(2)}) collective-permute-start(f32[8,1152]{1,0:T(8,128)} %get-tuple-element.10.refs_0_), channel_id=1, source_target_pairs={{2,4},{3,5},{4,2},{5,3},{6,8},{7,9},{8,6},{9,7},{10,12},{11,13},{1... | collective-permute-start | bytes 110600 | tf_op jit(solution)/shard_map/ppermute | solution.py:545
  7.2 0.0 collective-permute-start
  7.2 0.1 collective-permute-done.2.refs_3_
  7.3 0.4 %collective-permute-start.3 = (f32[8,1152]{1,0:T(8,128)S(1)}, f32[8,1152]{1,0:T(8,128)S(1)}, u32[]{:S(2)}, u32[]{:S(2)}) collective-permute-start(f32[8,1152]{1,0:T(8,128)S(1)} %collective-permute-done.2.refs_3_), channel_id=1, source_target_pairs={{0,2},{2,0},{4,6},{6,4},{8,10},{10,8},{12,14},{14,12},{16,18},{18,... | collective-permute-start | bytes 110600 | tf_op jit(solution)/shard_map/ppermute | solution.py:544
  7.7 0.0 copy-done
  7.7 0.0 copy-done.7
  7.7 0.1 fusion.projections
  7.9 0.0 copy-done.1
  7.9 0.0 copy-done.3
  7.9 0.0 copy-done.5
  7.9 0.0 copy-done.6
  7.9 0.0 copy-start.2
  7.9 0.7 %shard_map.185 = (bf16[128,1024]{1,0:T(8,128)(2,1)S(1)}, f32[10,128,128]{2,1,0:T(8,128)S(1)}) custom-call(bf16[16,128]{1,0:T(8,128)(2,1)S(1)} %copy-done.5, f32[2,8,128]{2,1,0:T(8,128)S(1)} %copy-done.3, f32[2,128]{1,0:T(2,128)S(1)} %copy-done.6, bf16[2,128,128]{2,1,0:T(8,128)(2,1)S(1)} %copy-done.1, f32[128,128]{1,0:T(8,128)S(1)} %fusion.projections), custom_call_target="tpu_custom_call" | custom-call | flops 1000000 | bytes 1000000 | tf_op jit(solution)/shard_map/pallas_call | solution.py:548
  8.7 0.0 copy-start.4
  8.7 1.1 %collective-permute-done.4.refs_5_ = f32[8,1152]{1,0:T(8,128)S(1)} collective-permute-done((f32[8,1152]{1,0:T(8,128)}, f32[8,1152]{1,0:T(8,128)S(1)}, u32[]{:S(2)}, u32[]{:S(2)}) %collective-permute-start.4) | collective-permute-done | bytes 36896 | tf_op jit(solution)/shard_map/ppermute | solution.py:545
  9.8 0.4 %collective-permute-done.1.refs_2_ = f32[8,1152]{1,0:T(8,128)S(1)} collective-permute-done((f32[8,1152]{1,0:T(8,128)}, f32[8,1152]{1,0:T(8,128)S(1)}, u32[]{:S(2)}, u32[]{:S(2)}) %collective-permute-start.1) | collective-permute-done | bytes 36896 | tf_op jit(solution)/shard_map/ppermute | solution.py:545
  10.2 0.0 collective-permute-done.refs_1_
  10.2 0.0 collective-permute-done.3.refs_4_
  10.2 0.0 copy-done.2
  10.2 0.0 copy-done.4
  10.2 13.6 %shard_map.186 = (f32[3,1,1024]{2,1,0:T(1,128)}, f32[3,1,1024]{2,1,0:T(1,128)}, f32[3,1,1024]{2,1,0:T(1,128)}) custom-call(f32[8,1152]{1,0:T(8,128)S(1)} %copy-done.2, f32[8,1152]{1,0:T(8,128)S(1)} %collective-permute-done.refs_1_, f32[8,1152]{1,0:T(8,128)S(1)} %collective-permute-done.1.refs_2_, f32[8,1152]{1,0:T(8,128)S(1)} %collective-permute-done.2.refs_3_, ...), custom_call_target="tpu_custom_call" | custom-call | tf_op jit(solution)/shard_map/pallas_call | solution.py:607
Async XLA Ops:
  0.6 7.1 %copy-start = (bf16[128,128]{1,0:T(8,128)(2,1)S(1)}, bf16[128,128]{1,0:T(8,128)(2,1)}, u32[]{:S(2)}) copy-start(bf16[128,128]{1,0:T(8,128)(2,1)} %param.30) | copy-start | bytes 98308
  0.7 7.1 %copy-start.7 = (bf16[128,128]{1,0:T(8,128)(2,1)S(1)}, bf16[128,128]{1,0:T(8,128)(2,1)}, u32[]{:S(2)}) copy-start(bf16[128,128]{1,0:T(8,128)(2,1)} %param.29) | copy-start | bytes 98308
  2.1 5.7 %copy-start.1 = (bf16[2,128,128]{2,1,0:T(8,128)(2,1)S(1)}, bf16[2,128,128]{2,1,0:T(8,128)(2,1)}, u32[]{:S(2)}) copy-start(bf16[2,128,128]{2,1,0:T(8,128)(2,1)} %mix.1) | copy-start | bytes 196612
  2.1 5.8 %copy-start.3 = (f32[2,8,128]{2,1,0:T(8,128)S(1)}, f32[2,8,128]{2,1,0:T(8,128)}, u32[]{:S(2)}) copy-start(f32[2,8,128]{2,1,0:T(8,128)} %coef.1) | copy-start | bytes 24580
  2.1 5.8 %copy-start.5 = (bf16[16,128]{1,0:T(8,128)(2,1)S(1)}, bf16[16,128]{1,0:T(8,128)(2,1)}, u32[]{:S(2)}) copy-start(bf16[16,128]{1,0:T(8,128)(2,1)} %kind.1) | copy-start | bytes 12292
  2.2 5.8 %copy-start.6 = (f32[2,128]{1,0:T(2,128)S(1)}, f32[2,128]{1,0:T(2,128)}, u32[]{:S(2)}) copy-start(f32[2,128]{1,0:T(2,128)} %gain.1) | copy-start | bytes 3076
  2.2 5.2 %collective-permute-start.2 = (f32[8,1152]{1,0:T(8,128)}, f32[8,1152]{1,0:T(8,128)S(1)}, u32[]{:S(2)}, u32[]{:S(2)}) collective-permute-start(f32[8,1152]{1,0:T(8,128)} %get-tuple-element.10.refs_0_), channel_id=1, source_target_pairs={{1,0},{0,1},{3,2},{2,3},{5,4},{4,5},{7,6},{6,7},{9,8},{8,9},{11,10... | collective-permute-start | bytes 110600 | tf_op jit(solution)/shard_map/ppermute | solution.py:540
  5.2 4.6 %collective-permute-start.4 = (f32[8,1152]{1,0:T(8,128)}, f32[8,1152]{1,0:T(8,128)S(1)}, u32[]{:S(2)}, u32[]{:S(2)}) collective-permute-start(f32[8,1152]{1,0:T(8,128)} %get-tuple-element.10.refs_0_), channel_id=1, source_target_pairs={{3,4},{2,5},{5,2},{4,3},{7,8},{6,9},{9,6},{8,7},{11,12},{10,13},{1... | collective-permute-start | bytes 110600 | tf_op jit(solution)/shard_map/ppermute | solution.py:545
  5.3 4.9 %collective-permute-start.1 = (f32[8,1152]{1,0:T(8,128)}, f32[8,1152]{1,0:T(8,128)S(1)}, u32[]{:S(2)}, u32[]{:S(2)}) collective-permute-start(f32[8,1152]{1,0:T(8,128)} %get-tuple-element.10.refs_0_), channel_id=1, source_target_pairs={{2,4},{3,5},{4,2},{5,3},{6,8},{7,9},{8,6},{9,7},{10,12},{11,13},{1... | collective-permute-start | bytes 110600 | tf_op jit(solution)/shard_map/ppermute | solution.py:545
  7.2 2.9 %collective-permute-start = (f32[8,1152]{1,0:T(8,128)}, f32[8,1152]{1,0:T(8,128)S(1)}, u32[]{:S(2)}, u32[]{:S(2)}) collective-permute-start(f32[8,1152]{1,0:T(8,128)} %get-tuple-element.10.refs_0_), channel_id=1, source_target_pairs={{0,2},{2,0},{4,6},{6,4},{8,10},{10,8},{12,14},{14,12},{16,18},{18,... | collective-permute-start | bytes 110600 | tf_op jit(solution)/shard_map/ppermute | solution.py:544
  7.3 2.8 %collective-permute-start.3 = (f32[8,1152]{1,0:T(8,128)S(1)}, f32[8,1152]{1,0:T(8,128)S(1)}, u32[]{:S(2)}, u32[]{:S(2)}) collective-permute-start(f32[8,1152]{1,0:T(8,128)S(1)} %collective-permute-done.2.refs_3_), channel_id=1, source_target_pairs={{0,2},{2,0},{4,6},{6,4},{8,10},{10,8},{12,14},{14,12},{16,18},{18,... | collective-permute-start | bytes 110600 | tf_op jit(solution)/shard_map/ppermute | solution.py:544
  7.9 2.2 %copy-start.2 = (f32[8,1152]{1,0:T(8,128)S(1)}, f32[8,1152]{1,0:T(8,128)}, u32[]{:S(2)}) copy-start(f32[8,1152]{1,0:T(8,128)} %get-tuple-element.10.refs_0_) | copy-start | bytes 110596
  8.7 1.5 %copy-start.4 = (f32[8,128]{1,0:T(8,128)S(1)}, f32[8,128]{1,0:T(8,128)}, u32[]{:S(2)}) copy-start(f32[8,128]{1,0:T(8,128)} %get-tuple-element.13.refs_8_) | copy-start | bytes 12292

commit v6 on v5

--- a/solution.py
+++ b/solution.py
@@ -128,30 +128,18 @@
     ext_tiles = tiles + 2 * ghost_tiles
     n = len(held)
     offers = refs[: 3 * n]
-    tables = refs[3 * n : 3 * n + 3]
-    refs = refs[3 * n + 3 :]
+    wide, columns, rung, small_in = refs[3 * n : 3 * n + 4]
+    refs = refs[3 * n + 4 :]
     outputs = refs[:3]
-    offered, held_data, rung, wide, columns, small = refs[3:9]
-    pos_out, vel_out, force_out, arrivals, departures = refs[9:14]
+    held_data, small, pos_out, vel_out, force_out, arrival, departures = refs[3:10]
     data = {o: held_data.at[at] for at, o in enumerate(held)}
-    inward = [
-        pltpu.make_async_copy(src, dst, arrivals.at[at])
-        for at, (src, dst) in enumerate(
-            zip(
-                (*offers, tables[2], *tables),
-                [offered.at[at] for at in range(3 * n)] + [rung, wide, columns, small],
-            )
-        )
-    ]
-    for c in inward:
-        c.start()
-    for c in inward[: 3 * n + 1]:
-        c.wait()
+    inward = pltpu.make_async_copy(small_in, small, arrival.at[0])
+    inward.start()
     place = rung[3:4]
     for at in range(n):
         for first in range(0, atoms + TILE, TILE):
             lanes = slice(first, first + TILE)
-            here, even, odd = (offered[3 * at + k, :, lanes] for k in range(3))
+            here, even, odd = (offers[3 * at + k][:, lanes] for k in range(3))
             held_data[at, :, lanes] = jnp.where(place == 0.0, here, jnp.where(place == 1.0, even, odd))
 
     (
@@ -172,7 +160,7 @@
         ints,
         sm,
         sem,
-    ) = refs[14:-3]
+    ) = refs[10:-3]
     basis, squares = refs[-3], refs[-2:]
     u_parts = wide.at[:, 0 : 3 * TILE]
     mix_kind = wide.at[:, 3 * TILE : 4 * TILE + 16]
@@ -383,8 +371,7 @@
             if keep in imports and {(o - 1) % count, (o + 1) % count} <= ready:
                 jobs.append(imports.pop(keep))
 
-    for c in inward[3 * n + 1 :]:
-        c.wait()
+    inward.wait()
     sequence = [(at, t) for at in range(len(layer0)) for t in range(tiles)]
     squares[0][...] = offsets(0, 0)
     for i, (at, t) in enumerate(sequence):
@@ -583,23 +570,19 @@
         ((n0, 8, TILE), jnp.int32),
     ]
     inner = [
-        ((3 * len(held), 8, atoms + TILE), f32),
         ((len(held), 8, atoms + TILE), f32),
-        ((8, TILE), f32),
-        ((channels, 8 * TILE), bf16),
-        ((NB + 2, channels, TILE), f32),
     ]
     outgoing = [((3, 1, atoms), f32)] * 3
     outer = [(kept, bf16)] + [((NEI * TILE, 2 * TILE), f32)] * 2
     scratch = [pltpu.VMEM(*buffer) for buffer in inner] + [pltpu.SMEM((8, TILE), f32)]
     scratch += [pltpu.VMEM(*buffer) for buffer in outgoing]
-    scratch += [pltpu.SemaphoreType.DMA((3 * len(held) + 4,)), pltpu.SemaphoreType.DMA((3,))]
+    scratch += [pltpu.SemaphoreType.DMA((1,)), pltpu.SemaphoreType.DMA((3,))]
     scratch += [pltpu.VMEM(*buffer) for buffer in buffers] + [
         pltpu.SMEM((n0, 8, TILE), jnp.int32),
         pltpu.SemaphoreType.DMA((n0,)),
     ]
     scratch += [pltpu.VMEM(*buffer) for buffer in outer]
-    limit = 9 * 2**20 + sum(
+    limit = 11 * 2**20 + sum(
         math.prod(dims[:-1]) * max(dims[-1], TILE) * jnp.dtype(kind).itemsize
         for dims, kind in inner + outgoing + buffers + outer
     )
@@ -607,13 +590,14 @@
     outs = pl.pallas_call(
         functools.partial(main_kernel, (count, atoms, ghost, kind_vectors.shape[0])),
         out_shape=[shape((3, 1, atoms), f32)] * 3,
-        in_specs=[pl.BlockSpec(memory_space=pl.ANY)] * (3 * len(held) + 3),
+        in_specs=[vmem] * (3 * len(held) + 3) + [pl.BlockSpec(memory_space=pl.ANY)],
         out_specs=[pl.BlockSpec(memory_space=pl.ANY)] * 3,
         scratch_shapes=scratch,
         compiler_params=pltpu.CompilerParams(vmem_limit_bytes=limit),
     )(
         *offers,
         *weights,
+        small,
         small,
     )
     return tuple(jnp.transpose(x, (1, 0, 2)) for x in outs)

time: 24 us -> 23.7 us (0.987)
  Pallas kernels: 15.8 us -> 15.5 us
where the time goes in v6:
time: 23.7 us; the launch traced here: 23.5 us
  Pallas kernels  15.5 us (65%)
  starting transfers between devices  5.45 us (23%)
  waiting for transfers between devices  1.59 us (7%)
  between operations  0.73 us (3%)
    pallas_call x1, Pallas kernels, local(): pl.pallas_call(functools.partial(main_kernel, (count, atoms, ghost, kind_...  13.3 us
    ppermute x1, starting transfers between devices, local(): here = packed if o == 0 else lax.ppermute(packed, 'dom', beside)  3.03 us
    ppermute x2, starting transfers between devices, local(): lax.ppermute(packed, ('rep', 'dom'), across + rim)  2.03 us
    pallas_call x1, Pallas kernels, local(): pl.pallas_call(pack_kernel, out_shape=[shape((8, atoms + TILE), f32), sha...  1.47 us
    ppermute x2, waiting for transfers between devices, local(): lax.ppermute(packed, ('rep', 'dom'), across + rim)  1.46 us
    pallas_call x1, Pallas kernels, local(): pl.pallas_call(weights_kernel, out_shape=[shape((channels, 8 * TILE), bf1...  0.75 us
  transfers between devices with their start and end apart: 5, of which 3 were waited for; matrix products, arithmetic and copies ran while one was open for 1% of the time, Pallas kernels for 3%

profile of v6, /device:TPU:0, one launch (start us, length us, event | category | flops | bytes accessed | tf_op | source)
XLA Modules:
  0.0 23.5 jit_solution(4837301005637499219)
XLA Ops:
  0.6 0.0 copy-start
  0.7 0.0 copy-start.7
  0.7 1.5 %shard_map.184 = (f32[8,1152]{1,0:T(8,128)}, f32[8,128]{1,0:T(8,128)}) custom-call(f32[3,1,1024]{2,1,0:T(1,128)} %bitcast.9, f32[3,1,1024]{2,1,0:T(1,128)} %bitcast.10, f32[3,1,1024]{2,1,0:T(1,128)} %bitcast.11, s32[1,1024]{1,0:T(1,128)} %kinds.1, s32[1,768]{1,0:T(1,128)} %ghosts.1, s32[1,4,8]{2,1,0:T(4,128)} %bitcast.12, s32[1,8]{1,0:T(1,128)} %counts.1, ...), custom_call_target="tpu_custom_call" | custom-call | tf_op jit(solution)/shard_map/pallas_call | solution.py:500
  2.1 0.0 copy-start.1
  2.1 0.0 copy-start.4
  2.1 0.0 copy-start.5
  2.2 0.0 copy-start.6
  2.2 3.0 %collective-permute-start.2 = (f32[8,1152]{1,0:T(8,128)}, f32[8,1152]{1,0:T(8,128)S(1)}, u32[]{:S(2)}, u32[]{:S(2)}) collective-permute-start(f32[8,1152]{1,0:T(8,128)} %get-tuple-element.10.refs_0_), channel_id=1, source_target_pairs={{1,0},{0,1},{3,2},{2,3},{5,4},{4,5},{7,6},{6,7},{9,8},{8,9},{11,10... | collective-permute-start | bytes 110600 | tf_op jit(solution)/shard_map/ppermute | solution.py:527
  5.2 0.1 collective-permute-start.4
  5.3 1.9 %collective-permute-start.1 = (f32[8,1152]{1,0:T(8,128)}, f32[8,1152]{1,0:T(8,128)S(1)}, u32[]{:S(2)}, u32[]{:S(2)}) collective-permute-start(f32[8,1152]{1,0:T(8,128)} %get-tuple-element.10.refs_0_), channel_id=1, source_target_pairs={{2,4},{3,5},{4,2},{5,3},{6,8},{7,9},{8,6},{9,7},{10,12},{11,13},{1... | collective-permute-start | bytes 110600 | tf_op jit(solution)/shard_map/ppermute | solution.py:532
  7.2 0.0 collective-permute-start
  7.2 0.1 collective-permute-done.2.refs_3_
  7.3 0.4 %collective-permute-start.3 = (f32[8,1152]{1,0:T(8,128)S(1)}, f32[8,1152]{1,0:T(8,128)S(1)}, u32[]{:S(2)}, u32[]{:S(2)}) collective-permute-start(f32[8,1152]{1,0:T(8,128)S(1)} %collective-permute-done.2.refs_3_), channel_id=1, source_target_pairs={{0,2},{2,0},{4,6},{6,4},{8,10},{10,8},{12,14},{14,12},{16,18},{18,... | collective-permute-start | bytes 110600 | tf_op jit(solution)/shard_map/ppermute | solution.py:531
  7.7 0.0 copy-done
  7.7 0.0 copy-done.7
  7.7 0.1 fusion.projections
  7.9 0.0 copy-done.1
  7.9 0.0 copy-done.4
  7.9 0.0 copy-done.5
  7.9 0.0 copy-done.6
  7.9 0.0 copy-start.2
  7.9 0.7 %shard_map.185 = (bf16[128,1024]{1,0:T(8,128)(2,1)S(1)}, f32[10,128,128]{2,1,0:T(8,128)S(1)}) custom-call(bf16[16,128]{1,0:T(8,128)(2,1)S(1)} %copy-done.5, f32[2,8,128]{2,1,0:T(8,128)S(1)} %copy-done.4, f32[2,128]{1,0:T(2,128)S(1)} %copy-done.6, bf16[2,128,128]{2,1,0:T(8,128)(2,1)S(1)} %copy-done.1, f32[128,128]{1,0:T(8,128)S(1)} %fusion.projections), custom_call_target="tpu_custom_call" | custom-call | flops 1000000 | bytes 1000000 | tf_op jit(solution)/shard_map/pallas_call | solution.py:535
  8.7 0.0 copy-start.3
  8.7 1.1 %collective-permute-done.4.refs_5_ = f32[8,1152]{1,0:T(8,128)S(1)} collective-permute-done((f32[8,1152]{1,0:T(8,128)}, f32[8,1152]{1,0:T(8,128)S(1)}, u32[]{:S(2)}, u32[]{:S(2)}) %collective-permute-start.4) | collective-permute-done | bytes 36896 | tf_op jit(solution)/shard_map/ppermute | solution.py:532
  9.8 0.4 %collective-permute-done.1.refs_2_ = f32[8,1152]{1,0:T(8,128)S(1)} collective-permute-done((f32[8,1152]{1,0:T(8,128)}, f32[8,1152]{1,0:T(8,128)S(1)}, u32[]{:S(2)}, u32[]{:S(2)}) %collective-permute-start.1) | collective-permute-done | bytes 36896 | tf_op jit(solution)/shard_map/ppermute | solution.py:532
  10.2 0.0 collective-permute-done.refs_1_
  10.2 0.0 collective-permute-done.3.refs_4_
  10.2 0.0 copy-done.2
  10.2 0.0 copy-done.3
  10.2 13.3 %shard_map.186 = (f32[3,1,1024]{2,1,0:T(1,128)}, f32[3,1,1024]{2,1,0:T(1,128)}, f32[3,1,1024]{2,1,0:T(1,128)}) custom-call(f32[8,1152]{1,0:T(8,128)S(1)} %copy-done.2, f32[8,1152]{1,0:T(8,128)S(1)} %collective-permute-done.refs_1_, f32[8,1152]{1,0:T(8,128)S(1)} %collective-permute-done.1.refs_2_, f32[8,1152]{1,0:T(8,128)S(1)} %collective-permute-done.2.refs_3_, ...), custom_call_target="tpu_custom_call" | custom-call | tf_op jit(solution)/shard_map/pallas_call | solution.py:590
Async XLA Ops:
  0.6 7.1 %copy-start = (bf16[128,128]{1,0:T(8,128)(2,1)S(1)}, bf16[128,128]{1,0:T(8,128)(2,1)}, u32[]{:S(2)}) copy-start(bf16[128,128]{1,0:T(8,128)(2,1)} %param.30) | copy-start | bytes 98308
  0.7 7.1 %copy-start.7 = (bf16[128,128]{1,0:T(8,128)(2,1)S(1)}, bf16[128,128]{1,0:T(8,128)(2,1)}, u32[]{:S(2)}) copy-start(bf16[128,128]{1,0:T(8,128)(2,1)} %param.29) | copy-start | bytes 98308
  2.1 5.7 %copy-start.1 = (bf16[2,128,128]{2,1,0:T(8,128)(2,1)S(1)}, bf16[2,128,128]{2,1,0:T(8,128)(2,1)}, u32[]{:S(2)}) copy-start(bf16[2,128,128]{2,1,0:T(8,128)(2,1)} %mix.1) | copy-start | bytes 196612
  2.1 5.8 %copy-start.4 = (f32[2,8,128]{2,1,0:T(8,128)S(1)}, f32[2,8,128]{2,1,0:T(8,128)}, u32[]{:S(2)}) copy-start(f32[2,8,128]{2,1,0:T(8,128)} %coef.1) | copy-start | bytes 24580
  2.1 5.8 %copy-start.5 = (bf16[16,128]{1,0:T(8,128)(2,1)S(1)}, bf16[16,128]{1,0:T(8,128)(2,1)}, u32[]{:S(2)}) copy-start(bf16[16,128]{1,0:T(8,128)(2,1)} %kind.1) | copy-start | bytes 12292
  2.2 5.8 %copy-start.6 = (f32[2,128]{1,0:T(2,128)S(1)}, f32[2,128]{1,0:T(2,128)}, u32[]{:S(2)}) copy-start(f32[2,128]{1,0:T(2,128)} %gain.1) | copy-start | bytes 3076
  2.2 5.2 %collective-permute-start.2 = (f32[8,1152]{1,0:T(8,128)}, f32[8,1152]{1,0:T(8,128)S(1)}, u32[]{:S(2)}, u32[]{:S(2)}) collective-permute-start(f32[8,1152]{1,0:T(8,128)} %get-tuple-element.10.refs_0_), channel_id=1, source_target_pairs={{1,0},{0,1},{3,2},{2,3},{5,4},{4,5},{7,6},{6,7},{9,8},{8,9},{11,10... | collective-permute-start | bytes 110600 | tf_op jit(solution)/shard_map/ppermute | solution.py:527
  5.2 4.6 %collective-permute-start.4 = (f32[8,1152]{1,0:T(8,128)}, f32[8,1152]{1,0:T(8,128)S(1)}, u32[]{:S(2)}, u32[]{:S(2)}) collective-permute-start(f32[8,1152]{1,0:T(8,128)} %get-tuple-element.10.refs_0_), channel_id=1, source_target_pairs={{3,4},{2,5},{5,2},{4,3},{7,8},{6,9},{9,6},{8,7},{11,12},{10,13},{1... | collective-permute-start | bytes 110600 | tf_op jit(solution)/shard_map/ppermute | solution.py:532
  5.3 4.9 %collective-permute-start.1 = (f32[8,1152]{1,0:T(8,128)}, f32[8,1152]{1,0:T(8,128)S(1)}, u32[]{:S(2)}, u32[]{:S(2)}) collective-permute-start(f32[8,1152]{1,0:T(8,128)} %get-tuple-element.10.refs_0_), channel_id=1, source_target_pairs={{2,4},{3,5},{4,2},{5,3},{6,8},{7,9},{8,6},{9,7},{10,12},{11,13},{1... | collective-permute-start | bytes 110600 | tf_op jit(solution)/shard_map/ppermute | solution.py:532
  7.2 2.9 %collective-permute-start = (f32[8,1152]{1,0:T(8,128)}, f32[8,1152]{1,0:T(8,128)S(1)}, u32[]{:S(2)}, u32[]{:S(2)}) collective-permute-start(f32[8,1152]{1,0:T(8,128)} %get-tuple-element.10.refs_0_), channel_id=1, source_target_pairs={{0,2},{2,0},{4,6},{6,4},{8,10},{10,8},{12,14},{14,12},{16,18},{18,... | collective-permute-start | bytes 110600 | tf_op jit(solution)/shard_map/ppermute | solution.py:531
  7.3 2.8 %collective-permute-start.3 = (f32[8,1152]{1,0:T(8,128)S(1)}, f32[8,1152]{1,0:T(8,128)S(1)}, u32[]{:S(2)}, u32[]{:S(2)}) collective-permute-start(f32[8,1152]{1,0:T(8,128)S(1)} %collective-permute-done.2.refs_3_), channel_id=1, source_target_pairs={{0,2},{2,0},{4,6},{6,4},{8,10},{10,8},{12,14},{14,12},{16,18},{18,... | collective-permute-start | bytes 110600 | tf_op jit(solution)/shard_map/ppermute | solution.py:531
  7.9 2.2 %copy-start.2 = (f32[8,1152]{1,0:T(8,128)S(1)}, f32[8,1152]{1,0:T(8,128)}, u32[]{:S(2)}) copy-start(f32[8,1152]{1,0:T(8,128)} %get-tuple-element.10.refs_0_) | copy-start | bytes 110596
  8.7 1.5 %copy-start.3 = (f32[8,128]{1,0:T(8,128)S(1)}, f32[8,128]{1,0:T(8,128)}, u32[]{:S(2)}) copy-start(f32[8,128]{1,0:T(8,128)} %get-tuple-element.13.refs_8_.refs_9_) | copy-start | bytes 12292
